TPU v7x, 32 devices: a whole 2x2x4 slice. The times are simulated.
32 devices in a mesh: grid: 16 (over z, y, core), orb: 2 (over x).
Axes of the slice: x: 2, y: 2, z: 4, core: 2. Of those that a mesh axis runs over, the one named last changes fastest.
Arguments:
- density: float32 [32, 3, 128, 128], P('grid', None, 'orb'), may hold values from -4 to 4
- basis_values: float32 [32, 1280, 768], P(('grid', 'orb')), may hold values from -0.5 to 0.5
- quad_weights: float32 [32, 1280], P(('grid', 'orb')), may hold values from 0.01 to 0.1
- ext_potential: float32 [32, 1280], P(('grid', 'orb')), may hold values from 0 to 4
- batch_blocks: int32 [32, 6], P(('grid', 'orb')), may hold values from 0 to 31, as said below
- domain_blocks: int32 [64, 4], P(('grid', 'orb')), may hold values from 0 to 31, as said below
- coefficients: float32 [64, 4, 128, 128], P(('grid', 'orb')), may hold values from -0.25 to 0.25
Outputs:
- density_out: float32 [32, 3, 128, 128], P('grid', None, 'orb')
- coefficients_out: float32 [64, 4, 128, 128], P(('grid', 'orb'))
Inputs may be any that keep to these rules, and one draw needn't show every extreme that they name: `batch_blocks`: the batches on grid index g (batch numbers g * 32 / 16 onward) list the 6 blocks from (g - 1) * 2 onward, taken modulo 32, each once, in some order. `domain_blocks`: the domains on grid index g list 4 distinct blocks among the 6 blocks from (g - 1) * 2 onward, taken modulo 32, at least one of the first 2 and one of the last 2 of them.
All inputs are finite; a program needn't handle non-finite values.
Results may differ from a plain program's by a relative error of at most 0.0003.
Values sent between devices are 32-bit elements; how exact they have to be, the bound alone decides.
No kernel may reach another device: no remote copies, remote signals or barrier semaphores. Data moves between devices by JAX's collectives and lax.ppermute only.
A program may use at most 64 MiB of HBM per device.

v0:
```python
import functools
import jax
import jax.numpy as jnp
from jax import lax
from jax.experimental import pallas as pl
from jax.experimental.pallas import tpu as pltpu
from jax.sharding import PartitionSpec as P

ITERS = 2
step_scale = 0.5

NB = 128
SB = 2 * NB
TILE = 8
HALF = NB // 2
PACKED = NB + TILE
VMEM_BYTES = 16 * 1024 * 1024
POINT_CHUNK = 256
f32 = jnp.float32
bf16 = jnp.bfloat16

LOW = slice(0, PACKED)
HIGH = slice(PACKED + HALF, 2 * PACKED + HALF)
A_ROWS = 2 * PACKED + HALF
B_ROWS = 2 * NB + HALF
PAIR = PACKED + NB
GIVE_ROWS = PAIR + HALF
EARLY = 9
KEEP_AT = 2 * NB + HALF


def split(value):
    high = value.astype(bf16)
    return high, (value - high.astype(f32)).astype(bf16)


def dot3(left, right, contract=((1,), (0,))):
    def one(a, b):
        return lax.dot_general(a, b, (contract, ((), ())), preferred_element_type=f32)

    return one(left[0], right[0]) + (one(left[0], right[1]) + one(left[1], right[0]))


def both(pair, *index):
    return pair[0][index], pair[1][index]


def row_col():
    rows = lax.broadcasted_iota(jnp.int32, (NB, NB), 0)
    return rows, lax.broadcasted_iota(jnp.int32, (NB, NB), 1)


def aligned(value, unit):
    return pl.multiple_of(value * unit, unit)


def core_of():
    return lax.rem(lax.axis_index("grid"), 2)


def relative(block, total_blocks):
    anchor = (lax.axis_index("grid") - 1) * 2
    return lax.rem(block - anchor + total_blocks, total_blocks)


def vmem(shape, kind=f32):
    return pltpu.VMEM(shape, kind)


def call(kernel, operands, outs, name, scratch=(), smem=(), plain=(), flops=0):
    specs, pinned = [], []
    for i, operand in enumerate(operands):
        specs.append(pl.BlockSpec(memory_space=pltpu.SMEM if i in smem else pltpu.VMEM))
        if i in smem or i in plain:
            pinned.append(hbm(operand) if i in smem else operand)
        else:
            pinned.append(pltpu.with_memory_space_constraint(operand, pltpu.VMEM))
    return pl.pallas_call(
        kernel,
        out_shape=list(outs),
        in_specs=specs,
        out_specs=[pl.BlockSpec(memory_space=pltpu.VMEM) for _ in outs],
        scratch_shapes=list(scratch),
        compiler_params=pltpu.CompilerParams(vmem_limit_bytes=VMEM_BYTES),
        cost_estimate=pl.CostEstimate(flops=flops, bytes_accessed=0, transcendentals=0),
        name=name,
    )(*pinned)


def sort_kernel(total_blocks, blocks, basis, th, tl, nh, nl, done, columns, arrived):
    def copy(j):
        source = basis.at[0, :, pl.ds(j * NB, NB)]
        return pltpu.make_async_copy(source, columns.at[j], arrived.at[j])

    for j in range(6):
        copy(j).start()
    for j in range(6):
        at = pl.ds(aligned(relative(blocks[0, j], total_blocks), NB), NB)
        copy(j).wait()
        column = columns[j]
        nh[:, at], nl[:, at] = split(column)
        th[at, :], tl[at, :] = split(column.T)
    done[...] = jnp.zeros_like(done)


def cut_kernel(own, halves, other, near, early, rest, sems):
    copies = [
        pltpu.make_async_copy(own, near, sems.at[0]),
        pltpu.make_async_copy(halves.at[pl.ds(0, EARLY)], early, sems.at[1]),
        pltpu.make_async_copy(halves.at[pl.ds(EARLY, 16 - EARLY)], rest, sems.at[2]),
    ]
    for copy in copies:
        copy.start()
    for copy in copies:
        copy.wait()


def hbm(value):
    return pltpu.with_memory_space_constraint(value, pltpu.HBM)


def cut(own, halves, other):
    return pl.pallas_call(
        cut_kernel,
        out_shape=[vmem(own.shape), vmem((EARLY, HALF, NB)), vmem((16 - EARLY, HALF, NB))],
        in_specs=[pl.BlockSpec(memory_space=pl.ANY)] * 2 + [pl.BlockSpec(memory_space=pltpu.VMEM)],
        out_specs=[pl.BlockSpec(memory_space=pltpu.VMEM)] * 3,
        scratch_shapes=[pltpu.SemaphoreType.DMA((3,))],
        compiler_params=pltpu.CompilerParams(vmem_limit_bytes=VMEM_BYTES),
        name="cut",
    )(hbm(own), hbm(halves), other)


def hold_kernel(value, done, out):
    out[...] = value[...]


def sort_basis(total_blocks, batch_blocks, basis_values, unit):
    points, window = basis_values.shape[1:]
    halves = [vmem((window, points), bf16)] * 2 + [vmem((points, window), bf16)] * 2
    return pl.pallas_call(
        functools.partial(sort_kernel, total_blocks),
        out_shape=halves + [vmem((TILE, NB))],
        in_specs=[pl.BlockSpec(memory_space=pltpu.SMEM), pl.BlockSpec(memory_space=pl.ANY)],
        out_specs=[pl.BlockSpec(memory_space=pltpu.VMEM)] * 5,
        scratch_shapes=[vmem((6, points, NB)), pltpu.SemaphoreType.DMA((6,))],
        compiler_params=pltpu.CompilerParams(vmem_limit_bytes=VMEM_BYTES),
        cost_estimate=pl.CostEstimate(flops=6 * unit, bytes_accessed=0, transcendentals=0),
        name="sort_basis",
    )(hbm(batch_blocks), hbm(basis_values))


def put_pair(pair, packed, off):
    rows, cols = row_col()
    first, last = pair[:NB, :NB], pair[NB:, NB:]
    diagonal = jnp.sum(jnp.where(rows == cols, last, 0.0), axis=0, keepdims=True)
    packed[:NB, :] = jnp.where(rows <= cols, first, last)
    packed[NB:PACKED, :] = jnp.broadcast_to(diagonal, (TILE, NB))
    off[...] = pair[:NB, NB:]


def put_side(low, cross, high, side_a, side_b):
    put_pair(low, side_a.at[LOW], side_b.at[:NB])
    put_pair(high, side_a.at[HIGH], side_b.at[KEEP_AT - NB : KEEP_AT])
    side_a[PACKED : PACKED + HALF, :] = cross[:HALF]
    side_b[NB : NB + HALF, :] = cross[HALF:]


def put_other(pair, cross_ref, give, keep):
    core = core_of()
    put_pair(pair, give.at[:PACKED], give.at[PACKED:PAIR])
    give[PAIR:, :] = cross_ref[pl.ds(aligned(1 - core, HALF), HALF), :]
    keep[...] = cross_ref[pl.ds(aligned(core, HALF), HALF), :]


def side_parts(side_a, side_b):
    low = (side_a[:NB, :], side_a[NB : NB + 1, :], side_b[:NB, :])
    start = PACKED + HALF
    high = (
        side_a[start : start + NB, :],
        side_a[start + NB : start + NB + 1, :],
        side_b[NB + HALF : KEEP_AT, :],
    )
    cross = jnp.concatenate([side_a[PACKED:start, :], side_b[NB : NB + HALF, :]], axis=0)
    return low, cross, high


def other_parts(side_b, other, cross_ref):
    core = core_of()
    cross_ref[pl.ds(aligned(core, HALF), HALF), :] = side_b[KEEP_AT:, :]
    cross_ref[pl.ds(aligned(1 - core, HALF), HALF), :] = other[PAIR:, :]
    return (other[:NB, :], other[NB : NB + 1, :], other[PACKED:PAIR, :]), cross_ref[...]


def unpack(part):
    merged, diagonal, off = part
    rows, cols = row_col()
    turned = merged.T
    first = jnp.where(rows <= cols, merged, turned)
    last = jnp.where(rows > cols, merged, jnp.where(rows < cols, turned, diagonal))
    return join(first, off, off.T, last)


def join(a, b, c, d):
    return jnp.concatenate(
        [jnp.concatenate([a, b], axis=1), jnp.concatenate([c, d], axis=1)], axis=0
    )


def upper_form(part):
    merged, diagonal, off = part
    rows, cols = row_col()
    twice = merged * 2.0
    first = jnp.where(rows < cols, twice, jnp.where(rows == cols, merged, 0.0))
    last = jnp.where(rows > cols, twice, jnp.where(rows == cols, diagonal, 0.0))
    return join(first, off * 2.0, jnp.zeros((NB, NB), f32), last)


def near_kernel(side_a, side_b, keep, arrived, out_a, out_b, out_keep):
    core = core_of()
    out_a[...] = side_a[...]
    out_b[...] = side_b[...]
    out_keep[...] = keep[...] + arrived[PAIR:, :]
    rows_a = pl.ds(pl.multiple_of((1 - core) * (PACKED + HALF), TILE), PACKED)
    rows_b = pl.ds(pl.multiple_of((1 - core) * (NB + HALF), TILE), NB)
    out_a[rows_a, :] = side_a[rows_a, :] + arrived[:PACKED, :]
    out_b[rows_b, :] = side_b[rows_b, :] + arrived[PACKED:PAIR, :]


def add_kernel(left, right, out):
    out[...] = left[...] + right[...]


def add_keep_kernel(side_b, arrived, keep, out):
    out[:KEEP_AT, :] = side_b[...] + arrived[...]
    out[KEEP_AT:, :] = keep[...]


def side_near(out_a, out_b, near):
    core = core_of()
    rows_a = pl.ds(pl.multiple_of((1 - core) * (PACKED + HALF), TILE), PACKED)
    rows_b = pl.ds(pl.multiple_of((1 - core) * (NB + HALF), TILE), NB)
    near[:PACKED, :] = out_a[rows_a, :]
    near[PACKED:PAIR, :] = out_b[rows_b, :]
    near[PAIR:, :] = out_b[KEEP_AT:, :]


def total_kernel(side_a, arrived_a, side_b, arrived_b, out_a, out_b, near):
    out_a[...] = side_a[...] + arrived_a[...]
    out_b[...] = side_b[...] + arrived_b[...]
    side_near(out_a, out_b, near)


def join_kernel(side_a, side_b, keep, arrived, out, out_keep):
    near_kernel(side_a, side_b, keep, arrived, out.at[:A_ROWS], out.at[A_ROWS:], out_keep)


def total_grid_kernel(side, arrived, keep, out_a, out_b, near):
    out_a[...] = side[:A_ROWS, :] + arrived[:A_ROWS, :]
    out_b[:KEEP_AT, :] = side[A_ROWS:, :] + arrived[A_ROWS:, :]
    out_b[KEEP_AT:, :] = keep[...]
    side_near(out_a, out_b, near)


def add_density(terms, th, tl, before, after):
    points = th.shape[1]
    for start in range(0, points, POINT_CHUNK):
        cols = slice(start, start + POINT_CHUNK)
        rho = before(cols)
        for matrix, at, count, values in terms:
            rows = pl.ds(pl.multiple_of(at, HALF), count)
            value = []
            for value_at, value_count in values:
                value_rows = pl.ds(pl.multiple_of(value_at, HALF), value_count)
                value.append(th[value_rows, cols].astype(f32) + tl[value_rows, cols].astype(f32))
            value = value[0] if len(value) == 1 else jnp.concatenate(value, axis=0)
            product = dot3(matrix, (th[rows, cols], tl[rows, cols]))
            rho = rho + jnp.sum(product * value, axis=0, keepdims=True)
        after(cols, rho)


def half_terms(source, first, pair, half, ends):
    body = join(*[source[2 * i + j + 1 - first] for i in range(2) for j in range(2)])
    at = pair * SB
    rows = [(at + half * HALF, HALF), (at + NB + half * HALF, HALF)]
    terms = [(split(body), at, SB, rows)]
    for index, row, col in ends:
        terms.append((split(source[index]), col * NB, NB, [(row * NB + half * HALF, HALF)]))
    return terms


def rho_first(th, tl, own, own_far, edge, other, other_far, early, rho):
    core = core_of()
    orb = lax.axis_index("orb")
    own_ends = ((0, 2, 1), (5, 3, 4))
    other_ends = ((5 * core, 4 - 3 * core, 3 - core),)
    edge_ends = ((5 - 5 * core, 1 + 3 * core, 2 + core),)
    terms = (
        half_terms(own, 0, 1, orb, own_ends)
        + half_terms(own_far, 0, 1, 1 - orb, own_ends)
        + half_terms(other, 0, 2 - 2 * core, orb, other_ends)
        + half_terms(other_far, 0, 2 - 2 * core, 1 - orb, other_ends)
        + half_terms(edge, 0, 2 * core, orb, edge_ends)
    )

    def store(cols, value):
        rho[:, cols] = value

    add_density(terms, th, tl, lambda cols: jnp.zeros((1, POINT_CHUNK), f32), store)


def far_kernel(lists, edge, sorted_first, out):
    first = 1 - core_of()
    for i in range(5):
        out[i * HALF : (i + 1) * HALF, :] = edge[i + first]
    lanes = lax.broadcasted_iota(jnp.int32, (TILE, NB), 1)
    row = jnp.zeros((TILE, NB), f32)
    for d in range(2):
        for i in range(4):
            row = jnp.where(lanes == 4 * d + i, lists[d, i].astype(f32), row)
    out[5 * HALF :, :] = row


def rho_side(th, tl, side_a, side_b, rho):
    core = core_of()
    low, cross, high = side_parts(side_a, side_b)
    at = core * SB
    terms = [
        (split(upper_form(low)), at, SB, [(at, SB)]),
        (split(upper_form(high)), at + SB, SB, [(at + SB, SB)]),
        (split(cross * 2.0), at + SB, NB, [(at + NB, NB)]),
    ]

    def store(cols, value):
        rho[:, cols] = value

    add_density(terms, th, tl, lambda cols: jnp.zeros((1, POINT_CHUNK), f32), store)


def scaled_rows(th, tl, at, count, scale):
    rows = pl.ds(pl.multiple_of(at, NB), count)
    return split((th[rows, :].astype(f32) + tl[rows, :].astype(f32)) * scale[...])


def fock_block(left, nh, nl, at, count):
    cols = pl.ds(pl.multiple_of(at, NB), count)
    return dot3(left, (nh[:, cols], nl[:, cols]))


def fock_other(terms, weights, external, th, tl, nh, nl, rho, scale, give, keep, cross_ref):
    core = core_of()

    def store(cols, value):
        potential = external[:, cols] - jnp.exp(jnp.log(value * value + 1.0) * (1.0 / 6.0))
        scale[:, cols] = weights[:, cols] * potential

    add_density(terms, th, tl, lambda cols: rho[:, cols], store)
    at = (2 - 2 * core) * SB
    pair = fock_block(scaled_rows(th, tl, at, SB, scale), nh, nl, at, SB)
    row = (3 - 2 * core) * NB
    cross_ref[...] = fock_block(scaled_rows(th, tl, row, NB, scale), nh, nl, row + NB, NB)
    put_other(pair, cross_ref, give, keep)


def fock_other_first(
    weights, external, th, tl, nh, nl, rho, edge_far, scale, give, keep, cross_ref
):
    core = core_of()
    ends = ((4 - 4 * core, 1 + 3 * core, 2 + core),)

    def far(index):
        return edge_far[pl.ds(aligned(index, HALF), HALF), :]

    body = join(*[far(2 * i + j + core) for i in range(2) for j in range(2)])
    half = 1 - lax.axis_index("orb")
    at = 2 * core * SB
    rows = [(at + half * HALF, HALF), (at + NB + half * HALF, HALF)]
    terms = [(split(body), at, SB, rows)]
    for index, row, col in ends:
        terms.append((split(far(index)), col * NB, NB, [(row * NB + half * HALF, HALF)]))
    fock_other(terms, weights, external, th, tl, nh, nl, rho, scale, give, keep, cross_ref)


def fock_other_later(
    weights, external, th, tl, nh, nl, rho, side_b, other, scale, give, keep, cross_ref
):
    core = core_of()
    part, cross = other_parts(side_b, other, cross_ref)
    at = (2 - 2 * core) * SB
    row = (3 - 2 * core) * NB
    terms = [
        (split(upper_form(part)), at, SB, [(at, SB)]),
        (split(cross * 2.0), row + NB, NB, [(row, NB)]),
    ]
    fock_other(terms, weights, external, th, tl, nh, nl, rho, scale, give, keep, cross_ref)


def fock_side(th, tl, nh, nl, scale, side_a, side_b):
    at = core_of() * SB
    low = fock_block(scaled_rows(th, tl, at, SB, scale), nh, nl, at, SB)
    both_rows = fock_block(scaled_rows(th, tl, at + NB, 3 * NB, scale), nh, nl, at + SB, SB)
    put_side(low, both_rows[:NB, :NB], both_rows[NB:], side_a, side_b)


def coefficient_parts(value, high, low, turned_high, turned_low):
    high[...], low[...] = split(value)
    turned_high[...], turned_low[...] = split(value.T)


def spread_kernel(
    total_blocks, own_lists, other_lists, own, early, partner, coef, ch, cl, th, tl
):
    coef[...] = jnp.zeros_like(coef)
    for d in range(4):
        for i in range(4):
            blocks = own_lists if d < 2 else other_lists
            at = aligned(relative(blocks[d % 2, i], total_blocks), NB)
            cols = slice(d * NB, (d + 1) * NB)
            if d < 2:
                coef[pl.ds(at, NB), cols] = own[4 * d + i]
                continue
            for half in range(2):
                index = 2 * (4 * (d - 2) + i) + half
                value = early[index] if index < EARLY else partner[index - EARLY]
                coef[pl.ds(at + half * HALF, HALF), cols] = value
    coefficient_parts(coef[...], ch, cl, th, tl)


def turn_kernel(coef, th, tl):
    th[...], tl[...] = split(coef[...].T)


def mixing(th, tl, at, count, gradient):
    cols = pl.ds(pl.multiple_of(at, NB), count)
    return [
        dot3((th[d * NB : (d + 1) * NB, cols], tl[d * NB : (d + 1) * NB, cols]), both(gradient, slice(None), slice(d * NB, (d + 1) * NB)))
        for d in range(4)
    ]


def domain_side(side_a, side_b, ch, cl, th, tl, gradient, mixed):
    low, cross, high = side_parts(side_a, side_b)
    at = core_of() * SB
    zero = jnp.zeros((NB, NB), f32)
    first = jnp.concatenate([unpack(low), jnp.concatenate([zero, cross.T], axis=1)], axis=0)
    last = jnp.concatenate([jnp.concatenate([cross, zero], axis=1), unpack(high)], axis=0)

    def coef(start):
        rows = pl.ds(pl.multiple_of(start, SB), SB)
        return ch[rows, :], cl[rows, :]

    upper = dot3(split(first), coef(at))
    lower = dot3(split(last), coef(at + SB))
    gradient[:NB, :] = upper[:NB]
    gradient[NB : 3 * NB, :] = upper[NB:] + lower[: 2 * NB]
    gradient[3 * NB :, :] = lower[2 * NB :]
    for d, value in enumerate(mixing(th, tl, at, 4 * NB, split(gradient[...]))):
        mixed[d] = value


def domain_new(
    total_blocks, own_lists, other_lists, coef, ch, cl, th, tl, gradient, mixed, side_b, other,
    fresh, fh, fl, work, cross_ref,
):
    core = core_of()
    part, cross = other_parts(side_b, other, cross_ref)
    zero = jnp.zeros((NB, NB), f32)
    beside = jnp.where(core == 0, cross, cross.T)
    across = jnp.where(core == 0, cross.T, cross)
    placed = jnp.concatenate(
        [jnp.where(core == 0, beside, zero), jnp.where(core == 0, zero, beside)], axis=1
    )
    slab = jnp.concatenate([unpack(part), placed], axis=0)
    other_at = (2 - 2 * core) * SB
    other_rows = pl.ds(pl.multiple_of(other_at, SB), SB)
    side_block = pl.ds(pl.multiple_of((3 - core) * NB, NB), NB)
    touching = pl.ds(pl.multiple_of((4 - 3 * core) * NB, NB), NB)
    work[pl.ds(pl.multiple_of(core * SB, SB), 4 * NB), :] = gradient[...]
    product = dot3(split(slab), (ch[other_rows, :], cl[other_rows, :]))
    work[other_rows, :] = product[:SB]
    back = dot3(split(across), (ch[side_block, :], cl[side_block, :]))
    work[touching, :] += back
    work[side_block, :] += product[SB:]
    first = mixing(th, tl, other_at, SB, split(work[other_rows, :]))
    second = mixing(th, tl, (3 - core) * NB, NB, split(product[SB:]))
    total = [mixed[d] + first[d] + second[d] for d in range(4)]
    for d in range(0, 4, 2):
        cols = slice(d * NB, (d + 2) * NB)
        square = split(join(total[d], zero, zero, total[d + 1]))
        moved = dot3((ch[:, cols], cl[:, cols]), square)
        for r in range(6):
            rows = slice(r * NB, (r + 1) * NB)
            for e in range(2):
                blocks = own_lists if d == 0 else other_lists
                present = relative(blocks[e, 0], total_blocks) == r
                for i in range(1, 4):
                    present = present | (relative(blocks[e, i], total_blocks) == r)
                at = slice((d + e) * NB, (d + e + 1) * NB)
                kept = jnp.where(present, work[rows, at], 0.0)
                value = coef[rows, at] - step_scale * (kept - moved[rows, e * NB : (e + 1) * NB])
                fresh[rows, at] = value
                fh[rows, at], fl[rows, at] = split(value)


def outer(fh, fl, at, count, from_at, from_count):
    left = pl.ds(pl.multiple_of(at, HALF), count)
    right = pl.ds(pl.multiple_of(from_at, NB), from_count)
    return dot3((fh[left, :], fl[left, :]), (fh[right, :], fl[right, :]), ((1,), (1,)))


def domain_other(
    total_blocks, own_lists, other_lists, coef, ch, cl, th, tl, gradient, mixed, side_b, other,
    fresh, fh, fl, give, keep, work, cross_ref,
):
    domain_new(
        total_blocks, own_lists, other_lists, coef, ch, cl, th, tl, gradient, mixed, side_b,
        other, fresh, fh, fl, work, cross_ref,
    )
    core = core_of()
    at = (2 - 2 * core) * SB
    row = (3 - 2 * core) * NB
    cross_ref[...] = outer(fh, fl, row, NB, row + NB, NB)
    put_other(outer(fh, fl, at, SB, at, SB), cross_ref, give, keep)


def density_side(fh, fl, side_a, side_b):
    at = core_of() * SB
    cross = outer(fh, fl, at + NB, NB, at + SB, NB)
    put_side(
        outer(fh, fl, at, SB, at, SB), cross, outer(fh, fl, at + SB, SB, at + SB, SB),
        side_a, side_b,
    )


def owner_half(fh, fl, pair, target, first):
    half = lax.axis_index("orb") * HALF
    for i in range(2):
        rows = outer(fh, fl, pair * SB + i * NB + half, HALF, pair * SB, SB)
        target[2 * i + 1 - first] = rows[:, :NB]
        target[2 * i + 2 - first] = rows[:, NB:]


def end_half(fh, fl, row, col):
    return outer(fh, fl, row * NB + lax.axis_index("orb") * HALF, HALF, col * NB, NB)


def domain_edge(
    total_blocks, own_lists, other_lists, coef, ch, cl, th, tl, gradient, mixed, side_b, other,
    fresh, fh, fl, edge, give, work, cross_ref,
):
    domain_new(
        total_blocks, own_lists, other_lists, coef, ch, cl, th, tl, gradient, mixed, side_b,
        other, fresh, fh, fl, work, cross_ref,
    )
    core = core_of()
    owner_half(fh, fl, 2 * core, edge, 1 - core)
    edge[4 - 4 * core] = end_half(fh, fl, 1 + 3 * core, 2 + core)
    owner_half(fh, fl, 2 - 2 * core, give, core)
    give[4 * core] = end_half(fh, fl, 4 - 3 * core, 3 - core)


def domain_last(total_blocks, own_lists, fresh, fh, fl, result, own):
    owner_half(fh, fl, 1, own, 0)
    own[0] = end_half(fh, fl, 2, 1)
    own[5] = end_half(fh, fl, 3, 4)
    for d in range(2):
        for i in range(4):
            at = aligned(relative(own_lists[d, i], total_blocks), NB)
            result[d, i] = fresh[pl.ds(at, NB), d * NB : (d + 1) * NB]


def owner_kernel(own, from_core, from_edge, out):
    core = core_of()
    lower = jnp.where(core == 0, from_core[...], from_edge[...])
    upper = jnp.where(core == 0, from_edge[...], from_core[...])
    out[0] = own[0] + upper[0]
    out[1:5] = own[1:5] + upper[1:] + lower[:4]
    out[5] = own[5] + lower[4]


def to_core(value):
    count = lax.axis_size("grid")
    return lax.ppermute(value, "grid", [(i, i ^ 1) for i in range(count)])


def to_edge(value):
    count = lax.axis_size("grid")
    route = [(i, (i + 1) % count if i % 2 else (i - 1) % count) for i in range(count)]
    return lax.ppermute(value, "grid", route)


def to_orb(value):
    return lax.ppermute(value, "orb", [(0, 1), (1, 0)])


A_OUT = vmem((A_ROWS, NB))
B_OUT = vmem((B_ROWS, NB))
BK_OUT = vmem((B_ROWS + HALF, NB))
GIVE_OUT = vmem((GIVE_ROWS, NB))
KEEP_OUT = vmem((HALF, NB))
CROSS = vmem((NB, NB))


def total_over_all(made, before_last, before_sum):
    side_a, side_b, keep, arrived = made
    side_a, side_b, keep = call(
        near_kernel, (side_a, side_b, keep, arrived), (A_OUT, B_OUT, KEEP_OUT), "add_near"
    )
    first_b = to_edge(side_b)
    first_a = to_orb(side_a)
    (side_a,) = call(add_kernel, (side_a, first_a), (A_OUT,), "add_a")
    (side_b,) = call(add_keep_kernel, (side_b, first_b, keep), (BK_OUT,), "add_b")
    last_a = to_edge(side_a)
    side_b = before_last(side_b)
    last_b = before_sum(to_orb(side_b))
    side_a, side_b, near = call(
        total_kernel, (side_a, last_a, side_b, last_b), (A_OUT, BK_OUT, GIVE_OUT), "add_all"
    )
    return side_a, side_b, to_core(near)


def total_over_grid(made):
    side_a, side_b, keep, arrived = made
    side, keep = call(
        join_kernel,
        (side_a, side_b, keep, arrived),
        (vmem((A_ROWS + B_ROWS, NB)), KEEP_OUT),
        "add_near",
    )
    side_a, side_b, near = call(
        total_grid_kernel, (side, to_edge(side), keep), (A_OUT, BK_OUT, GIVE_OUT), "add_all"
    )
    return side_a, side_b, to_core(near)


def shards(
    density, basis_values, quad_weights, ext_potential, batch_blocks, domain_blocks, coefficients
):
    total_blocks = density.shape[0] * lax.axis_size("grid")
    points = basis_values.shape[1]
    core = lax.rem(lax.axis_index("grid"), 2)
    window = 6 * NB
    row_out = vmem((1, points))
    coef_out = vmem((window, 4 * NB))
    coef_half = vmem((window, 4 * NB), bf16)
    turned_half = vmem((4 * NB, window), bf16)
    unit = 2 * 3 * points * SB * SB

    blocks = coefficients.reshape(8, NB, NB)
    own = density.reshape(6, HALF, NB)
    edge = to_edge(own)
    own_far = to_orb(own)
    other = to_core(own)
    *basis, done = sort_basis(total_blocks, batch_blocks, basis_values, unit)
    th, tl, nh, nl = basis
    near, early, rest = cut(own, blocks.reshape(16, HALF, NB), other)
    early = to_orb(early)
    (own_far,) = call(hold_kernel, (own_far, done), (vmem((6, HALF, NB)),), "hold")
    other_far = to_core(own_far)
    (edge_message,) = call(
        far_kernel,
        (domain_blocks, edge, done),
        (vmem((5 * HALF + TILE, NB)),),
        "far_message",
        smem=(0,),
    )
    edge_far = to_orb(edge_message)
    (rho,) = call(
        rho_first,
        (th, tl, near, own_far, edge, other, other_far, early),
        (row_out,),
        "rho_first",
        flops=5 * unit,
    )
    edge_far, rest, rho = lax.optimization_barrier((edge_far, rest, rho))
    partner = to_orb(rest)
    other_lists = edge_far[5 * HALF, :8].reshape(2, 4).astype(jnp.int32)

    packed = None
    for iteration in range(ITERS):
        if iteration == 0:
            kernel, operands = fock_other_first, (edge_far,)
        else:
            side_a, side_b, arriving = packed
            (rho,) = call(rho_side, (th, tl, side_a, side_b), (row_out,), "rho_side", flops=3 * unit)
            kernel, operands = fock_other_later, (side_b, arriving)
        scale, give, keep = call(
            kernel,
            (quad_weights, ext_potential, *basis, rho, *operands),
            (row_out, GIVE_OUT, KEEP_OUT),
            "fock_other",
            scratch=(CROSS,),
            plain=(0, 1),
            flops=3 * unit,
        )
        arrived = to_core(give)
        side_a, side_b = call(
            fock_side, (*basis, scale), (A_OUT, B_OUT), "fock_side", flops=3 * unit
        )
        ready = {}

        def before_last(value):
            if iteration == 0:
                value, ready["partner"] = lax.optimization_barrier((value, partner))
                return value
            turned = call(turn_kernel, (coef,), (turned_half, turned_half), "turn", flops=unit)
            value, *ready["turned"] = lax.optimization_barrier((value, *turned))
            return value

        def before_sum(value):
            if iteration > 0:
                return value
            spread = call(
                functools.partial(spread_kernel, total_blocks),
                (domain_blocks, other_lists, blocks, hbm(early), hbm(ready["partner"])),
                (coef_out, coef_half, coef_half, turned_half, turned_half),
                "spread",
                smem=(0, 1),
                plain=(2, 3, 4),
                flops=3 * unit,
            )
            value, *ready["spread"] = lax.optimization_barrier((value, *spread))
            return value

        side_a, side_b, arriving = total_over_all(
            (side_a, side_b, keep, arrived), before_last, before_sum
        )
        if iteration == 0:
            coef, *halves = ready["spread"]
        else:
            halves = (ch, cl, *ready["turned"])
        gradient, mixed = call(
            domain_side,
            (side_a, side_b, *halves),
            (vmem((4 * NB, 4 * NB)), vmem((4, NB, NB))),
            "domain_side",
            flops=unit,
        )
        operands = (
            domain_blocks, other_lists, coef, *halves, gradient, mixed, side_b, arriving
        )
        scratch = (coef_out, CROSS)
        if iteration < ITERS - 1:
            coef, ch, cl, give, keep = call(
                functools.partial(domain_other, total_blocks),
                operands,
                (coef_out, coef_half, coef_half, GIVE_OUT, KEEP_OUT),
                "domain_other",
                scratch=scratch,
                smem=(0, 1),
                flops=2 * unit,
            )
            arrived = to_core(give)
            side_a, side_b = call(density_side, (ch, cl), (A_OUT, B_OUT), "density_side", flops=unit)
            packed = total_over_grid((side_a, side_b, keep, arrived))
    message = vmem((5, HALF, NB))
    coef, ch, cl, edge, give = call(
        functools.partial(domain_edge, total_blocks),
        operands,
        (coef_out, coef_half, coef_half, message, message),
        "domain_edge",
        scratch=scratch,
        smem=(0, 1),
        flops=2 * unit,
    )
    from_edge = to_edge(edge)
    from_core = to_core(give)
    result, own = call(
        functools.partial(domain_last, total_blocks),
        (domain_blocks, coef, ch, cl),
        (jax.ShapeDtypeStruct(coefficients.shape, f32), vmem((6, HALF, NB))),
        "domain_last",
        smem=(0,),
        flops=unit,
    )
    (rows,) = call(
        owner_kernel,
        (own, from_core, from_edge),
        (jax.ShapeDtypeStruct((6, HALF, NB), f32),),
        "owner_rows",
    )
    return (rows.reshape(density.shape), result)


def solution(mesh):
    in_specs = (
        P("grid", None, "orb", None),
        P(("grid", "orb"), None, None),
        P(("grid", "orb"), None),
        P(("grid", "orb"), None),
        P(("grid", "orb"), None),
        P(("grid", "orb"), None),
        P(("grid", "orb"), None, None, None),
    )
    out_specs = (P("grid", None, "orb", None), P(("grid", "orb"), None, None, None))
    return jax.shard_map(shards, mesh=mesh, in_specs=in_specs, out_specs=out_specs, check_vma=False)
```

profile of v0, /device:TPU:0, one launch (start us, length us, event | category | flops | bytes accessed | tf_op | source)
XLA Modules:
  0.0 97.4 jit_solution(11995221941998536098)
XLA Ops:
  0.6 0.5 collective-permute-start.2
  1.1 2.6 %collective-permute-start.3 = (f32[6,64,128]{2,1,0:T(8,128)}, f32[6,64,128]{2,1,0:T(8,128)S(1)}, u32[]{:S(2)}, u32[]{:S(2)}) collective-permute-start(f32[6,64,128]{2,1,0:T(8,128)} %bitcast.7), channel_id=1, source_target_pairs={{0,1},{1,0},{2,3},{3,2},{4,5},{5,4},{6,7},{7,6},{8,9},{9,8},{10,11... | collective-permute-start | bytes 589832 | tf_op jit(solution)/shard_map/ppermute | solution.py:593
  3.7 4.3 %collective-permute-start = (f32[6,64,128]{2,1,0:T(8,128)}, f32[6,64,128]{2,1,0:T(8,128)S(1)}, u32[]{:S(2)}, u32[]{:S(2)}) collective-permute-start(f32[6,64,128]{2,1,0:T(8,128)} %bitcast.8), channel_id=1, source_target_pairs={{0,30},{2,4},{4,2},{6,8},{8,6},{10,12},{12,10},{14,16},{16,14},{18... | collective-permute-start | bytes 589832 | tf_op jit(solution)/shard_map/ppermute | solution.py:589
  8.0 1.1 %cut.1 = (f32[6,64,128]{2,1,0:T(8,128)S(1)}, f32[9,64,128]{2,1,0:T(8,128)S(1)}, f32[7,64,128]{2,1,0:T(8,128)S(1)}) custom-call(f32[6,64,128]{2,1,0:T(8,128)} %bitcast.9, f32[16,64,128]{2,1,0:T(8,128)} %bitcast.4, f32[6,64,128]{2,1,0:T(8,128)S(1)} %collective-permute-done.2.other), custom_call_target="tpu_custom_call" | custom-call | tf_op jit(solution)/shard_map/cut/pallas_call | solution.py:123
  9.2 0.6 collective-permute-start.5
  9.8 3.3 %sort_basis.1 = (bf16[768,1280]{1,0:T(8,128)(2,1)S(1)}, bf16[768,1280]{1,0:T(8,128)(2,1)S(1)}, bf16[1280,768]{1,0:T(8,128)(2,1)S(1)}, bf16[1280,768]{1,0:T(8,128)(2,1)S(1)}, f32[8,128]{1,0:T(8,128)S(1)}) custom-call(s32[1,6]{1,0:T(1,128)} %blocks.1, f32[1,1280,768]{2,1,0:T(8,128)} %basis.1), custom_call_target="tpu_custom_call" | custom-call | flops 3019898880 | tf_op jit(solution)/shard_map/sort_basis/pallas_call | solution.py:141
  13.2 0.7 far_message.1
  14.0 1.6 %collective-permute-start.1 = (f32[328,128]{1,0:T(8,128)S(1)}, f32[328,128]{1,0:T(8,128)S(1)}, u32[]{:S(2)}, u32[]{:S(2)}) collective-permute-start(f32[328,128]{1,0:T(8,128)S(1)} %far_message.1), channel_id=1, source_target_pairs={{0,1},{1,0},{2,3},{3,2},{4,5},{5,4},{6,7},{7,6},{8,9},{9,8},{10,11... | collective-permute-start | bytes 503816 | tf_op jit(solution)/shard_map/ppermute | solution.py:593
  15.5 0.5 collective-permute-done.5.early
  16.0 2.7 %rho_first.1.rho = f32[1,1280]{1,0:T(1,128)S(1)} custom-call(bf16[768,1280]{1,0:T(8,128)(2,1)S(1)} %get-tuple-element.78.th, bf16[768,1280]{1,0:T(8,128)(2,1)S(1)} %get-tuple-element.79.tl, f32[6,64,128]{2,1,0:T(8,128)S(1)} %get-tuple-element.80.own, f32[6,64,128]{2,1,0:T(8,128)S(1)} %hold.1.own_far, f32[6,64,128]{2,1,0:T(8,128)S(1)} %collective-permute-done.edge, ...), custom_call_target="tpu_custom_call" | custom-call | flops 2516582400 | tf_op jit(solution)/shard_map/rho_first/pallas_call | solution.py:78
  18.7 2.0 %collective-permute-done.1.edge_far = f32[328,128]{1,0:T(8,128)S(1)} collective-permute-done((f32[328,128]{1,0:T(8,128)S(1)}, f32[328,128]{1,0:T(8,128)S(1)}, u32[]{:S(2)}, u32[]{:S(2)}) %collective-permute-start.1) | collective-permute-done | bytes 167968 | tf_op jit(solution)/shard_map/ppermute | solution.py:593
  20.7 1.7 %fock_other.2 = (f32[1,1280]{1,0:T(1,128)S(1)}, f32[328,128]{1,0:T(8,128)S(1)}, f32[64,128]{1,0:T(8,128)S(1)}) custom-call(f32[1,1280]{1,0:T(1,128)S(1)} %copy-done.7, f32[1,1280]{1,0:T(1,128)S(1)} %copy-done.8, bf16[768,1280]{1,0:T(8,128)(2,1)S(1)} %get-tuple-element.78.th, bf16[768,1280]{1,0:T(8,128)(2,1)S(1)} %get-tuple-element.79.tl, ...), custom_call_target="tpu_custom_call" | custom-call | flops 1509949440 | tf_op jit(solution)/shard_map/fock_other/pallas_call | solution.py:78
  22.5 1.6 %collective-permute-start.8 = (f32[7,64,128]{2,1,0:T(8,128)S(1)}, f32[7,64,128]{2,1,0:T(8,128)S(1)}, u32[]{:S(2)}, u32[]{:S(2)}) collective-permute-start(f32[7,64,128]{2,1,0:T(8,128)S(1)} %get-tuple-element.93), channel_id=1, source_target_pairs={{0,1},{1,0},{2,3},{3,2},{4,5},{5,4},{6,7},{7,6},{8,9},{9,8},{10,11... | collective-permute-start | bytes 688136 | tf_op jit(solution)/shard_map/ppermute | solution.py:593
  24.0 1.8 %fock_side.2 = (f32[336,128]{1,0:T(8,128)S(1)}, f32[320,128]{1,0:T(8,128)S(1)}) custom-call(bf16[768,1280]{1,0:T(8,128)(2,1)S(1)} %get-tuple-element.78.th, bf16[768,1280]{1,0:T(8,128)(2,1)S(1)} %get-tuple-element.79.tl, bf16[1280,768]{1,0:T(8,128)(2,1)S(1)} %get-tuple-element.83.nh, bf16[1280,768]{1,0:T(8,128)(2,1)S(1)} %get-tuple-element.84.nl, ...), custom_call_target="tpu_custom_call" | custom-call | flops 1509949440 | tf_op jit(solution)/shard_map/fock_side/pallas_call | solution.py:78
  25.9 0.6 collective-permute-start.10
  26.5 2.9 %collective-permute-start.7 = (f32[320,128]{1,0:T(8,128)S(1)}, f32[320,128]{1,0:T(8,128)S(1)}, u32[]{:S(2)}, u32[]{:S(2)}) collective-permute-start(f32[320,128]{1,0:T(8,128)S(1)} %get-tuple-element.91.side_b), channel_id=1, source_target_pairs={{0,30},{2,4},{4,2},{6,8},{8,6},{10,12},{12,10},{14,16},{16,14},{18... | collective-permute-start | bytes 491528 | tf_op jit(solution)/shard_map/ppermute | solution.py:589
  29.4 4.5 %collective-permute-done.7.arrived = f32[320,128]{1,0:T(8,128)S(1)} collective-permute-done((f32[320,128]{1,0:T(8,128)S(1)}, f32[320,128]{1,0:T(8,128)S(1)}, u32[]{:S(2)}, u32[]{:S(2)}) %collective-permute-start.7) | collective-permute-done | bytes 163872 | tf_op jit(solution)/shard_map/ppermute | solution.py:589
  33.9 1.6 %collective-permute-start.9 = (f32[384,128]{1,0:T(8,128)S(1)}, f32[384,128]{1,0:T(8,128)S(1)}, u32[]{:S(2)}, u32[]{:S(2)}) collective-permute-start(f32[384,128]{1,0:T(8,128)S(1)} %add_b.2.side_b), channel_id=1, source_target_pairs={{0,1},{1,0},{2,3},{3,2},{4,5},{5,4},{6,7},{7,6},{8,9},{9,8},{10,11... | collective-permute-start | bytes 589832 | tf_op jit(solution)/shard_map/ppermute | solution.py:593
  35.5 2.7 %collective-permute-start.11 = (f32[336,128]{1,0:T(8,128)S(1)}, f32[336,128]{1,0:T(8,128)S(1)}, u32[]{:S(2)}, u32[]{:S(2)}) collective-permute-start(f32[336,128]{1,0:T(8,128)S(1)} %add_a.2.side_a), channel_id=1, source_target_pairs={{0,30},{2,4},{4,2},{6,8},{8,6},{10,12},{12,10},{14,16},{16,14},{18... | collective-permute-start | bytes 516104 | tf_op jit(solution)/shard_map/ppermute | solution.py:589
  38.3 0.6 convert_element_type.6.other_lists
  38.9 1.8 %spread.1 = (f32[768,512]{1,0:T(8,128)S(1)}, bf16[768,512]{1,0:T(8,128)(2,1)S(1)}, bf16[768,512]{1,0:T(8,128)(2,1)S(1)}, bf16[512,768]{1,0:T(8,128)(2,1)S(1)}, bf16[512,768]{1,0:T(8,128)(2,1)S(1)}) custom-call(s32[2,4]{1,0:T(2,128)} %own_lists.7, s32[2,4]{1,0:T(2,128)} %convert_element_type.6.other_lists, f32[8,128,128]{2,1,0:T(8,128)S(1)} %bitcast.5, ...), custom_call_target="tpu_custom_call" | custom-call | flops 1509949440 | tf_op jit(solution)/shard_map/spread/pallas_call | solution.py:78
  40.7 2.4 %collective-permute-done.11.arrived_a = f32[336,128]{1,0:T(8,128)S(1)} collective-permute-done((f32[336,128]{1,0:T(8,128)S(1)}, f32[336,128]{1,0:T(8,128)S(1)}, u32[]{:S(2)}, u32[]{:S(2)}) %collective-permute-start.11) | collective-permute-done | bytes 172064 | tf_op jit(solution)/shard_map/ppermute | solution.py:589
  43.3 1.4 %domain_side.2 = (f32[512,512]{1,0:T(8,128)S(1)}, f32[4,128,128]{2,1,0:T(8,128)S(1)}) custom-call(f32[336,128]{1,0:T(8,128)S(1)} %get-tuple-element.108.side_a, f32[384,128]{1,0:T(8,128)S(1)} %get-tuple-element.109.side_b, bf16[768,512]{1,0:T(8,128)(2,1)S(1)} %get-tuple-element.102.ch, bf16[768,512]{1,0:T(8,128)(2,1)S(1)} %get-tuple-element.103.cl, ...), custom_call_target="tpu_custom_call" | custom-call | flops 503316480 | tf_op jit(solution)/shard_map/domain_side/pallas_call | solution.py:78
  44.7 3.7 %domain_other.1 = (f32[768,512]{1,0:T(8,128)S(1)}, bf16[768,512]{1,0:T(8,128)(2,1)S(1)}, bf16[768,512]{1,0:T(8,128)(2,1)S(1)}, f32[328,128]{1,0:T(8,128)S(1)}, f32[64,128]{1,0:T(8,128)S(1)}) custom-call(s32[2,4]{1,0:T(2,128)} %own_lists.7, s32[2,4]{1,0:T(2,128)} %convert_element_type.6.other_lists, f32[768,512]{1,0:T(8,128)S(1)} %get-tuple-element.101.coef, ...), custom_call_target="tpu_custom_call" | custom-call | flops 1006632960 | tf_op jit(solution)/shard_map/domain_other/pallas_call | solution.py:78
  48.4 0.6 collective-permute-start.13
  49.0 0.7 density_side.1
  49.7 0.3 collective-permute-done.13.arrived
  50.1 2.7 %collective-permute-start.14 = (f32[656,128]{1,0:T(8,128)S(1)}, f32[656,128]{1,0:T(8,128)S(1)}, u32[]{:S(2)}, u32[]{:S(2)}) collective-permute-start(f32[656,128]{1,0:T(8,128)S(1)} %get-tuple-element.120.side), channel_id=1, source_target_pairs={{0,30},{2,4},{4,2},{6,8},{8,6},{10,12},{12,10},{14,16},{16,14},{18... | collective-permute-start | bytes 1007624 | tf_op jit(solution)/shard_map/ppermute | solution.py:589
  52.8 6.7 %collective-permute-done.14.arrived = f32[656,128]{1,0:T(8,128)S(1)} collective-permute-done((f32[656,128]{1,0:T(8,128)S(1)}, f32[656,128]{1,0:T(8,128)S(1)}, u32[]{:S(2)}, u32[]{:S(2)}) %collective-permute-start.14) | collective-permute-done | bytes 335904 | tf_op jit(solution)/shard_map/ppermute | solution.py:589
  59.6 1.2 %collective-permute-start.15 = (f32[328,128]{1,0:T(8,128)S(1)}, f32[328,128]{1,0:T(8,128)S(1)}, u32[]{:S(2)}, u32[]{:S(2)}) collective-permute-start(f32[328,128]{1,0:T(8,128)S(1)} %get-tuple-element.124), channel_id=1, source_target_pairs={{0,2},{2,0},{4,6},{6,4},{8,10},{10,8},{12,14},{14,12},{16,18},{18,... | collective-permute-start | bytes 503816 | tf_op jit(solution)/shard_map/ppermute | solution.py:583
  60.8 1.5 %rho_side.1.rho = f32[1,1280]{1,0:T(1,128)S(1)} custom-call(bf16[768,1280]{1,0:T(8,128)(2,1)S(1)} %get-tuple-element.78.th, bf16[768,1280]{1,0:T(8,128)(2,1)S(1)} %copy-done.1, f32[336,128]{1,0:T(8,128)S(1)} %get-tuple-element.122.side_a, f32[384,128]{1,0:T(8,128)S(1)} %get-tuple-element.123.side_b), custom_call_target="tpu_custom_call" | custom-call | flops 1509949440 | tf_op jit(solution)/shard_map/rho_side/pallas_call | solution.py:78
  62.4 0.6 copy-done.5
  62.9 2.4 %fock_other.3 = (f32[1,1280]{1,0:T(1,128)S(1)}, f32[328,128]{1,0:T(8,128)S(1)}, f32[64,128]{1,0:T(8,128)S(1)}) custom-call(f32[1,1280]{1,0:T(1,128)S(1)} %copy-done.7, f32[1,1280]{1,0:T(1,128)S(1)} %copy-done.8, bf16[768,1280]{1,0:T(8,128)(2,1)S(1)} %get-tuple-element.78.th, bf16[768,1280]{1,0:T(8,128)(2,1)S(1)} %copy-done.1, ...), custom_call_target="tpu_custom_call" | custom-call | flops 1509949440 | tf_op jit(solution)/shard_map/fock_other/pallas_call | solution.py:78
  65.4 1.7 %fock_side.3 = (f32[336,128]{1,0:T(8,128)S(1)}, f32[320,128]{1,0:T(8,128)S(1)}) custom-call(bf16[768,1280]{1,0:T(8,128)(2,1)S(1)} %get-tuple-element.78.th, bf16[768,1280]{1,0:T(8,128)(2,1)S(1)} %copy-done.1, bf16[1280,768]{1,0:T(8,128)(2,1)S(1)} %copy-done.3, bf16[1280,768]{1,0:T(8,128)(2,1)S(1)} %copy-done.5, f32[1,1280]{1,0:T(1,128)S(1)} %get-tuple-element.125.scale), custom_call_target="tpu_custom_call" | custom-call | flops 1509949440 | tf_op jit(solution)/shard_map/fock_side/pallas_call | solution.py:78
  67.2 2.7 %collective-permute-start.17 = (f32[320,128]{1,0:T(8,128)S(1)}, f32[320,128]{1,0:T(8,128)S(1)}, u32[]{:S(2)}, u32[]{:S(2)}) collective-permute-start(f32[320,128]{1,0:T(8,128)S(1)} %get-tuple-element.130.side_b), channel_id=1, source_target_pairs={{0,30},{2,4},{4,2},{6,8},{8,6},{10,12},{12,10},{14,16},{16,14},{18... | collective-permute-start | bytes 491528 | tf_op jit(solution)/shard_map/ppermute | solution.py:589
  70.0 0.5 collective-permute-start.18
  70.5 0.5 turn.1
  71.0 3.7 %collective-permute-done.17.arrived = f32[320,128]{1,0:T(8,128)S(1)} collective-permute-done((f32[320,128]{1,0:T(8,128)S(1)}, f32[320,128]{1,0:T(8,128)S(1)}, u32[]{:S(2)}, u32[]{:S(2)}) %collective-permute-start.17) | collective-permute-done | bytes 163872 | tf_op jit(solution)/shard_map/ppermute | solution.py:589
  74.8 0.6 collective-permute-start.20
  75.5 2.4 %collective-permute-start.19 = (f32[336,128]{1,0:T(8,128)S(1)}, f32[336,128]{1,0:T(8,128)S(1)}, u32[]{:S(2)}, u32[]{:S(2)}) collective-permute-start(f32[336,128]{1,0:T(8,128)S(1)} %add_a.3.side_a), channel_id=1, source_target_pairs={{0,30},{2,4},{4,2},{6,8},{8,6},{10,12},{12,10},{14,16},{16,14},{18... | collective-permute-start | bytes 516104 | tf_op jit(solution)/shard_map/ppermute | solution.py:589
  77.8 5.2 %collective-permute-done.19.arrived_a = f32[336,128]{1,0:T(8,128)S(1)} collective-permute-done((f32[336,128]{1,0:T(8,128)S(1)}, f32[336,128]{1,0:T(8,128)S(1)}, u32[]{:S(2)}, u32[]{:S(2)}) %collective-permute-start.19) | collective-permute-done | bytes 172064 | tf_op jit(solution)/shard_map/ppermute | solution.py:589
  83.2 1.4 %domain_side.3 = (f32[512,512]{1,0:T(8,128)S(1)}, f32[4,128,128]{2,1,0:T(8,128)S(1)}) custom-call(f32[336,128]{1,0:T(8,128)S(1)} %get-tuple-element.138.side_a, f32[384,128]{1,0:T(8,128)S(1)} %get-tuple-element.139.side_b, bf16[768,512]{1,0:T(8,128)(2,1)S(1)} %get-tuple-element.114.fh.ch, bf16[768,512]{1,0:T(8,128)(2,1)S(1)} %get-tuple-element.115.fl.cl, ...), custom_call_target="tpu_custom_call" | custom-call | flops 503316480 | tf_op jit(solution)/shard_map/domain_side/pallas_call | solution.py:78
  84.6 4.1 %domain_edge.1 = (f32[768,512]{1,0:T(8,128)S(1)}, bf16[768,512]{1,0:T(8,128)(2,1)S(1)}, bf16[768,512]{1,0:T(8,128)(2,1)S(1)}, f32[5,64,128]{2,1,0:T(8,128)S(1)}, f32[5,64,128]{2,1,0:T(8,128)S(1)}) custom-call(s32[2,4]{1,0:T(2,128)} %own_lists.7, s32[2,4]{1,0:T(2,128)} %convert_element_type.6.other_lists, f32[768,512]{1,0:T(8,128)S(1)} %get-tuple-element.113.coef, ...), custom_call_target="tpu_custom_call" | custom-call | flops 1006632960 | tf_op jit(solution)/shard_map/domain_edge/pallas_call | solution.py:78
  88.7 0.6 collective-permute-start.22
  89.2 2.3 %collective-permute-start.23 = (f32[5,64,128]{2,1,0:T(8,128)S(1)}, f32[5,64,128]{2,1,0:T(8,128)S(1)}, u32[]{:S(2)}, u32[]{:S(2)}) collective-permute-start(f32[5,64,128]{2,1,0:T(8,128)S(1)} %get-tuple-element.148), channel_id=1, source_target_pairs={{0,30},{2,4},{4,2},{6,8},{8,6},{10,12},{12,10},{14,16},{16,14},{18... | collective-permute-start | bytes 491528 | tf_op jit(solution)/shard_map/ppermute | solution.py:589
  91.5 2.1 %domain_last.1 = (f32[2,4,128,128]{3,2,1,0:T(8,128)}, f32[6,64,128]{2,1,0:T(8,128)S(1)}) custom-call(s32[2,4]{1,0:T(2,128)} %own_lists.7, f32[768,512]{1,0:T(8,128)S(1)} %get-tuple-element.143.fresh, bf16[768,512]{1,0:T(8,128)(2,1)S(1)} %get-tuple-element.144.fh, bf16[768,512]{1,0:T(8,128)(2,1)S(1)} %get-tuple-element.145.fl), custom_call_target="tpu_custom_call" | custom-call | flops 503316480 | tf_op jit(solution)/shard_map/domain_last/pallas_call | solution.py:78
  93.7 3.0 %collective-permute-done.23.from_edge = f32[5,64,128]{2,1,0:T(8,128)S(1)} collective-permute-done((f32[5,64,128]{2,1,0:T(8,128)S(1)}, f32[5,64,128]{2,1,0:T(8,128)S(1)}, u32[]{:S(2)}, u32[]{:S(2)}) %collective-permute-start.23) | collective-permute-done | bytes 163872 | tf_op jit(solution)/shard_map/ppermute | solution.py:589
  96.7 0.7 owner_rows.1
  (53 shorter events, 1.0 us)
Async XLA Ops:
  0.6 7.4 %collective-permute-start.2 = (f32[6,64,128]{2,1,0:T(8,128)}, f32[6,64,128]{2,1,0:T(8,128)S(1)}, u32[]{:S(2)}, u32[]{:S(2)}) collective-permute-start(f32[6,64,128]{2,1,0:T(8,128)} %bitcast.6), channel_id=1, source_target_pairs={{0,2},{2,0},{4,6},{6,4},{8,10},{10,8},{12,14},{14,12},{16,18},{18,... | collective-permute-start | bytes 589832 | tf_op jit(solution)/shard_map/ppermute | solution.py:583
  1.1 12.0 %collective-permute-start.3 = (f32[6,64,128]{2,1,0:T(8,128)}, f32[6,64,128]{2,1,0:T(8,128)S(1)}, u32[]{:S(2)}, u32[]{:S(2)}) collective-permute-start(f32[6,64,128]{2,1,0:T(8,128)} %bitcast.7), channel_id=1, source_target_pairs={{0,1},{1,0},{2,3},{3,2},{4,5},{5,4},{6,7},{7,6},{8,9},{9,8},{10,11... | collective-permute-start | bytes 589832 | tf_op jit(solution)/shard_map/ppermute | solution.py:593
  3.7 9.5 %collective-permute-start = (f32[6,64,128]{2,1,0:T(8,128)}, f32[6,64,128]{2,1,0:T(8,128)S(1)}, u32[]{:S(2)}, u32[]{:S(2)}) collective-permute-start(f32[6,64,128]{2,1,0:T(8,128)} %bitcast.8), channel_id=1, source_target_pairs={{0,30},{2,4},{4,2},{6,8},{8,6},{10,12},{12,10},{14,16},{16,14},{18... | collective-permute-start | bytes 589832 | tf_op jit(solution)/shard_map/ppermute | solution.py:589
  9.2 6.8 %collective-permute-start.5 = (f32[9,64,128]{2,1,0:T(8,128)S(1)}, f32[9,64,128]{2,1,0:T(8,128)S(1)}, u32[]{:S(2)}, u32[]{:S(2)}) collective-permute-start(f32[9,64,128]{2,1,0:T(8,128)S(1)} %get-tuple-element.81), channel_id=1, source_target_pairs={{0,1},{1,0},{2,3},{3,2},{4,5},{5,4},{6,7},{7,6},{8,9},{9,8},{10,11... | collective-permute-start | bytes 884744 | tf_op jit(solution)/shard_map/ppermute | solution.py:593
  13.1 10.9 %copy-start = (bf16[768,1280]{1,0:T(8,128)(2,1)}, bf16[768,1280]{1,0:T(8,128)(2,1)S(1)}, u32[]{:S(2)}) copy-start(bf16[768,1280]{1,0:T(8,128)(2,1)S(1)} %get-tuple-element.79.tl) | copy-start | bytes 5898244
  13.1 10.9 %copy-start.2 = (bf16[1280,768]{1,0:T(8,128)(2,1)}, bf16[1280,768]{1,0:T(8,128)(2,1)S(1)}, u32[]{:S(2)}) copy-start(bf16[1280,768]{1,0:T(8,128)(2,1)S(1)} %get-tuple-element.83.nh) | copy-start | bytes 5898244
  13.1 10.9 %copy-start.4 = (bf16[1280,768]{1,0:T(8,128)(2,1)}, bf16[1280,768]{1,0:T(8,128)(2,1)S(1)}, u32[]{:S(2)}) copy-start(bf16[1280,768]{1,0:T(8,128)(2,1)S(1)} %get-tuple-element.84.nl) | copy-start | bytes 5898244
  13.2 2.4 %collective-permute-start.4 = (f32[6,64,128]{2,1,0:T(8,128)S(1)}, f32[6,64,128]{2,1,0:T(8,128)S(1)}, u32[]{:S(2)}, u32[]{:S(2)}) collective-permute-start(f32[6,64,128]{2,1,0:T(8,128)S(1)} %hold.1.own_far), channel_id=1, source_target_pairs={{0,2},{2,0},{4,6},{6,4},{8,10},{10,8},{12,14},{14,12},{16,18},{18,... | collective-permute-start | bytes 589832 | tf_op jit(solution)/shard_map/ppermute | solution.py:583
  14.0 6.7 %collective-permute-start.1 = (f32[328,128]{1,0:T(8,128)S(1)}, f32[328,128]{1,0:T(8,128)S(1)}, u32[]{:S(2)}, u32[]{:S(2)}) collective-permute-start(f32[328,128]{1,0:T(8,128)S(1)} %far_message.1), channel_id=1, source_target_pairs={{0,1},{1,0},{2,3},{3,2},{4,5},{5,4},{6,7},{7,6},{8,9},{9,8},{10,11... | collective-permute-start | bytes 503816 | tf_op jit(solution)/shard_map/ppermute | solution.py:593
  16.0 2.7 %copy-start.9 = (f32[9,64,128]{2,1,0:T(8,128)}, f32[9,64,128]{2,1,0:T(8,128)S(1)}, u32[]{:S(2)}) copy-start(f32[9,64,128]{2,1,0:T(8,128)S(1)} %collective-permute-done.5.early) | copy-start | bytes 884740
  16.0 4.7 %copy-start.7 = (f32[1,1280]{1,0:T(1,128)S(1)}, f32[1,1280]{1,0:T(1,128)}, u32[]{:S(2)}) copy-start(f32[1,1280]{1,0:T(1,128)} %weights.3) | copy-start | bytes 15364
  16.0 4.7 %copy-start.8 = (f32[1,1280]{1,0:T(1,128)S(1)}, f32[1,1280]{1,0:T(1,128)}, u32[]{:S(2)}) copy-start(f32[1,1280]{1,0:T(1,128)} %external.3) | copy-start | bytes 15364
  22.4 3.4 %collective-permute-start.6 = (f32[328,128]{1,0:T(8,128)S(1)}, f32[328,128]{1,0:T(8,128)S(1)}, u32[]{:S(2)}, u32[]{:S(2)}) collective-permute-start(f32[328,128]{1,0:T(8,128)S(1)} %get-tuple-element.90), channel_id=1, source_target_pairs={{0,2},{2,0},{4,6},{6,4},{8,10},{10,8},{12,14},{14,12},{16,18},{18,... | collective-permute-start | bytes 503816 | tf_op jit(solution)/shard_map/ppermute | solution.py:583
  22.5 11.5 %collective-permute-start.8 = (f32[7,64,128]{2,1,0:T(8,128)S(1)}, f32[7,64,128]{2,1,0:T(8,128)S(1)}, u32[]{:S(2)}, u32[]{:S(2)}) collective-permute-start(f32[7,64,128]{2,1,0:T(8,128)S(1)} %get-tuple-element.93), channel_id=1, source_target_pairs={{0,1},{1,0},{2,3},{3,2},{4,5},{5,4},{6,7},{7,6},{8,9},{9,8},{10,11... | collective-permute-start | bytes 688136 | tf_op jit(solution)/shard_map/ppermute | solution.py:593
  24.0 14.9 %copy-start.6 = (f32[2,4,128,128]{3,2,1,0:T(8,128)S(1)}, f32[2,4,128,128]{3,2,1,0:T(8,128)}, u32[]{:S(2)}) copy-start(f32[2,4,128,128]{3,2,1,0:T(8,128)} %param.13) | copy-start | bytes 1572868
  25.9 9.6 %collective-permute-start.10 = (f32[336,128]{1,0:T(8,128)S(1)}, f32[336,128]{1,0:T(8,128)S(1)}, u32[]{:S(2)}, u32[]{:S(2)}) collective-permute-start(f32[336,128]{1,0:T(8,128)S(1)} %get-tuple-element.106.left), channel_id=1, source_target_pairs={{0,1},{1,0},{2,3},{3,2},{4,5},{5,4},{6,7},{7,6},{8,9},{9,8},{10,11... | collective-permute-start | bytes 516104 | tf_op jit(solution)/shard_map/ppermute | solution.py:593
  26.5 7.4 %collective-permute-start.7 = (f32[320,128]{1,0:T(8,128)S(1)}, f32[320,128]{1,0:T(8,128)S(1)}, u32[]{:S(2)}, u32[]{:S(2)}) collective-permute-start(f32[320,128]{1,0:T(8,128)S(1)} %get-tuple-element.91.side_b), channel_id=1, source_target_pairs={{0,30},{2,4},{4,2},{6,8},{8,6},{10,12},{12,10},{14,16},{16,14},{18... | collective-permute-start | bytes 491528 | tf_op jit(solution)/shard_map/ppermute | solution.py:589
  33.9 5.0 %copy-start.10 = (f32[7,64,128]{2,1,0:T(8,128)}, f32[7,64,128]{2,1,0:T(8,128)S(1)}, u32[]{:S(2)}) copy-start(f32[7,64,128]{2,1,0:T(8,128)S(1)} %collective-permute-done.8.partner) | copy-start | bytes 688132
  33.9 6.8 %collective-permute-start.9 = (f32[384,128]{1,0:T(8,128)S(1)}, f32[384,128]{1,0:T(8,128)S(1)}, u32[]{:S(2)}, u32[]{:S(2)}) collective-permute-start(f32[384,128]{1,0:T(8,128)S(1)} %add_b.2.side_b), channel_id=1, source_target_pairs={{0,1},{1,0},{2,3},{3,2},{4,5},{5,4},{6,7},{7,6},{8,9},{9,8},{10,11... | collective-permute-start | bytes 589832 | tf_op jit(solution)/shard_map/ppermute | solution.py:593
  35.5 7.6 %collective-permute-start.11 = (f32[336,128]{1,0:T(8,128)S(1)}, f32[336,128]{1,0:T(8,128)S(1)}, u32[]{:S(2)}, u32[]{:S(2)}) collective-permute-start(f32[336,128]{1,0:T(8,128)S(1)} %add_a.2.side_a), channel_id=1, source_target_pairs={{0,30},{2,4},{4,2},{6,8},{8,6},{10,12},{12,10},{14,16},{16,14},{18... | collective-permute-start | bytes 516104 | tf_op jit(solution)/shard_map/ppermute | solution.py:589
  43.2 1.5 %collective-permute-start.12 = (f32[328,128]{1,0:T(8,128)S(1)}, f32[328,128]{1,0:T(8,128)S(1)}, u32[]{:S(2)}, u32[]{:S(2)}) collective-permute-start(f32[328,128]{1,0:T(8,128)S(1)} %get-tuple-element.112), channel_id=1, source_target_pairs={{0,2},{2,0},{4,6},{6,4},{8,10},{10,8},{12,14},{14,12},{16,18},{18,... | collective-permute-start | bytes 503816 | tf_op jit(solution)/shard_map/ppermute | solution.py:583
  48.4 12.4 %copy-start.1 = (bf16[768,1280]{1,0:T(8,128)(2,1)S(1)}, bf16[768,1280]{1,0:T(8,128)(2,1)}, u32[]{:S(2)}) copy-start(bf16[768,1280]{1,0:T(8,128)(2,1)} %copy-done) | copy-start | bytes 5898244
  48.4 1.6 %collective-permute-start.13 = (f32[328,128]{1,0:T(8,128)S(1)}, f32[328,128]{1,0:T(8,128)S(1)}, u32[]{:S(2)}, u32[]{:S(2)}) collective-permute-start(f32[328,128]{1,0:T(8,128)S(1)} %get-tuple-element.119), channel_id=1, source_target_pairs={{0,2},{2,0},{4,6},{6,4},{8,10},{10,8},{12,14},{14,12},{16,18},{18,... | collective-permute-start | bytes 503816 | tf_op jit(solution)/shard_map/ppermute | solution.py:583
  50.1 9.5 %collective-permute-start.14 = (f32[656,128]{1,0:T(8,128)S(1)}, f32[656,128]{1,0:T(8,128)S(1)}, u32[]{:S(2)}, u32[]{:S(2)}) collective-permute-start(f32[656,128]{1,0:T(8,128)S(1)} %get-tuple-element.120.side), channel_id=1, source_target_pairs={{0,30},{2,4},{4,2},{6,8},{8,6},{10,12},{12,10},{14,16},{16,14},{18... | collective-permute-start | bytes 1007624 | tf_op jit(solution)/shard_map/ppermute | solution.py:589
  59.6 2.8 %collective-permute-start.15 = (f32[328,128]{1,0:T(8,128)S(1)}, f32[328,128]{1,0:T(8,128)S(1)}, u32[]{:S(2)}, u32[]{:S(2)}) collective-permute-start(f32[328,128]{1,0:T(8,128)S(1)} %get-tuple-element.124), channel_id=1, source_target_pairs={{0,2},{2,0},{4,6},{6,4},{8,10},{10,8},{12,14},{14,12},{16,18},{18,... | collective-permute-start | bytes 503816 | tf_op jit(solution)/shard_map/ppermute | solution.py:583
  60.8 1.6 %copy-start.3 = (bf16[1280,768]{1,0:T(8,128)(2,1)S(1)}, bf16[1280,768]{1,0:T(8,128)(2,1)}, u32[]{:S(2)}) copy-start(bf16[1280,768]{1,0:T(8,128)(2,1)} %copy-done.2) | copy-start | bytes 5898244
  60.8 2.1 %copy-start.5 = (bf16[1280,768]{1,0:T(8,128)(2,1)S(1)}, bf16[1280,768]{1,0:T(8,128)(2,1)}, u32[]{:S(2)}) copy-start(bf16[1280,768]{1,0:T(8,128)(2,1)} %copy-done.4) | copy-start | bytes 5898244
  65.4 1.8 %collective-permute-start.16 = (f32[328,128]{1,0:T(8,128)S(1)}, f32[328,128]{1,0:T(8,128)S(1)}, u32[]{:S(2)}, u32[]{:S(2)}) collective-permute-start(f32[328,128]{1,0:T(8,128)S(1)} %get-tuple-element.129), channel_id=1, source_target_pairs={{0,2},{2,0},{4,6},{6,4},{8,10},{10,8},{12,14},{14,12},{16,18},{18,... | collective-permute-start | bytes 503816 | tf_op jit(solution)/shard_map/ppermute | solution.py:583
  67.2 7.5 %collective-permute-start.17 = (f32[320,128]{1,0:T(8,128)S(1)}, f32[320,128]{1,0:T(8,128)S(1)}, u32[]{:S(2)}, u32[]{:S(2)}) collective-permute-start(f32[320,128]{1,0:T(8,128)S(1)} %get-tuple-element.130.side_b), channel_id=1, source_target_pairs={{0,30},{2,4},{4,2},{6,8},{8,6},{10,12},{12,10},{14,16},{16,14},{18... | collective-permute-start | bytes 491528 | tf_op jit(solution)/shard_map/ppermute | solution.py:589
  70.0 5.5 %collective-permute-start.18 = (f32[336,128]{1,0:T(8,128)S(1)}, f32[336,128]{1,0:T(8,128)S(1)}, u32[]{:S(2)}, u32[]{:S(2)}) collective-permute-start(f32[336,128]{1,0:T(8,128)S(1)} %get-tuple-element.136.left), channel_id=1, source_target_pairs={{0,1},{1,0},{2,3},{3,2},{4,5},{5,4},{6,7},{7,6},{8,9},{9,8},{10,11... | collective-permute-start | bytes 516104 | tf_op jit(solution)/shard_map/ppermute | solution.py:593
  74.8 8.3 %collective-permute-start.20 = (f32[384,128]{1,0:T(8,128)S(1)}, f32[384,128]{1,0:T(8,128)S(1)}, u32[]{:S(2)}, u32[]{:S(2)}) collective-permute-start(f32[384,128]{1,0:T(8,128)S(1)} %add_b.3.side_b), channel_id=1, source_target_pairs={{0,1},{1,0},{2,3},{3,2},{4,5},{5,4},{6,7},{7,6},{8,9},{9,8},{10,11... | collective-permute-start | bytes 589832 | tf_op jit(solution)/shard_map/ppermute | solution.py:593
  75.5 7.6 %collective-permute-start.19 = (f32[336,128]{1,0:T(8,128)S(1)}, f32[336,128]{1,0:T(8,128)S(1)}, u32[]{:S(2)}, u32[]{:S(2)}) collective-permute-start(f32[336,128]{1,0:T(8,128)S(1)} %add_a.3.side_a), channel_id=1, source_target_pairs={{0,30},{2,4},{4,2},{6,8},{8,6},{10,12},{12,10},{14,16},{16,14},{18... | collective-permute-start | bytes 516104 | tf_op jit(solution)/shard_map/ppermute | solution.py:589
  83.1 1.5 %collective-permute-start.21 = (f32[328,128]{1,0:T(8,128)S(1)}, f32[328,128]{1,0:T(8,128)S(1)}, u32[]{:S(2)}, u32[]{:S(2)}) collective-permute-start(f32[328,128]{1,0:T(8,128)S(1)} %get-tuple-element.142), channel_id=1, source_target_pairs={{0,2},{2,0},{4,6},{6,4},{8,10},{10,8},{12,14},{14,12},{16,18},{18,... | collective-permute-start | bytes 503816 | tf_op jit(solution)/shard_map/ppermute | solution.py:583
  88.7 5.0 %collective-permute-start.22 = (f32[5,64,128]{2,1,0:T(8,128)S(1)}, f32[5,64,128]{2,1,0:T(8,128)S(1)}, u32[]{:S(2)}, u32[]{:S(2)}) collective-permute-start(f32[5,64,128]{2,1,0:T(8,128)S(1)} %get-tuple-element.147), channel_id=1, source_target_pairs={{0,2},{2,0},{4,6},{6,4},{8,10},{10,8},{12,14},{14,12},{16,18},{18,... | collective-permute-start | bytes 491528 | tf_op jit(solution)/shard_map/ppermute | solution.py:583
  89.2 7.4 %collective-permute-start.23 = (f32[5,64,128]{2,1,0:T(8,128)S(1)}, f32[5,64,128]{2,1,0:T(8,128)S(1)}, u32[]{:S(2)}, u32[]{:S(2)}) collective-permute-start(f32[5,64,128]{2,1,0:T(8,128)S(1)} %get-tuple-element.148), channel_id=1, source_target_pairs={{0,30},{2,4},{4,2},{6,8},{8,6},{10,12},{12,10},{14,16},{16,14},{18... | collective-permute-start | bytes 491528 | tf_op jit(solution)/shard_map/ppermute | solution.py:589
where the time goes:
time: 97.6 us; the launch traced here: 97.4 us
  Pallas kernels  33.7 us (35%)
  starting transfers between devices  32.9 us (34%)
  waiting for transfers between devices  28.6 us (29%)
  local copies, waits for them, and re-layouts  1.25 us (1%)
    pallas_call x27, Pallas kernels, call(): pl.pallas_call(kernel, out_shape=list(outs), in_specs=specs, out_specs=[p...  29.3 us
    ppermute x7, waiting for transfers between devices, to_edge(): return lax.ppermute(value, 'grid', route)  25.6 us
    ppermute x7, starting transfers between devices, to_edge(): return lax.ppermute(value, 'grid', route)  20.1 us
    ppermute x8, starting transfers between devices, to_orb(): return lax.ppermute(value, 'orb', [(0, 1), (1, 0)])  9.58 us
    pallas_call x1, Pallas kernels, sort_basis(): pl.pallas_call(functools.partial(sort_kernel, total_blocks), out_shape=ha...  3.28 us
    ppermute x9, starting transfers between devices, to_core(): return lax.ppermute(value, 'grid', [(i, i ^ 1) for i in range(count)])  3.24 us
    ppermute x8, waiting for transfers between devices, to_orb(): return lax.ppermute(value, 'orb', [(0, 1), (1, 0)])  2.57 us
  transfers between devices with their start and end apart: 24, of which 10 were waited for; matrix products, arithmetic and copies ran while one was open for 1% of the time, Pallas kernels for 21%

commit v1 on v0

--- a/solution.py
+++ b/solution.py
@@ -26,6 +26,7 @@
 PAIR = PACKED + NB
 GIVE_ROWS = PAIR + HALF
 EARLY = 9
+STRIP = HALF + TILE
 KEEP_AT = 2 * NB + HALF
 
 
@@ -38,7 +39,9 @@
     def one(a, b):
         return lax.dot_general(a, b, (contract, ((), ())), preferred_element_type=f32)
 
-    return one(left[0], right[0]) + (one(left[0], right[1]) + one(left[1], right[0]))
+    cross_left = jnp.concatenate([left[0], left[1]], axis=contract[0][0])
+    cross_right = jnp.concatenate([right[1], right[0]], axis=contract[1][0])
+    return one(left[0], right[0]) + one(cross_left, cross_right)
 
 
 def both(pair, *index):
@@ -103,7 +106,7 @@
     done[...] = jnp.zeros_like(done)
 
 
-def cut_kernel(own, halves, other, near, early, rest, sems):
+def cut_kernel(lists, own, halves, other, near, early, rest, row, sems):
     copies = [
         pltpu.make_async_copy(own, near, sems.at[0]),
         pltpu.make_async_copy(halves.at[pl.ds(0, EARLY)], early, sems.at[1]),
@@ -111,6 +114,12 @@
     ]
     for copy in copies:
         copy.start()
+    lanes = lax.broadcasted_iota(jnp.int32, (TILE, NB), 1)
+    values = jnp.zeros((TILE, NB), f32)
+    for d in range(2):
+        for i in range(4):
+            values = jnp.where(lanes == 4 * d + i, lists[d, i].astype(f32), values)
+    row[...] = values
     for copy in copies:
         copy.wait()
 
@@ -119,16 +128,19 @@
     return pltpu.with_memory_space_constraint(value, pltpu.HBM)
 
 
-def cut(own, halves, other):
+def cut(lists, own, halves, other):
     return pl.pallas_call(
         cut_kernel,
-        out_shape=[vmem(own.shape), vmem((EARLY, HALF, NB)), vmem((16 - EARLY, HALF, NB))],
-        in_specs=[pl.BlockSpec(memory_space=pl.ANY)] * 2 + [pl.BlockSpec(memory_space=pltpu.VMEM)],
-        out_specs=[pl.BlockSpec(memory_space=pltpu.VMEM)] * 3,
+        out_shape=[vmem(own.shape), vmem((EARLY, HALF, NB)), vmem((16 - EARLY, HALF, NB))]
+        + [vmem((TILE, NB))],
+        in_specs=[pl.BlockSpec(memory_space=pltpu.SMEM)]
+        + [pl.BlockSpec(memory_space=pl.ANY)] * 2
+        + [pl.BlockSpec(memory_space=pltpu.VMEM)],
+        out_specs=[pl.BlockSpec(memory_space=pltpu.VMEM)] * 4,
         scratch_shapes=[pltpu.SemaphoreType.DMA((3,))],
         compiler_params=pltpu.CompilerParams(vmem_limit_bytes=VMEM_BYTES),
         name="cut",
-    )(hbm(own), hbm(halves), other)
+    )(hbm(lists), hbm(own), hbm(halves), other)
 
 
 def hold_kernel(value, done, out):
@@ -227,13 +239,17 @@
     out_b[rows_b, :] = side_b[rows_b, :] + arrived[PACKED:PAIR, :]
 
 
+def near_keep_kernel(side_a, side_b, keep, arrived, out_a, out_b):
+    near_kernel(side_a, side_b, keep, arrived, out_a.at[:A_ROWS], out_b, out_a.at[A_ROWS:])
+
+
 def add_kernel(left, right, out):
     out[...] = left[...] + right[...]
 
 
-def add_keep_kernel(side_b, arrived, keep, out):
-    out[:KEEP_AT, :] = side_b[...] + arrived[...]
-    out[KEEP_AT:, :] = keep[...]
+def add_keep_kernel(side_a, arrived, out, keep):
+    out[...] = side_a[:A_ROWS, :] + arrived[:A_ROWS, :]
+    keep[...] = side_a[A_ROWS:, :] + arrived[A_ROWS:, :]
 
 
 def side_near(out_a, out_b, near):
@@ -245,21 +261,23 @@
     near[PAIR:, :] = out_b[KEEP_AT:, :]
 
 
-def total_kernel(side_a, arrived_a, side_b, arrived_b, out_a, out_b, near):
+def total_kernel(side_a, arrived_a, side_b, arrived_b, keep, out_a, out_b, near):
     out_a[...] = side_a[...] + arrived_a[...]
-    out_b[...] = side_b[...] + arrived_b[...]
-    side_near(out_a, out_b, near)
-
-
-def join_kernel(side_a, side_b, keep, arrived, out, out_keep):
-    near_kernel(side_a, side_b, keep, arrived, out.at[:A_ROWS], out.at[A_ROWS:], out_keep)
-
-
-def total_grid_kernel(side, arrived, keep, out_a, out_b, near):
-    out_a[...] = side[:A_ROWS, :] + arrived[:A_ROWS, :]
-    out_b[:KEEP_AT, :] = side[A_ROWS:, :] + arrived[A_ROWS:, :]
+    out_b[:KEEP_AT, :] = side_b[...] + arrived_b[...]
     out_b[KEEP_AT:, :] = keep[...]
     side_near(out_a, out_b, near)
+
+
+def near_sum_kernel(near, keep, arrived, out, out_keep):
+    out[:PAIR, :] = near[...] + arrived[:PAIR, :]
+    out[PAIR:, :] = jnp.zeros((STRIP, NB), f32)
+    out_keep[...] = keep[...] + arrived[PAIR:, :]
+
+
+def near_total_kernel(near, keep, mine, arrived, out, cross):
+    out[:PAIR, :] = near[:PAIR, :] + arrived[:PAIR, :]
+    cross[...] = mine[PAIR:, :] + arrived[PAIR:, :]
+    out[PAIR:, :] = keep[...]
 
 
 def add_density(terms, th, tl, before, after):
@@ -309,32 +327,44 @@
     add_density(terms, th, tl, lambda cols: jnp.zeros((1, POINT_CHUNK), f32), store)
 
 
-def far_kernel(lists, edge, sorted_first, out):
+def far_kernel(row, edge, sorted_first, out):
     first = 1 - core_of()
     for i in range(5):
         out[i * HALF : (i + 1) * HALF, :] = edge[i + first]
-    lanes = lax.broadcasted_iota(jnp.int32, (TILE, NB), 1)
-    row = jnp.zeros((TILE, NB), f32)
-    for d in range(2):
-        for i in range(4):
-            row = jnp.where(lanes == 4 * d + i, lists[d, i].astype(f32), row)
-    out[5 * HALF :, :] = row
-
-
-def rho_side(th, tl, side_a, side_b, rho):
-    core = core_of()
-    low, cross, high = side_parts(side_a, side_b)
-    at = core * SB
-    terms = [
-        (split(upper_form(low)), at, SB, [(at, SB)]),
-        (split(upper_form(high)), at + SB, SB, [(at + SB, SB)]),
-        (split(cross * 2.0), at + SB, NB, [(at + NB, NB)]),
-    ]
-
+    out[5 * HALF :, :] = row[...]
+
+
+def packed_part(ref):
+    return ref[:NB, :], ref[NB : NB + 1, :], ref[PACKED:PAIR, :]
+
+
+def rho_near(th, tl, near, cross, rho):
     def store(cols, value):
         rho[:, cols] = value
 
+    side = core_of() * SB
+    terms = [
+        (split(upper_form(packed_part(near))), SB, SB, [(SB, SB)]),
+        (split(cross[...] * 2.0), side + SB, NB, [(side + NB, NB)]),
+    ]
     add_density(terms, th, tl, lambda cols: jnp.zeros((1, POINT_CHUNK), f32), store)
+
+
+def rho_other(th, tl, before, near, other, rho, mid):
+    core = core_of()
+    mid[pl.ds(aligned(core, HALF), HALF), :] = near[PAIR:, :]
+    mid[pl.ds(aligned(1 - core, HALF), HALF), :] = other[PAIR:, :]
+    at = (2 - 2 * core) * SB
+    row = (3 - 2 * core) * NB
+    terms = [
+        (split(upper_form(packed_part(other))), at, SB, [(at, SB)]),
+        (split(mid[...] * 2.0), row + NB, NB, [(row, NB)]),
+    ]
+
+    def store(cols, value):
+        rho[:, cols] = value
+
+    add_density(terms, th, tl, lambda cols: before[:, cols], store)
 
 
 def scaled_rows(th, tl, at, count, scale):
@@ -351,10 +381,12 @@
     core = core_of()
 
     def store(cols, value):
-        potential = external[:, cols] - jnp.exp(jnp.log(value * value + 1.0) * (1.0 / 6.0))
-        scale[:, cols] = weights[:, cols] * potential
+        scale[:, cols] = value
 
     add_density(terms, th, tl, lambda cols: rho[:, cols], store)
+    value = scale[...]
+    potential = external[...] - jnp.exp(jnp.log(value * value + 1.0) * (1.0 / 6.0))
+    scale[...] = weights[...] * potential
     at = (2 - 2 * core) * SB
     pair = fock_block(scaled_rows(th, tl, at, SB, scale), nh, nl, at, SB)
     row = (3 - 2 * core) * NB
@@ -382,16 +414,13 @@
 
 
 def fock_other_later(
-    weights, external, th, tl, nh, nl, rho, side_b, other, scale, give, keep, cross_ref
+    weights, external, th, tl, nh, nl, rho, mine, arrived, scale, give, keep, cross_ref
 ):
-    core = core_of()
-    part, cross = other_parts(side_b, other, cross_ref)
-    at = (2 - 2 * core) * SB
-    row = (3 - 2 * core) * NB
-    terms = [
-        (split(upper_form(part)), at, SB, [(at, SB)]),
-        (split(cross * 2.0), row + NB, NB, [(row, NB)]),
+    at = core_of() * 2 * SB
+    part = [
+        a + b for a, b in zip(packed_part(mine), packed_part(arrived))
     ]
+    terms = [(split(upper_form(part)), at, SB, [(at, SB)])]
     fock_other(terms, weights, external, th, tl, nh, nl, rho, scale, give, keep, cross_ref)
 
 
@@ -408,7 +437,7 @@
 
 
 def spread_kernel(
-    total_blocks, own_lists, other_lists, own, early, partner, coef, ch, cl, th, tl
+    total_blocks, own_lists, other_lists, own, early, partner, coef, ch, cl, th, tl, present
 ):
     coef[...] = jnp.zeros_like(coef)
     for d in range(4):
@@ -424,10 +453,26 @@
                 value = early[index] if index < EARLY else partner[index - EARLY]
                 coef[pl.ds(at + half * HALF, HALF), cols] = value
     coefficient_parts(coef[...], ch, cl, th, tl)
-
-
-def turn_kernel(coef, th, tl):
-    th[...], tl[...] = split(coef[...].T)
+    for d in range(4):
+        blocks = own_lists if d < 2 else other_lists
+        for r in range(6):
+            held = relative(blocks[d % 2, 0], total_blocks) == r
+            for i in range(1, 4):
+                held = held | (relative(blocks[d % 2, i], total_blocks) == r)
+            row = 6 * d + r
+            present[row : row + 1, :] = jnp.full((1, NB), jnp.where(held, 1.0, 0.0), f32)
+
+
+def gather_kernel(first, second, coef, ch, cl, th, tl):
+    core = core_of()
+    for source, at, block, count in (
+        (first, 0, 4 * core, 2),
+        (first, SB, 2 + core, 1),
+        (second, 0, 4 - 4 * core, 2),
+        (second, SB, 3 - core, 1),
+    ):
+        coef[pl.ds(aligned(block, NB), count * NB), :] = source[at : at + count * NB, :]
+    coefficient_parts(coef[...], ch, cl, th, tl)
 
 
 def mixing(th, tl, at, count, gradient):
@@ -458,9 +503,8 @@
         mixed[d] = value
 
 
-def domain_new(
-    total_blocks, own_lists, other_lists, coef, ch, cl, th, tl, gradient, mixed, side_b, other,
-    fresh, fh, fl, work, cross_ref,
+def domain_mixed(
+    ch, cl, th, tl, gradient, mixed, side_b, other, work, total, cross_ref
 ):
     core = core_of()
     part, cross = other_parts(side_b, other, cross_ref)
@@ -483,98 +527,191 @@
     work[side_block, :] += product[SB:]
     first = mixing(th, tl, other_at, SB, split(work[other_rows, :]))
     second = mixing(th, tl, (3 - core) * NB, NB, split(product[SB:]))
-    total = [mixed[d] + first[d] + second[d] for d in range(4)]
+    for d in range(4):
+        total[d] = mixed[d] + first[d] + second[d]
+
+
+def new_blocks(present, coef, ch, cl, work, total, places, fresh, fh, fl):
+    zero = jnp.zeros((NB, NB), f32)
     for d in range(0, 4, 2):
         cols = slice(d * NB, (d + 2) * NB)
         square = split(join(total[d], zero, zero, total[d + 1]))
-        moved = dot3((ch[:, cols], cl[:, cols]), square)
-        for r in range(6):
-            rows = slice(r * NB, (r + 1) * NB)
-            for e in range(2):
-                blocks = own_lists if d == 0 else other_lists
-                present = relative(blocks[e, 0], total_blocks) == r
-                for i in range(1, 4):
-                    present = present | (relative(blocks[e, i], total_blocks) == r)
-                at = slice((d + e) * NB, (d + e + 1) * NB)
-                kept = jnp.where(present, work[rows, at], 0.0)
-                value = coef[rows, at] - step_scale * (kept - moved[rows, e * NB : (e + 1) * NB])
-                fresh[rows, at] = value
-                fh[rows, at], fl[rows, at] = split(value)
-
-
-def outer(fh, fl, at, count, from_at, from_count):
-    left = pl.ds(pl.multiple_of(at, HALF), count)
-    right = pl.ds(pl.multiple_of(from_at, NB), from_count)
-    return dot3((fh[left, :], fl[left, :]), (fh[right, :], fl[right, :]), ((1,), (1,)))
+        for block, count, at in places:
+            rows = pl.ds(aligned(block, NB), count * NB)
+            moved = dot3((ch[rows, cols], cl[rows, cols]), square)
+            for r in range(count):
+                rows = pl.ds(aligned(block + r, NB), NB)
+                out_rows = slice(at + r * NB, at + (r + 1) * NB)
+                for e in range(2):
+                    out_cols = slice((d + e) * NB, (d + e + 1) * NB)
+                    kept = work[rows, out_cols] * present[pl.ds(6 * (d + e) + block + r, 1), :]
+                    piece = moved[r * NB : (r + 1) * NB, e * NB : (e + 1) * NB]
+                    value = coef[rows, out_cols] - step_scale * (kept - piece)
+                    fresh[out_rows, out_cols] = value
+                    fh[out_rows, out_cols], fl[out_rows, out_cols] = split(value)
+
+
+def outer(left, at, count, right, from_at, from_count):
+    left_rows, right_rows = pl.ds(at, count), pl.ds(from_at, from_count)
+    return dot3(
+        (left[0][left_rows, :], left[1][left_rows, :]),
+        (right[0][right_rows, :], right[1][right_rows, :]),
+        ((1,), (1,)),
+    )
+
+
+def domain_far_rows(
+    present, coef, ch, cl, th, tl, gradient, mixed, side_b, other,
+    fresh, fh, fl, work, total, cross_ref,
+):
+    domain_mixed(ch, cl, th, tl, gradient, mixed, side_b, other, work, total, cross_ref)
+    core = core_of()
+    places = ((4 * core, 2, 0), (2 + core, 1, SB))
+    new_blocks(present, coef, ch, cl, work, total, places, fresh, fh, fl)
+
+
+def domain_far(
+    present, coef, ch, cl, th, tl, gradient, mixed, side_b, other,
+    fresh, fh, fl, work, total, message, cross_ref,
+):
+    domain_far_rows(
+        present, coef, ch, cl, th, tl, gradient, mixed, side_b, other,
+        fresh, fh, fl, work, total, cross_ref,
+    )
+    core = core_of()
+    far = (fh, fl)
+    put_pair(outer(far, 0, SB, far, 0, SB), message.at[:PACKED], message.at[PACKED:PAIR])
+    cross = outer(far, SB, NB, far, aligned(1 - core, NB), NB)
+    message[PAIR:, :] = jnp.where(core == 0, cross.T, cross)
+
+
+def other_blocks(present, coef, ch, cl, work, total, fresh, fh, fl):
+    core = core_of()
+    places = ((4 - 4 * core, 2, 0), (3 - core, 1, SB))
+    new_blocks(present, coef, ch, cl, work, total, places, fresh, fh, fl)
 
 
 def domain_other(
-    total_blocks, own_lists, other_lists, coef, ch, cl, th, tl, gradient, mixed, side_b, other,
-    fresh, fh, fl, give, keep, work, cross_ref,
+    present, coef, ch, cl, work, total, fresh, fh, fl, give, keep, cross_ref
 ):
-    domain_new(
-        total_blocks, own_lists, other_lists, coef, ch, cl, th, tl, gradient, mixed, side_b,
-        other, fresh, fh, fl, work, cross_ref,
-    )
-    core = core_of()
-    at = (2 - 2 * core) * SB
-    row = (3 - 2 * core) * NB
-    cross_ref[...] = outer(fh, fl, row, NB, row + NB, NB)
-    put_other(outer(fh, fl, at, SB, at, SB), cross_ref, give, keep)
-
-
-def density_side(fh, fl, side_a, side_b):
-    at = core_of() * SB
-    cross = outer(fh, fl, at + NB, NB, at + SB, NB)
-    put_side(
-        outer(fh, fl, at, SB, at, SB), cross, outer(fh, fl, at + SB, SB, at + SB, SB),
-        side_a, side_b,
-    )
-
-
-def owner_half(fh, fl, pair, target, first):
-    half = lax.axis_index("orb") * HALF
+    other_blocks(present, coef, ch, cl, work, total, fresh, fh, fl)
+    core = core_of()
+    rest = (fh, fl)
+    cross = outer(rest, SB, NB, rest, aligned(core, NB), NB)
+    cross_ref[...] = jnp.where(core == 0, cross, cross.T)
+    put_other(outer(rest, 0, SB, rest, 0, SB), cross_ref, give, keep)
+
+
+def near_rows(f1, f2):
+    core = core_of()
+    touching, beside = f1[SB:, :], f2[SB:, :]
+    return jnp.concatenate(
+        [jnp.where(core == 0, touching, beside), jnp.where(core == 0, beside, touching)], axis=0
+    )
+
+
+def density_near(f1h, f1l, f2h, f2l, near):
+    rows = (near_rows(f1h, f2h), near_rows(f1l, f2l))
+    put_pair(dot3(rows, rows, ((1,), (1,))), near.at[:PACKED], near.at[PACKED:])
+
+
+def half_rows(ref):
+    def store(index, value):
+        ref[pl.ds(aligned(index, HALF), HALF), :] = value
+
+    return store
+
+
+def half_blocks(ref):
+    def store(index, value):
+        ref[index] = value
+
+    return store
+
+
+def owner_half(left, store, first):
+    half = lax.axis_index("orb")
     for i in range(2):
-        rows = outer(fh, fl, pair * SB + i * NB + half, HALF, pair * SB, SB)
-        target[2 * i + 1 - first] = rows[:, :NB]
-        target[2 * i + 2 - first] = rows[:, NB:]
-
-
-def end_half(fh, fl, row, col):
-    return outer(fh, fl, row * NB + lax.axis_index("orb") * HALF, HALF, col * NB, NB)
+        rows = outer(left, pl.multiple_of(i * NB + half * HALF, HALF), HALF, left, 0, SB)
+        store(2 * i + 1 - first, rows[:, :NB])
+        store(2 * i + 2 - first, rows[:, NB:])
 
 
 def domain_edge(
-    total_blocks, own_lists, other_lists, coef, ch, cl, th, tl, gradient, mixed, side_b, other,
-    fresh, fh, fl, edge, give, work, cross_ref,
+    present, coef, ch, cl, th, tl, gradient, mixed, side_b, other,
+    fresh, fh, fl, work, total, edge, cross_ref,
 ):
-    domain_new(
-        total_blocks, own_lists, other_lists, coef, ch, cl, th, tl, gradient, mixed, side_b,
-        other, fresh, fh, fl, work, cross_ref,
-    )
-    core = core_of()
-    owner_half(fh, fl, 2 * core, edge, 1 - core)
-    edge[4 - 4 * core] = end_half(fh, fl, 1 + 3 * core, 2 + core)
-    owner_half(fh, fl, 2 - 2 * core, give, core)
-    give[4 * core] = end_half(fh, fl, 4 - 3 * core, 3 - core)
-
-
-def domain_last(total_blocks, own_lists, fresh, fh, fl, result, own):
-    owner_half(fh, fl, 1, own, 0)
-    own[0] = end_half(fh, fl, 2, 1)
-    own[5] = end_half(fh, fl, 3, 4)
+    domain_far_rows(
+        present, coef, ch, cl, th, tl, gradient, mixed, side_b, other,
+        fresh, fh, fl, work, total, cross_ref,
+    )
+    core = core_of()
+    far = (fh, fl)
+    owner_half(far, half_rows(edge), 1 - core)
+    edge[5 * HALF :, :] = jnp.zeros((2 * TILE, NB), f32)
+    at = pl.multiple_of((1 - core) * NB + lax.axis_index("orb") * HALF, HALF)
+    half_rows(edge)(4 - 4 * core, outer(far, at, HALF, far, SB, NB))
+
+
+def domain_give(present, coef, ch, cl, work, total, fresh, fh, fl, give):
+    other_blocks(present, coef, ch, cl, work, total, fresh, fh, fl)
+    core = core_of()
+    rest = (fh, fl)
+    owner_half(rest, half_blocks(give), core)
+    at = pl.multiple_of(core * NB + lax.axis_index("orb") * HALF, HALF)
+    give[4 * core] = outer(rest, at, HALF, rest, SB, NB)
+
+
+def domain_last(total_blocks, own_lists, fresh1, f1h, f1l, fresh2, f2h, f2l, result, own, window, nh, nl):
+    core = core_of()
+    half = lax.axis_index("orb")
+    nh[...] = near_rows(f1h, f2h)
+    nl[...] = near_rows(f1l, f2l)
+    near = (nh, nl)
+    owner_half(near, half_blocks(own), 0)
+    rows = pl.multiple_of(half * HALF, HALF)
+
+    def far_or_rest(row_at, first_at, second_at):
+        left = (nh[pl.ds(row_at, HALF), :], nl[pl.ds(row_at, HALF), :])
+        first = pl.ds(first_at, NB)
+        second = pl.ds(second_at, NB)
+        right = [
+            jnp.where(core == 0, a[first, :], b[second, :]) for a, b in ((f1h, f2h), (f1l, f2l))
+        ]
+        return dot3(left, right, ((1,), (1,)))
+
+    def rest_or_far(row_at, first_at, second_at):
+        left = (nh[pl.ds(row_at, HALF), :], nl[pl.ds(row_at, HALF), :])
+        first = pl.ds(first_at, NB)
+        second = pl.ds(second_at, NB)
+        right = [
+            jnp.where(core == 0, b[first, :], a[second, :]) for a, b in ((f1h, f2h), (f1l, f2l))
+        ]
+        return dot3(left, right, ((1,), (1,)))
+
+    own[0] = far_or_rest(rows, NB, NB)
+    own[5] = rest_or_far(pl.multiple_of(NB + half * HALF, HALF), 0, 0)
+    for source, at, block, count in (
+        (fresh1, 0, 4 * core, 2),
+        (fresh1, SB, 2 + core, 1),
+        (fresh2, 0, 4 - 4 * core, 2),
+        (fresh2, SB, 3 - core, 1),
+    ):
+        window[pl.ds(aligned(block, NB), count * NB), :] = source[at : at + count * NB, :SB]
     for d in range(2):
         for i in range(4):
             at = aligned(relative(own_lists[d, i], total_blocks), NB)
-            result[d, i] = fresh[pl.ds(at, NB), d * NB : (d + 1) * NB]
+            result[d, i] = window[pl.ds(at, NB), d * NB : (d + 1) * NB]
 
 
 def owner_kernel(own, from_core, from_edge, out):
     core = core_of()
-    lower = jnp.where(core == 0, from_core[...], from_edge[...])
-    upper = jnp.where(core == 0, from_edge[...], from_core[...])
+    edge = [from_edge[i * HALF : (i + 1) * HALF, :] for i in range(5)]
+    lower = [jnp.where(core == 0, from_core[i], edge[i]) for i in range(5)]
+    upper = [jnp.where(core == 0, edge[i], from_core[i]) for i in range(5)]
     out[0] = own[0] + upper[0]
-    out[1:5] = own[1:5] + upper[1:] + lower[:4]
+    for i in range(1, 5):
+        out[i] = own[i] + upper[i] + lower[i - 1]
     out[5] = own[5] + lower[4]
 
 
@@ -603,32 +740,24 @@
 
 def total_over_all(made, before_last, before_sum):
     side_a, side_b, keep, arrived = made
-    side_a, side_b, keep = call(
-        near_kernel, (side_a, side_b, keep, arrived), (A_OUT, B_OUT, KEEP_OUT), "add_near"
+    side_a, side_b = call(
+        near_keep_kernel,
+        (side_a, side_b, keep, arrived),
+        (vmem((A_ROWS + HALF, NB)), B_OUT),
+        "add_near",
     )
     first_b = to_edge(side_b)
     first_a = to_orb(side_a)
-    (side_a,) = call(add_kernel, (side_a, first_a), (A_OUT,), "add_a")
-    (side_b,) = call(add_keep_kernel, (side_b, first_b, keep), (BK_OUT,), "add_b")
+    side_a, keep = call(add_keep_kernel, (side_a, first_a), (A_OUT, KEEP_OUT), "add_a")
     last_a = to_edge(side_a)
+    (side_b,) = call(add_kernel, (side_b, first_b), (B_OUT,), "add_b")
     side_b = before_last(side_b)
     last_b = before_sum(to_orb(side_b))
     side_a, side_b, near = call(
-        total_kernel, (side_a, last_a, side_b, last_b), (A_OUT, BK_OUT, GIVE_OUT), "add_all"
-    )
-    return side_a, side_b, to_core(near)
-
-
-def total_over_grid(made):
-    side_a, side_b, keep, arrived = made
-    side, keep = call(
-        join_kernel,
-        (side_a, side_b, keep, arrived),
-        (vmem((A_ROWS + B_ROWS, NB)), KEEP_OUT),
-        "add_near",
-    )
-    side_a, side_b, near = call(
-        total_grid_kernel, (side, to_edge(side), keep), (A_OUT, BK_OUT, GIVE_OUT), "add_all"
+        total_kernel,
+        (side_a, last_a, side_b, last_b, keep),
+        (A_OUT, BK_OUT, GIVE_OUT),
+        "add_all",
     )
     return side_a, side_b, to_core(near)
 
@@ -653,16 +782,15 @@
     other = to_core(own)
     *basis, done = sort_basis(total_blocks, batch_blocks, basis_values, unit)
     th, tl, nh, nl = basis
-    near, early, rest = cut(own, blocks.reshape(16, HALF, NB), other)
+    near, early, rest, list_row = cut(domain_blocks, own, blocks.reshape(16, HALF, NB), other)
     early = to_orb(early)
     (own_far,) = call(hold_kernel, (own_far, done), (vmem((6, HALF, NB)),), "hold")
     other_far = to_core(own_far)
     (edge_message,) = call(
         far_kernel,
-        (domain_blocks, edge, done),
+        (list_row, edge, done),
         (vmem((5 * HALF + TILE, NB)),),
         "far_message",
-        smem=(0,),
     )
     edge_far = to_orb(edge_message)
     (rho,) = call(
@@ -681,9 +809,7 @@
         if iteration == 0:
             kernel, operands = fock_other_first, (edge_far,)
         else:
-            side_a, side_b, arriving = packed
-            (rho,) = call(rho_side, (th, tl, side_a, side_b), (row_out,), "rho_side", flops=3 * unit)
-            kernel, operands = fock_other_later, (side_b, arriving)
+            kernel, operands = fock_other_later, packed
         scale, give, keep = call(
             kernel,
             (quad_weights, ext_potential, *basis, rho, *operands),
@@ -703,8 +829,14 @@
             if iteration == 0:
                 value, ready["partner"] = lax.optimization_barrier((value, partner))
                 return value
-            turned = call(turn_kernel, (coef,), (turned_half, turned_half), "turn", flops=unit)
-            value, *ready["turned"] = lax.optimization_barrier((value, *turned))
+            gathered = call(
+                gather_kernel,
+                (fresh1, fresh2),
+                (coef_out, coef_half, coef_half, turned_half, turned_half),
+                "gather",
+                flops=unit,
+            )
+            value, *ready["gathered"] = lax.optimization_barrier((value, *gathered))
             return value
 
         def before_sum(value):
@@ -713,7 +845,7 @@
             spread = call(
                 functools.partial(spread_kernel, total_blocks),
                 (domain_blocks, other_lists, blocks, hbm(early), hbm(ready["partner"])),
-                (coef_out, coef_half, coef_half, turned_half, turned_half),
+                (coef_out, coef_half, coef_half, turned_half, turned_half, vmem((24, NB))),
                 "spread",
                 smem=(0, 1),
                 plain=(2, 3, 4),
@@ -726,9 +858,9 @@
             (side_a, side_b, keep, arrived), before_last, before_sum
         )
         if iteration == 0:
-            coef, *halves = ready["spread"]
+            coef, *halves, present = ready["spread"]
         else:
-            halves = (ch, cl, *ready["turned"])
+            coef, *halves = ready["gathered"]
         gradient, mixed = call(
             domain_side,
             (side_a, side_b, *halves),
@@ -737,41 +869,73 @@
             flops=unit,
         )
         operands = (
-            domain_blocks, other_lists, coef, *halves, gradient, mixed, side_b, arriving
+            present, coef, *halves, gradient, mixed, side_b, arriving
         )
-        scratch = (coef_out, CROSS)
+        new_outs = (vmem((3 * NB, 4 * NB)),) + (vmem((3 * NB, 4 * NB), bf16),) * 2
+        far_outs = new_outs + (coef_out, vmem((4, NB, NB)))
         if iteration < ITERS - 1:
-            coef, ch, cl, give, keep = call(
-                functools.partial(domain_other, total_blocks),
+            fresh1, f1h, f1l, work, total, mine = call(
+                domain_far,
                 operands,
-                (coef_out, coef_half, coef_half, GIVE_OUT, KEEP_OUT),
-                "domain_other",
-                scratch=scratch,
-                smem=(0, 1),
+                far_outs + (vmem((PAIR + NB, NB)),),
+                "domain_far",
+                scratch=(CROSS,),
                 flops=2 * unit,
             )
+            from_far = to_edge(mine)
+            fresh2, f2h, f2l, give, keep = call(
+                domain_other,
+                (present, coef, *halves[:2], work, total),
+                new_outs + (GIVE_OUT, KEEP_OUT),
+                "domain_other",
+                scratch=(CROSS,),
+                flops=unit,
+            )
             arrived = to_core(give)
-            side_a, side_b = call(density_side, (ch, cl), (A_OUT, B_OUT), "density_side", flops=unit)
-            packed = total_over_grid((side_a, side_b, keep, arrived))
+            (near,) = call(
+                density_near, (f1h, f1l, f2h, f2l), (vmem((PAIR, NB)),), "density_near"
+            )
+            near, keep = call(
+                near_sum_kernel,
+                (near, keep, arrived),
+                (vmem((PAIR + STRIP, NB)), KEEP_OUT),
+                "add_near",
+            )
+            from_near = to_edge(near)
+            near_total, cross = call(
+                near_total_kernel, (near, keep, mine, from_far), (GIVE_OUT, CROSS), "add_far"
+            )
+            arriving = to_core(near_total)
+            (rho,) = call(rho_near, (th, tl, near_total, cross), (row_out,), "rho_near", flops=unit)
+            (rho,) = call(
+                rho_other,
+                (th, tl, rho, near_total, arriving),
+                (row_out,),
+                "rho_other",
+                scratch=(CROSS,),
+            )
+            packed = (mine, from_near)
     message = vmem((5, HALF, NB))
-    coef, ch, cl, edge, give = call(
-        functools.partial(domain_edge, total_blocks),
-        operands,
-        (coef_out, coef_half, coef_half, message, message),
-        "domain_edge",
-        scratch=scratch,
-        smem=(0, 1),
-        flops=2 * unit,
+    edge_message = vmem((5 * HALF + 2 * TILE, NB))
+    fresh1, f1h, f1l, work, total, edge = call(
+        domain_edge, operands, far_outs + (edge_message,), "domain_edge", scratch=(CROSS,), flops=2 * unit
     )
     from_edge = to_edge(edge)
+    fresh2, f2h, f2l, give = call(
+        domain_give,
+        (present, coef, *halves[:2], work, total),
+        new_outs + (message,),
+        "domain_give",
+        flops=unit,
+    )
     from_core = to_core(give)
     result, own = call(
         functools.partial(domain_last, total_blocks),
-        (domain_blocks, coef, ch, cl),
+        (domain_blocks, fresh1, f1h, f1l, fresh2, f2h, f2l),
         (jax.ShapeDtypeStruct(coefficients.shape, f32), vmem((6, HALF, NB))),
         "domain_last",
+        scratch=(vmem((window, SB)),) + (vmem((SB, 4 * NB), bf16),) * 2,
         smem=(0,),
-        flops=unit,
     )
     (rows,) = call(
         owner_kernel,

time: 97.6 us -> 91.5 us (0.938)
  waiting for transfers between devices: 28.6 us -> 25.5 us
  starting transfers between devices: 32.9 us -> 31.1 us
    ppermute x7 -> x8, waiting for transfers between devices: 25.6 us -> 12.9 us  [to_edge(): return lax.ppermute(value, 'grid', route)]
    ppermute x8, waiting for transfers between devices: 2.57 us -> 11.2 us  [to_orb(): return lax.ppermute(value, 'orb', [(0, 1), (1, 0)])]
    ppermute x9, starting transfers between devices: 3.24 us -> 1.07 us  [to_core(): return lax.ppermute(value, 'grid', [(i, i ^ 1) for i in range(count)])]
    ppermute x8, starting transfers between devices: 9.58 us -> 10.9 us  [to_orb(): return lax.ppermute(value, 'orb', [(0, 1), (1, 0)])]
    pallas_call x27 -> x30, Pallas kernels: 29.3 us -> 28 us  [call(): pl.pallas_call(kernel, out_shape=list(outs), in_specs=specs, out_specs=[p...]
    ppermute x9, waiting for transfers between devices: 0.36 us -> 1.46 us  [to_core(): return lax.ppermute(value, 'grid', [(i, i ^ 1) for i in range(count)])]
    ppermute x7 -> x8, starting transfers between devices: 20.1 us -> 19 us  [to_edge(): return lax.ppermute(value, 'grid', route)]
  transfers between devices with their start and end apart: 24 -> 25, of which waited for: 10 -> 12; matrix products, arithmetic and copies ran while one was open for 1% -> 1% of each run, Pallas kernels for 21% -> 26%
where the time goes in v1:
time: 91.5 us; the launch traced here: 91.3 us
  Pallas kernels  33.1 us (36%)
  starting transfers between devices  31.1 us (34%)
  waiting for transfers between devices  25.5 us (28%)
  between operations  0.99 us (1%)
    pallas_call x30, Pallas kernels, call(): pl.pallas_call(kernel, out_shape=list(outs), in_specs=specs, out_specs=[p...  28 us
    ppermute x8, starting transfers between devices, to_edge(): return lax.ppermute(value, 'grid', route)  19 us
    ppermute x8, waiting for transfers between devices, to_edge(): return lax.ppermute(value, 'grid', route)  12.9 us
    ppermute x8, waiting for transfers between devices, to_orb(): return lax.ppermute(value, 'orb', [(0, 1), (1, 0)])  11.2 us
    ppermute x8, starting transfers between devices, to_orb(): return lax.ppermute(value, 'orb', [(0, 1), (1, 0)])  10.9 us
    pallas_call x1, Pallas kernels, sort_basis(): pl.pallas_call(functools.partial(sort_kernel, total_blocks), out_shape=ha...  3.28 us
    pallas_call x1, Pallas kernels, cut(): pl.pallas_call(cut_kernel, out_shape=[vmem(own.shape), vmem((EARLY, HALF,...  1.83 us
  transfers between devices with their start and end apart: 25, of which 12 were waited for; matrix products, arithmetic and copies ran while one was open for 1% of the time, Pallas kernels for 26%

profile of v1, /device:TPU:0, one launch (start us, length us, event | category | flops | bytes accessed | tf_op | source)
XLA Modules:
  0.0 91.3 jit_solution(11350805204781037326)
XLA Ops:
  0.6 0.5 collective-permute-start
  1.1 2.6 %collective-permute-start.3 = (f32[6,64,128]{2,1,0:T(8,128)}, f32[6,64,128]{2,1,0:T(8,128)S(1)}, u32[]{:S(2)}, u32[]{:S(2)}) collective-permute-start(f32[6,64,128]{2,1,0:T(8,128)} %bitcast.7), channel_id=1, source_target_pairs={{0,1},{1,0},{2,3},{3,2},{4,5},{5,4},{6,7},{7,6},{8,9},{9,8},{10,11... | collective-permute-start | bytes 589832 | tf_op jit(solution)/shard_map/ppermute | solution.py:730
  3.7 4.3 %collective-permute-start.1 = (f32[6,64,128]{2,1,0:T(8,128)}, f32[6,64,128]{2,1,0:T(8,128)S(1)}, u32[]{:S(2)}, u32[]{:S(2)}) collective-permute-start(f32[6,64,128]{2,1,0:T(8,128)} %bitcast.8), channel_id=1, source_target_pairs={{0,30},{2,4},{4,2},{6,8},{8,6},{10,12},{12,10},{14,16},{16,14},{18... | collective-permute-start | bytes 589832 | tf_op jit(solution)/shard_map/ppermute | solution.py:726
  8.0 1.8 %cut.1 = (f32[6,64,128]{2,1,0:T(8,128)S(1)}, f32[9,64,128]{2,1,0:T(8,128)S(1)}, f32[7,64,128]{2,1,0:T(8,128)S(1)}, f32[8,128]{1,0:T(8,128)S(1)}) custom-call(s32[2,4]{1,0:T(2,128)} %own_lists.3, f32[6,64,128]{2,1,0:T(8,128)} %bitcast.9, f32[16,64,128]{2,1,0:T(8,128)} %bitcast.4, f32[6,64,128]{2,1,0:T(8,128)S(1)} %collective-permute-done.other), custom_call_target="tpu_custom_call" | custom-call | tf_op jit(solution)/shard_map/cut/pallas_call | solution.py:132
  9.9 0.6 collective-permute-start.5
  10.5 3.3 %sort_basis.1 = (bf16[768,1280]{1,0:T(8,128)(2,1)S(1)}, bf16[768,1280]{1,0:T(8,128)(2,1)S(1)}, bf16[1280,768]{1,0:T(8,128)(2,1)S(1)}, bf16[1280,768]{1,0:T(8,128)(2,1)S(1)}, f32[8,128]{1,0:T(8,128)S(1)}) custom-call(s32[1,6]{1,0:T(1,128)} %blocks.1, f32[1,1280,768]{2,1,0:T(8,128)} %basis.1), custom_call_target="tpu_custom_call" | custom-call | flops 3019898880 | tf_op jit(solution)/shard_map/sort_basis/pallas_call | solution.py:153
  14.0 1.6 %collective-permute-start.2 = (f32[328,128]{1,0:T(8,128)S(1)}, f32[328,128]{1,0:T(8,128)S(1)}, u32[]{:S(2)}, u32[]{:S(2)}) collective-permute-start(f32[328,128]{1,0:T(8,128)S(1)} %far_message.1), channel_id=1, source_target_pairs={{0,1},{1,0},{2,3},{3,2},{4,5},{5,4},{6,7},{7,6},{8,9},{9,8},{10,11... | collective-permute-start | bytes 503816 | tf_op jit(solution)/shard_map/ppermute | solution.py:730
  15.5 1.2 %collective-permute-done.5.early = f32[9,64,128]{2,1,0:T(8,128)S(1)} collective-permute-done((f32[9,64,128]{2,1,0:T(8,128)S(1)}, f32[9,64,128]{2,1,0:T(8,128)S(1)}, u32[]{:S(2)}, u32[]{:S(2)}) %collective-permute-start.5) | collective-permute-done | bytes 294944 | tf_op jit(solution)/shard_map/ppermute | solution.py:730
  16.7 2.8 %rho_first.1.rho = f32[1,1280]{1,0:T(1,128)S(1)} custom-call(bf16[768,1280]{1,0:T(8,128)(2,1)S(1)} %get-tuple-element.95.th, bf16[768,1280]{1,0:T(8,128)(2,1)S(1)} %get-tuple-element.96.tl, f32[6,64,128]{2,1,0:T(8,128)S(1)} %get-tuple-element.102.own, f32[6,64,128]{2,1,0:T(8,128)S(1)} %hold.1.own_far, f32[6,64,128]{2,1,0:T(8,128)S(1)} %collective-permute-done.1.edge, ...), custom_call_target="tpu_custom_call" | custom-call | flops 2516582400 | tf_op jit(solution)/shard_map/rho_first/pallas_call | solution.py:81
  19.5 1.2 %collective-permute-done.2.edge_far = f32[328,128]{1,0:T(8,128)S(1)} collective-permute-done((f32[328,128]{1,0:T(8,128)S(1)}, f32[328,128]{1,0:T(8,128)S(1)}, u32[]{:S(2)}, u32[]{:S(2)}) %collective-permute-start.2) | collective-permute-done | bytes 167968 | tf_op jit(solution)/shard_map/ppermute | solution.py:730
  20.7 1.6 %fock_other.2 = (f32[1,1280]{1,0:T(1,128)S(1)}, f32[328,128]{1,0:T(8,128)S(1)}, f32[64,128]{1,0:T(8,128)S(1)}) custom-call(f32[1,1280]{1,0:T(1,128)S(1)} %copy-done.7, f32[1,1280]{1,0:T(1,128)S(1)} %copy-done.8, bf16[768,1280]{1,0:T(8,128)(2,1)S(1)} %get-tuple-element.95.th, bf16[768,1280]{1,0:T(8,128)(2,1)S(1)} %get-tuple-element.96.tl, ...), custom_call_target="tpu_custom_call" | custom-call | flops 1509949440 | tf_op jit(solution)/shard_map/fock_other/pallas_call | solution.py:81
  22.4 1.6 %collective-permute-start.8 = (f32[7,64,128]{2,1,0:T(8,128)S(1)}, f32[7,64,128]{2,1,0:T(8,128)S(1)}, u32[]{:S(2)}, u32[]{:S(2)}) collective-permute-start(f32[7,64,128]{2,1,0:T(8,128)S(1)} %get-tuple-element.112), channel_id=1, source_target_pairs={{0,1},{1,0},{2,3},{3,2},{4,5},{5,4},{6,7},{7,6},{8,9},{9,8},{10,11... | collective-permute-start | bytes 688136 | tf_op jit(solution)/shard_map/ppermute | solution.py:730
  24.0 1.7 %fock_side.2 = (f32[336,128]{1,0:T(8,128)S(1)}, f32[320,128]{1,0:T(8,128)S(1)}) custom-call(bf16[768,1280]{1,0:T(8,128)(2,1)S(1)} %get-tuple-element.95.th, bf16[768,1280]{1,0:T(8,128)(2,1)S(1)} %get-tuple-element.96.tl, bf16[1280,768]{1,0:T(8,128)(2,1)S(1)} %get-tuple-element.97.nh, bf16[1280,768]{1,0:T(8,128)(2,1)S(1)} %get-tuple-element.98.nl, ...), custom_call_target="tpu_custom_call" | custom-call | flops 1509949440 | tf_op jit(solution)/shard_map/fock_side/pallas_call | solution.py:81
  25.7 0.6 collective-permute-start.10
  26.3 3.0 %collective-permute-start.7 = (f32[320,128]{1,0:T(8,128)S(1)}, f32[320,128]{1,0:T(8,128)S(1)}, u32[]{:S(2)}, u32[]{:S(2)}) collective-permute-start(f32[320,128]{1,0:T(8,128)S(1)} %get-tuple-element.111.left), channel_id=1, source_target_pairs={{0,30},{2,4},{4,2},{6,8},{8,6},{10,12},{12,10},{14,16},{16,14},{18... | collective-permute-start | bytes 491528 | tf_op jit(solution)/shard_map/ppermute | solution.py:726
  29.3 4.5 %collective-permute-done.7.right = f32[320,128]{1,0:T(8,128)S(1)} collective-permute-done((f32[320,128]{1,0:T(8,128)S(1)}, f32[320,128]{1,0:T(8,128)S(1)}, u32[]{:S(2)}, u32[]{:S(2)}) %collective-permute-start.7) | collective-permute-done | bytes 163872 | tf_op jit(solution)/shard_map/ppermute | solution.py:726
  33.8 1.6 %collective-permute-start.9 = (f32[320,128]{1,0:T(8,128)S(1)}, f32[320,128]{1,0:T(8,128)S(1)}, u32[]{:S(2)}, u32[]{:S(2)}) collective-permute-start(f32[320,128]{1,0:T(8,128)S(1)} %add_b.2.side_b), channel_id=1, source_target_pairs={{0,1},{1,0},{2,3},{3,2},{4,5},{5,4},{6,7},{7,6},{8,9},{9,8},{10,11... | collective-permute-start | bytes 491528 | tf_op jit(solution)/shard_map/ppermute | solution.py:730
  35.4 2.7 %collective-permute-start.11 = (f32[336,128]{1,0:T(8,128)S(1)}, f32[336,128]{1,0:T(8,128)S(1)}, u32[]{:S(2)}, u32[]{:S(2)}) collective-permute-start(f32[336,128]{1,0:T(8,128)S(1)} %get-tuple-element.128.side_a), channel_id=1, source_target_pairs={{0,30},{2,4},{4,2},{6,8},{8,6},{10,12},{12,10},{14,16},{16,14},{18... | collective-permute-start | bytes 516104 | tf_op jit(solution)/shard_map/ppermute | solution.py:726
  38.2 0.6 convert_element_type.6.other_lists
  38.8 1.8 %spread.1 = (f32[768,512]{1,0:T(8,128)S(1)}, bf16[768,512]{1,0:T(8,128)(2,1)S(1)}, bf16[768,512]{1,0:T(8,128)(2,1)S(1)}, bf16[512,768]{1,0:T(8,128)(2,1)S(1)}, b...) custom-call(s32[2,4]{1,0:T(2,128)} %own_lists.3, s32[2,4]{1,0:T(2,128)} %convert_element_type.6.other_lists, ...), custom_call_target="tpu_custom_call" | custom-call | flops 1509949440 | tf_op jit(solution)/shard_map/spread/pallas_call | solution.py:81
  40.6 2.4 %collective-permute-done.11.arrived_a = f32[336,128]{1,0:T(8,128)S(1)} collective-permute-done((f32[336,128]{1,0:T(8,128)S(1)}, f32[336,128]{1,0:T(8,128)S(1)}, u32[]{:S(2)}, u32[]{:S(2)}) %collective-permute-start.11) | collective-permute-done | bytes 172064 | tf_op jit(solution)/shard_map/ppermute | solution.py:726
  43.1 1.4 %domain_side.2 = (f32[512,512]{1,0:T(8,128)S(1)}, f32[4,128,128]{2,1,0:T(8,128)S(1)}) custom-call(f32[336,128]{1,0:T(8,128)S(1)} %get-tuple-element.131.side_a, f32[384,128]{1,0:T(8,128)S(1)} %get-tuple-element.132.side_b, bf16[768,512]{1,0:T(8,128)(2,1)S(1)} %get-tuple-element.123.ch, bf16[768,512]{1,0:T(8,128)(2,1)S(1)} %get-tuple-element.124.cl, ...), custom_call_target="tpu_custom_call" | custom-call | flops 503316480 | tf_op jit(solution)/shard_map/domain_side/pallas_call | solution.py:81
  44.6 2.3 %domain_far.1 = (f32[384,512]{1,0:T(8,128)S(1)}, bf16[384,512]{1,0:T(8,128)(2,1)S(1)}, bf16[384,512]{1,0:T(8,128)(2,1)S(1)}, f32[768,512]{1,0:T(8,128)S(1)}, f32...) custom-call(f32[24,128]{1,0:T(8,128)S(1)} %get-tuple-element.121.present, f32[768,512]{1,0:T(8,128)S(1)} %get-tuple-element.122.coef, ...), custom_call_target="tpu_custom_call" | custom-call | flops 1006632960 | tf_op jit(solution)/shard_map/domain_far/pallas_call | solution.py:81
  46.9 2.7 %collective-permute-start.14 = (f32[392,128]{1,0:T(8,128)S(1)}, f32[392,128]{1,0:T(8,128)S(1)}, u32[]{:S(2)}, u32[]{:S(2)}) collective-permute-start(f32[392,128]{1,0:T(8,128)S(1)} %get-tuple-element.146.mine), channel_id=1, source_target_pairs={{0,30},{2,4},{4,2},{6,8},{8,6},{10,12},{12,10},{14,16},{16,14},{18... | collective-permute-start | bytes 602120 | tf_op jit(solution)/shard_map/ppermute | solution.py:726
  49.6 1.3 %domain_other.1 = (f32[384,512]{1,0:T(8,128)S(1)}, bf16[384,512]{1,0:T(8,128)(2,1)S(1)}, bf16[384,512]{1,0:T(8,128)(2,1)S(1)}, f32[328,128]{1,0:T(8,128)S(1)}, f32[64,128]{1,0:T(8,128)S(1)}) custom-call(f32[24,128]{1,0:T(8,128)S(1)} %get-tuple-element.121.present, f32[768,512]{1,0:T(8,128)S(1)} %get-tuple-element.122.coef, ...), custom_call_target="tpu_custom_call" | custom-call | flops 503316480 | tf_op jit(solution)/shard_map/domain_other/pallas_call | solution.py:81
  51.4 1.0 %collective-permute-done.13.arrived = f32[328,128]{1,0:T(8,128)S(1)} collective-permute-done((f32[328,128]{1,0:T(8,128)S(1)}, f32[328,128]{1,0:T(8,128)S(1)}, u32[]{:S(2)}, u32[]{:S(2)}) %collective-permute-start.13) | collective-permute-done | bytes 167968 | tf_op jit(solution)/shard_map/ppermute | solution.py:720
  52.4 1.8 %collective-permute-start.16 = (f32[336,128]{1,0:T(8,128)S(1)}, f32[336,128]{1,0:T(8,128)S(1)}, u32[]{:S(2)}, u32[]{:S(2)}) collective-permute-start(f32[336,128]{1,0:T(8,128)S(1)} %get-tuple-element.144.near), channel_id=1, source_target_pairs={{0,30},{2,4},{4,2},{6,8},{8,6},{10,12},{12,10},{14,16},{16,14},{18... | collective-permute-start | bytes 516104 | tf_op jit(solution)/shard_map/ppermute | solution.py:726
  54.3 0.6 collective-permute-done.14.arrived
  55.0 0.9 rho_near.1.before
  56.4 0.9 rho_other.1.rho
  57.3 2.8 %collective-permute-done.16.arrived = f32[336,128]{1,0:T(8,128)S(1)} collective-permute-done((f32[336,128]{1,0:T(8,128)S(1)}, f32[336,128]{1,0:T(8,128)S(1)}, u32[]{:S(2)}, u32[]{:S(2)}) %collective-permute-start.16) | collective-permute-done | bytes 172064 | tf_op jit(solution)/shard_map/ppermute | solution.py:726
  60.0 2.1 %fock_other.3 = (f32[1,1280]{1,0:T(1,128)S(1)}, f32[328,128]{1,0:T(8,128)S(1)}, f32[64,128]{1,0:T(8,128)S(1)}) custom-call(f32[1,1280]{1,0:T(1,128)S(1)} %copy-done.7, f32[1,1280]{1,0:T(1,128)S(1)} %copy-done.8, bf16[768,1280]{1,0:T(8,128)(2,1)S(1)} %get-tuple-element.95.th, bf16[768,1280]{1,0:T(8,128)(2,1)S(1)} %copy-done.1, ...), custom_call_target="tpu_custom_call" | custom-call | flops 1509949440 | tf_op jit(solution)/shard_map/fock_other/pallas_call | solution.py:81
  62.2 1.6 %fock_side.3 = (f32[336,128]{1,0:T(8,128)S(1)}, f32[320,128]{1,0:T(8,128)S(1)}) custom-call(bf16[768,1280]{1,0:T(8,128)(2,1)S(1)} %get-tuple-element.95.th, bf16[768,1280]{1,0:T(8,128)(2,1)S(1)} %copy-done.1, bf16[1280,768]{1,0:T(8,128)(2,1)S(1)} %copy-done.3, bf16[1280,768]{1,0:T(8,128)(2,1)S(1)} %copy-done.5, f32[1,1280]{1,0:T(1,128)S(1)} %get-tuple-element.149.scale), custom_call_target="tpu_custom_call" | custom-call | flops 1509949440 | tf_op jit(solution)/shard_map/fock_side/pallas_call | solution.py:81
  63.9 1.0 %collective-permute-start.19 = (f32[400,128]{1,0:T(8,128)S(1)}, f32[400,128]{1,0:T(8,128)S(1)}, u32[]{:S(2)}, u32[]{:S(2)}) collective-permute-start(f32[400,128]{1,0:T(8,128)S(1)} %get-tuple-element.167.side_a), channel_id=1, source_target_pairs={{0,1},{1,0},{2,3},{3,2},{4,5},{5,4},{6,7},{7,6},{8,9},{9,8},{10,11... | collective-permute-start | bytes 614408 | tf_op jit(solution)/shard_map/ppermute | solution.py:730
  64.9 1.9 %collective-permute-start.18 = (f32[320,128]{1,0:T(8,128)S(1)}, f32[320,128]{1,0:T(8,128)S(1)}, u32[]{:S(2)}, u32[]{:S(2)}) collective-permute-start(f32[320,128]{1,0:T(8,128)S(1)} %get-tuple-element.154.left), channel_id=1, source_target_pairs={{0,30},{2,4},{4,2},{6,8},{8,6},{10,12},{12,10},{14,16},{16,14},{18... | collective-permute-start | bytes 491528 | tf_op jit(solution)/shard_map/ppermute | solution.py:726
  66.8 4.7 %collective-permute-done.19.arrived = f32[400,128]{1,0:T(8,128)S(1)} collective-permute-done((f32[400,128]{1,0:T(8,128)S(1)}, f32[400,128]{1,0:T(8,128)S(1)}, u32[]{:S(2)}, u32[]{:S(2)}) %collective-permute-start.19) | collective-permute-done | bytes 204832 | tf_op jit(solution)/shard_map/ppermute | solution.py:730
  71.5 0.5 collective-permute-start.20
  72.0 0.8 gather.1
  72.9 1.5 %collective-permute-start.21 = (f32[320,128]{1,0:T(8,128)S(1)}, f32[320,128]{1,0:T(8,128)S(1)}, u32[]{:S(2)}, u32[]{:S(2)}) collective-permute-start(f32[320,128]{1,0:T(8,128)S(1)} %add_b.3.side_b), channel_id=1, source_target_pairs={{0,1},{1,0},{2,3},{3,2},{4,5},{5,4},{6,7},{7,6},{8,9},{9,8},{10,11... | collective-permute-start | bytes 491528 | tf_op jit(solution)/shard_map/ppermute | solution.py:730
  74.3 4.1 %collective-permute-done.21.arrived_b = f32[320,128]{1,0:T(8,128)S(1)} collective-permute-done((f32[320,128]{1,0:T(8,128)S(1)}, f32[320,128]{1,0:T(8,128)S(1)}, u32[]{:S(2)}, u32[]{:S(2)}) %collective-permute-start.21) | collective-permute-done | bytes 163872 | tf_op jit(solution)/shard_map/ppermute | solution.py:730
  78.4 0.7 collective-permute-done.20.arrived_a
  79.2 1.4 %domain_side.3 = (f32[512,512]{1,0:T(8,128)S(1)}, f32[4,128,128]{2,1,0:T(8,128)S(1)}) custom-call(f32[336,128]{1,0:T(8,128)S(1)} %get-tuple-element.171.side_a, f32[384,128]{1,0:T(8,128)S(1)} %get-tuple-element.172.side_b, bf16[768,512]{1,0:T(8,128)(2,1)S(1)} %get-tuple-element.163.ch, bf16[768,512]{1,0:T(8,128)(2,1)S(1)} %get-tuple-element.164.cl, ...), custom_call_target="tpu_custom_call" | custom-call | flops 503316480 | tf_op jit(solution)/shard_map/domain_side/pallas_call | solution.py:81
  80.6 2.4 %domain_edge.1 = (f32[384,512]{1,0:T(8,128)S(1)}, bf16[384,512]{1,0:T(8,128)(2,1)S(1)}, bf16[384,512]{1,0:T(8,128)(2,1)S(1)}, f32[768,512]{1,0:T(8,128)S(1)}, f3...) custom-call(f32[24,128]{1,0:T(8,128)S(1)} %get-tuple-element.121.present, f32[768,512]{1,0:T(8,128)S(1)} %get-tuple-element.162.coef, ...), custom_call_target="tpu_custom_call" | custom-call | flops 1006632960 | tf_op jit(solution)/shard_map/domain_edge/pallas_call | solution.py:81
  83.1 2.1 %collective-permute-start.24 = (f32[336,128]{1,0:T(8,128)S(1)}, f32[336,128]{1,0:T(8,128)S(1)}, u32[]{:S(2)}, u32[]{:S(2)}) collective-permute-start(f32[336,128]{1,0:T(8,128)S(1)} %get-tuple-element.186), channel_id=1, source_target_pairs={{0,30},{2,4},{4,2},{6,8},{8,6},{10,12},{12,10},{14,16},{16,14},{18... | collective-permute-start | bytes 516104 | tf_op jit(solution)/shard_map/ppermute | solution.py:726
  85.1 1.2 %domain_give.1 = (f32[384,512]{1,0:T(8,128)S(1)}, bf16[384,512]{1,0:T(8,128)(2,1)S(1)}, bf16[384,512]{1,0:T(8,128)(2,1)S(1)}, f32[5,64,128]{2,1,0:T(8,128)S(1)}) custom-call(f32[24,128]{1,0:T(8,128)S(1)} %get-tuple-element.121.present, f32[768,512]{1,0:T(8,128)S(1)} %get-tuple-element.162.coef, bf16[768,512]{1,0:T(8,128)(2,1)S(1)} %get-tuple-element.163.ch, ...), custom_call_target="tpu_custom_call" | custom-call | flops 503316480 | tf_op jit(solution)/shard_map/domain_give/pallas_call | solution.py:81
  86.4 2.3 %domain_last.1 = (f32[2,4,128,128]{3,2,1,0:T(8,128)}, f32[6,64,128]{2,1,0:T(8,128)S(1)}) custom-call(s32[2,4]{1,0:T(2,128)} %own_lists.3, f32[384,512]{1,0:T(8,128)S(1)} %get-tuple-element.176.fresh1, bf16[384,512]{1,0:T(8,128)(2,1)S(1)} %get-tuple-element.177.f1h, bf16[384,512]{1,0:T(8,128)(2,1)S(1)} %get-tuple-element.178.f1l, ...), custom_call_target="tpu_custom_call" | custom-call | tf_op jit(solution)/shard_map/domain_last/pallas_call | solution.py:81
  88.7 1.9 %collective-permute-done.24.from_edge = f32[336,128]{1,0:T(8,128)S(1)} collective-permute-done((f32[336,128]{1,0:T(8,128)S(1)}, f32[336,128]{1,0:T(8,128)S(1)}, u32[]{:S(2)}, u32[]{:S(2)}) %collective-permute-start.24) | collective-permute-done | bytes 172064 | tf_op jit(solution)/shard_map/ppermute | solution.py:726
  90.6 0.7 owner_rows.1
  (58 shorter events, 1.9 us)
Async XLA Ops:
  0.6 7.4 %collective-permute-start = (f32[6,64,128]{2,1,0:T(8,128)}, f32[6,64,128]{2,1,0:T(8,128)S(1)}, u32[]{:S(2)}, u32[]{:S(2)}) collective-permute-start(f32[6,64,128]{2,1,0:T(8,128)} %bitcast.6), channel_id=1, source_target_pairs={{0,2},{2,0},{4,6},{6,4},{8,10},{10,8},{12,14},{14,12},{16,18},{18,... | collective-permute-start | bytes 589832 | tf_op jit(solution)/shard_map/ppermute | solution.py:720
  1.1 12.7 %collective-permute-start.3 = (f32[6,64,128]{2,1,0:T(8,128)}, f32[6,64,128]{2,1,0:T(8,128)S(1)}, u32[]{:S(2)}, u32[]{:S(2)}) collective-permute-start(f32[6,64,128]{2,1,0:T(8,128)} %bitcast.7), channel_id=1, source_target_pairs={{0,1},{1,0},{2,3},{3,2},{4,5},{5,4},{6,7},{7,6},{8,9},{9,8},{10,11... | collective-permute-start | bytes 589832 | tf_op jit(solution)/shard_map/ppermute | solution.py:730
  3.7 10.2 %collective-permute-start.1 = (f32[6,64,128]{2,1,0:T(8,128)}, f32[6,64,128]{2,1,0:T(8,128)S(1)}, u32[]{:S(2)}, u32[]{:S(2)}) collective-permute-start(f32[6,64,128]{2,1,0:T(8,128)} %bitcast.8), channel_id=1, source_target_pairs={{0,30},{2,4},{4,2},{6,8},{8,6},{10,12},{12,10},{14,16},{16,14},{18... | collective-permute-start | bytes 589832 | tf_op jit(solution)/shard_map/ppermute | solution.py:726
  9.9 6.8 %collective-permute-start.5 = (f32[9,64,128]{2,1,0:T(8,128)S(1)}, f32[9,64,128]{2,1,0:T(8,128)S(1)}, u32[]{:S(2)}, u32[]{:S(2)}) collective-permute-start(f32[9,64,128]{2,1,0:T(8,128)S(1)} %get-tuple-element.103), channel_id=1, source_target_pairs={{0,1},{1,0},{2,3},{3,2},{4,5},{5,4},{6,7},{7,6},{8,9},{9,8},{10,11... | collective-permute-start | bytes 884744 | tf_op jit(solution)/shard_map/ppermute | solution.py:730
  13.8 10.2 %copy-start = (bf16[768,1280]{1,0:T(8,128)(2,1)}, bf16[768,1280]{1,0:T(8,128)(2,1)S(1)}, u32[]{:S(2)}) copy-start(bf16[768,1280]{1,0:T(8,128)(2,1)S(1)} %get-tuple-element.96.tl) | copy-start | bytes 5898244
  13.8 10.2 %copy-start.2 = (bf16[1280,768]{1,0:T(8,128)(2,1)}, bf16[1280,768]{1,0:T(8,128)(2,1)S(1)}, u32[]{:S(2)}) copy-start(bf16[1280,768]{1,0:T(8,128)(2,1)S(1)} %get-tuple-element.97.nh) | copy-start | bytes 5898244
  13.8 10.2 %copy-start.4 = (bf16[1280,768]{1,0:T(8,128)(2,1)}, bf16[1280,768]{1,0:T(8,128)(2,1)S(1)}, u32[]{:S(2)}) copy-start(bf16[1280,768]{1,0:T(8,128)(2,1)S(1)} %get-tuple-element.98.nl) | copy-start | bytes 5898244
  13.8 1.7 %collective-permute-start.4 = (f32[6,64,128]{2,1,0:T(8,128)S(1)}, f32[6,64,128]{2,1,0:T(8,128)S(1)}, u32[]{:S(2)}, u32[]{:S(2)}) collective-permute-start(f32[6,64,128]{2,1,0:T(8,128)S(1)} %hold.1.own_far), channel_id=1, source_target_pairs={{0,2},{2,0},{4,6},{6,4},{8,10},{10,8},{12,14},{14,12},{16,18},{18,... | collective-permute-start | bytes 589832 | tf_op jit(solution)/shard_map/ppermute | solution.py:720
  14.0 6.7 %collective-permute-start.2 = (f32[328,128]{1,0:T(8,128)S(1)}, f32[328,128]{1,0:T(8,128)S(1)}, u32[]{:S(2)}, u32[]{:S(2)}) collective-permute-start(f32[328,128]{1,0:T(8,128)S(1)} %far_message.1), channel_id=1, source_target_pairs={{0,1},{1,0},{2,3},{3,2},{4,5},{5,4},{6,7},{7,6},{8,9},{9,8},{10,11... | collective-permute-start | bytes 503816 | tf_op jit(solution)/shard_map/ppermute | solution.py:730
  16.7 2.8 %copy-start.9 = (f32[9,64,128]{2,1,0:T(8,128)}, f32[9,64,128]{2,1,0:T(8,128)S(1)}, u32[]{:S(2)}) copy-start(f32[9,64,128]{2,1,0:T(8,128)S(1)} %collective-permute-done.5.early) | copy-start | bytes 884740
  16.7 4.0 %copy-start.7 = (f32[1,1280]{1,0:T(1,128)S(1)}, f32[1,1280]{1,0:T(1,128)}, u32[]{:S(2)}) copy-start(f32[1,1280]{1,0:T(1,128)} %weights.3) | copy-start | bytes 15364
  16.7 4.0 %copy-start.8 = (f32[1,1280]{1,0:T(1,128)S(1)}, f32[1,1280]{1,0:T(1,128)}, u32[]{:S(2)}) copy-start(f32[1,1280]{1,0:T(1,128)} %external.3) | copy-start | bytes 15364
  22.3 3.3 %collective-permute-start.6 = (f32[328,128]{1,0:T(8,128)S(1)}, f32[328,128]{1,0:T(8,128)S(1)}, u32[]{:S(2)}, u32[]{:S(2)}) collective-permute-start(f32[328,128]{1,0:T(8,128)S(1)} %get-tuple-element.110), channel_id=1, source_target_pairs={{0,2},{2,0},{4,6},{6,4},{8,10},{10,8},{12,14},{14,12},{16,18},{18,... | collective-permute-start | bytes 503816 | tf_op jit(solution)/shard_map/ppermute | solution.py:720
  22.4 11.4 %collective-permute-start.8 = (f32[7,64,128]{2,1,0:T(8,128)S(1)}, f32[7,64,128]{2,1,0:T(8,128)S(1)}, u32[]{:S(2)}, u32[]{:S(2)}) collective-permute-start(f32[7,64,128]{2,1,0:T(8,128)S(1)} %get-tuple-element.112), channel_id=1, source_target_pairs={{0,1},{1,0},{2,3},{3,2},{4,5},{5,4},{6,7},{7,6},{8,9},{9,8},{10,11... | collective-permute-start | bytes 688136 | tf_op jit(solution)/shard_map/ppermute | solution.py:730
  24.0 14.8 %copy-start.6 = (f32[2,4,128,128]{3,2,1,0:T(8,128)S(1)}, f32[2,4,128,128]{3,2,1,0:T(8,128)}, u32[]{:S(2)}) copy-start(f32[2,4,128,128]{3,2,1,0:T(8,128)} %param.13) | copy-start | bytes 1572868
  25.7 9.6 %collective-permute-start.10 = (f32[400,128]{1,0:T(8,128)S(1)}, f32[400,128]{1,0:T(8,128)S(1)}, u32[]{:S(2)}, u32[]{:S(2)}) collective-permute-start(f32[400,128]{1,0:T(8,128)S(1)} %get-tuple-element.127.side_a), channel_id=1, source_target_pairs={{0,1},{1,0},{2,3},{3,2},{4,5},{5,4},{6,7},{7,6},{8,9},{9,8},{10,11... | collective-permute-start | bytes 614408 | tf_op jit(solution)/shard_map/ppermute | solution.py:730
  26.3 7.4 %collective-permute-start.7 = (f32[320,128]{1,0:T(8,128)S(1)}, f32[320,128]{1,0:T(8,128)S(1)}, u32[]{:S(2)}, u32[]{:S(2)}) collective-permute-start(f32[320,128]{1,0:T(8,128)S(1)} %get-tuple-element.111.left), channel_id=1, source_target_pairs={{0,30},{2,4},{4,2},{6,8},{8,6},{10,12},{12,10},{14,16},{16,14},{18... | collective-permute-start | bytes 491528 | tf_op jit(solution)/shard_map/ppermute | solution.py:726
  33.8 5.0 %copy-start.10 = (f32[7,64,128]{2,1,0:T(8,128)}, f32[7,64,128]{2,1,0:T(8,128)S(1)}, u32[]{:S(2)}) copy-start(f32[7,64,128]{2,1,0:T(8,128)S(1)} %collective-permute-done.8.partner) | copy-start | bytes 688132
  33.8 6.8 %collective-permute-start.9 = (f32[320,128]{1,0:T(8,128)S(1)}, f32[320,128]{1,0:T(8,128)S(1)}, u32[]{:S(2)}, u32[]{:S(2)}) collective-permute-start(f32[320,128]{1,0:T(8,128)S(1)} %add_b.2.side_b), channel_id=1, source_target_pairs={{0,1},{1,0},{2,3},{3,2},{4,5},{5,4},{6,7},{7,6},{8,9},{9,8},{10,11... | collective-permute-start | bytes 491528 | tf_op jit(solution)/shard_map/ppermute | solution.py:730
  35.4 7.6 %collective-permute-start.11 = (f32[336,128]{1,0:T(8,128)S(1)}, f32[336,128]{1,0:T(8,128)S(1)}, u32[]{:S(2)}, u32[]{:S(2)}) collective-permute-start(f32[336,128]{1,0:T(8,128)S(1)} %get-tuple-element.128.side_a), channel_id=1, source_target_pairs={{0,30},{2,4},{4,2},{6,8},{8,6},{10,12},{12,10},{14,16},{16,14},{18... | collective-permute-start | bytes 516104 | tf_op jit(solution)/shard_map/ppermute | solution.py:726
  43.1 1.5 %collective-permute-start.12 = (f32[328,128]{1,0:T(8,128)S(1)}, f32[328,128]{1,0:T(8,128)S(1)}, u32[]{:S(2)}, u32[]{:S(2)}) collective-permute-start(f32[328,128]{1,0:T(8,128)S(1)} %get-tuple-element.135), channel_id=1, source_target_pairs={{0,2},{2,0},{4,6},{6,4},{8,10},{10,8},{12,14},{14,12},{16,18},{18,... | collective-permute-start | bytes 503816 | tf_op jit(solution)/shard_map/ppermute | solution.py:720
  46.9 8.0 %collective-permute-start.14 = (f32[392,128]{1,0:T(8,128)S(1)}, f32[392,128]{1,0:T(8,128)S(1)}, u32[]{:S(2)}, u32[]{:S(2)}) collective-permute-start(f32[392,128]{1,0:T(8,128)S(1)} %get-tuple-element.146.mine), channel_id=1, source_target_pairs={{0,30},{2,4},{4,2},{6,8},{8,6},{10,12},{12,10},{14,16},{16,14},{18... | collective-permute-start | bytes 602120 | tf_op jit(solution)/shard_map/ppermute | solution.py:726
  50.9 4.1 %copy-start.1 = (bf16[768,1280]{1,0:T(8,128)(2,1)S(1)}, bf16[768,1280]{1,0:T(8,128)(2,1)}, u32[]{:S(2)}) copy-start(bf16[768,1280]{1,0:T(8,128)(2,1)} %copy-done) | copy-start | bytes 5898244
  50.9 1.5 %collective-permute-start.13 = (f32[328,128]{1,0:T(8,128)S(1)}, f32[328,128]{1,0:T(8,128)S(1)}, u32[]{:S(2)}, u32[]{:S(2)}) collective-permute-start(f32[328,128]{1,0:T(8,128)S(1)} %get-tuple-element.143), channel_id=1, source_target_pairs={{0,2},{2,0},{4,6},{6,4},{8,10},{10,8},{12,14},{14,12},{16,18},{18,... | collective-permute-start | bytes 503816 | tf_op jit(solution)/shard_map/ppermute | solution.py:720
  52.4 7.6 %collective-permute-start.16 = (f32[336,128]{1,0:T(8,128)S(1)}, f32[336,128]{1,0:T(8,128)S(1)}, u32[]{:S(2)}, u32[]{:S(2)}) collective-permute-start(f32[336,128]{1,0:T(8,128)S(1)} %get-tuple-element.144.near), channel_id=1, source_target_pairs={{0,30},{2,4},{4,2},{6,8},{8,6},{10,12},{12,10},{14,16},{16,14},{18... | collective-permute-start | bytes 516104 | tf_op jit(solution)/shard_map/ppermute | solution.py:726
  54.9 1.5 %collective-permute-start.15 = (f32[328,128]{1,0:T(8,128)S(1)}, f32[328,128]{1,0:T(8,128)S(1)}, u32[]{:S(2)}, u32[]{:S(2)}) collective-permute-start(f32[328,128]{1,0:T(8,128)S(1)} %get-tuple-element.147.near), channel_id=1, source_target_pairs={{0,2},{2,0},{4,6},{6,4},{8,10},{10,8},{12,14},{14,12},{16,18},{18,... | collective-permute-start | bytes 503816 | tf_op jit(solution)/shard_map/ppermute | solution.py:720
  55.9 4.1 %copy-start.3 = (bf16[1280,768]{1,0:T(8,128)(2,1)S(1)}, bf16[1280,768]{1,0:T(8,128)(2,1)}, u32[]{:S(2)}) copy-start(bf16[1280,768]{1,0:T(8,128)(2,1)} %copy-done.2) | copy-start | bytes 5898244
  55.9 4.1 %copy-start.5 = (bf16[1280,768]{1,0:T(8,128)(2,1)S(1)}, bf16[1280,768]{1,0:T(8,128)(2,1)}, u32[]{:S(2)}) copy-start(bf16[1280,768]{1,0:T(8,128)(2,1)} %copy-done.4) | copy-start | bytes 5898244
  62.1 1.7 %collective-permute-start.17 = (f32[328,128]{1,0:T(8,128)S(1)}, f32[328,128]{1,0:T(8,128)S(1)}, u32[]{:S(2)}, u32[]{:S(2)}) collective-permute-start(f32[328,128]{1,0:T(8,128)S(1)} %get-tuple-element.153), channel_id=1, source_target_pairs={{0,2},{2,0},{4,6},{6,4},{8,10},{10,8},{12,14},{14,12},{16,18},{18,... | collective-permute-start | bytes 503816 | tf_op jit(solution)/shard_map/ppermute | solution.py:720
  63.9 7.6 %collective-permute-start.19 = (f32[400,128]{1,0:T(8,128)S(1)}, f32[400,128]{1,0:T(8,128)S(1)}, u32[]{:S(2)}, u32[]{:S(2)}) collective-permute-start(f32[400,128]{1,0:T(8,128)S(1)} %get-tuple-element.167.side_a), channel_id=1, source_target_pairs={{0,1},{1,0},{2,3},{3,2},{4,5},{5,4},{6,7},{7,6},{8,9},{9,8},{10,11... | collective-permute-start | bytes 614408 | tf_op jit(solution)/shard_map/ppermute | solution.py:730
  64.9 7.9 %collective-permute-start.18 = (f32[320,128]{1,0:T(8,128)S(1)}, f32[320,128]{1,0:T(8,128)S(1)}, u32[]{:S(2)}, u32[]{:S(2)}) collective-permute-start(f32[320,128]{1,0:T(8,128)S(1)} %get-tuple-element.154.left), channel_id=1, source_target_pairs={{0,30},{2,4},{4,2},{6,8},{8,6},{10,12},{12,10},{14,16},{16,14},{18... | collective-permute-start | bytes 491528 | tf_op jit(solution)/shard_map/ppermute | solution.py:726
  71.5 7.6 %collective-permute-start.20 = (f32[336,128]{1,0:T(8,128)S(1)}, f32[336,128]{1,0:T(8,128)S(1)}, u32[]{:S(2)}, u32[]{:S(2)}) collective-permute-start(f32[336,128]{1,0:T(8,128)S(1)} %get-tuple-element.168.side_a), channel_id=1, source_target_pairs={{0,30},{2,4},{4,2},{6,8},{8,6},{10,12},{12,10},{14,16},{16,14},{18... | collective-permute-start | bytes 516104 | tf_op jit(solution)/shard_map/ppermute | solution.py:726
  72.9 5.5 %collective-permute-start.21 = (f32[320,128]{1,0:T(8,128)S(1)}, f32[320,128]{1,0:T(8,128)S(1)}, u32[]{:S(2)}, u32[]{:S(2)}) collective-permute-start(f32[320,128]{1,0:T(8,128)S(1)} %add_b.3.side_b), channel_id=1, source_target_pairs={{0,1},{1,0},{2,3},{3,2},{4,5},{5,4},{6,7},{7,6},{8,9},{9,8},{10,11... | collective-permute-start | bytes 491528 | tf_op jit(solution)/shard_map/ppermute | solution.py:730
  79.1 1.5 %collective-permute-start.22 = (f32[328,128]{1,0:T(8,128)S(1)}, f32[328,128]{1,0:T(8,128)S(1)}, u32[]{:S(2)}, u32[]{:S(2)}) collective-permute-start(f32[328,128]{1,0:T(8,128)S(1)} %get-tuple-element.175), channel_id=1, source_target_pairs={{0,2},{2,0},{4,6},{6,4},{8,10},{10,8},{12,14},{14,12},{16,18},{18,... | collective-permute-start | bytes 503816 | tf_op jit(solution)/shard_map/ppermute | solution.py:720
  83.1 7.6 %collective-permute-start.24 = (f32[336,128]{1,0:T(8,128)S(1)}, f32[336,128]{1,0:T(8,128)S(1)}, u32[]{:S(2)}, u32[]{:S(2)}) collective-permute-start(f32[336,128]{1,0:T(8,128)S(1)} %get-tuple-element.186), channel_id=1, source_target_pairs={{0,30},{2,4},{4,2},{6,8},{8,6},{10,12},{12,10},{14,16},{16,14},{18... | collective-permute-start | bytes 516104 | tf_op jit(solution)/shard_map/ppermute | solution.py:726
  86.3 2.4 %collective-permute-start.23 = (f32[5,64,128]{2,1,0:T(8,128)S(1)}, f32[5,64,128]{2,1,0:T(8,128)S(1)}, u32[]{:S(2)}, u32[]{:S(2)}) collective-permute-start(f32[5,64,128]{2,1,0:T(8,128)S(1)} %get-tuple-element.185), channel_id=1, source_target_pairs={{0,2},{2,0},{4,6},{6,4},{8,10},{10,8},{12,14},{14,12},{16,18},{18,... | collective-permute-start | bytes 491528 | tf_op jit(solution)/shard_map/ppermute | solution.py:720

commit v2 on v1

--- a/solution.py
+++ b/solution.py
@@ -25,7 +25,7 @@
 B_ROWS = 2 * NB + HALF
 PAIR = PACKED + NB
 GIVE_ROWS = PAIR + HALF
-EARLY = 9
+EARLY = 8
 STRIP = HALF + TILE
 KEEP_AT = 2 * NB + HALF
 
@@ -426,8 +426,9 @@
 
 def fock_side(th, tl, nh, nl, scale, side_a, side_b):
     at = core_of() * SB
-    low = fock_block(scaled_rows(th, tl, at, SB, scale), nh, nl, at, SB)
-    both_rows = fock_block(scaled_rows(th, tl, at + NB, 3 * NB, scale), nh, nl, at + SB, SB)
+    scaled = scaled_rows(th, tl, at, 4 * NB, scale)
+    low = fock_block(both(scaled, slice(0, SB)), nh, nl, at, SB)
+    both_rows = fock_block(both(scaled, slice(NB, 4 * NB)), nh, nl, at + SB, SB)
     put_side(low, both_rows[:NB, :NB], both_rows[NB:], side_a, side_b)
 
 
@@ -475,12 +476,19 @@
     coefficient_parts(coef[...], ch, cl, th, tl)
 
 
-def mixing(th, tl, at, count, gradient):
-    cols = pl.ds(pl.multiple_of(at, NB), count)
-    return [
-        dot3((th[d * NB : (d + 1) * NB, cols], tl[d * NB : (d + 1) * NB, cols]), both(gradient, slice(None), slice(d * NB, (d + 1) * NB)))
-        for d in range(4)
-    ]
+def mixing(th, tl, places, gradient):
+    rows = lax.broadcasted_iota(jnp.int32, (SB, SB), 0) < NB
+    same = rows == (lax.broadcasted_iota(jnp.int32, (SB, SB), 1) < NB)
+    result = []
+    for pair in range(2):
+        at = slice(pair * SB, (pair + 1) * SB)
+        left = []
+        for ref in (th, tl):
+            parts = [ref[at, pl.ds(pl.multiple_of(start, NB), count)] for start, count in places]
+            left.append(parts[0] if len(parts) == 1 else jnp.concatenate(parts, axis=1))
+        value = dot3(left, both(gradient, slice(None), at))
+        result.append(jnp.where(same, value, 0.0))
+    return result
 
 
 def domain_side(side_a, side_b, ch, cl, th, tl, gradient, mixed):
@@ -499,8 +507,8 @@
     gradient[:NB, :] = upper[:NB]
     gradient[NB : 3 * NB, :] = upper[NB:] + lower[: 2 * NB]
     gradient[3 * NB :, :] = lower[2 * NB :]
-    for d, value in enumerate(mixing(th, tl, at, 4 * NB, split(gradient[...]))):
-        mixed[d] = value
+    for pair, value in enumerate(mixing(th, tl, [(at, 4 * NB)], split(gradient[...]))):
+        mixed[pair] = value
 
 
 def domain_mixed(
@@ -525,17 +533,16 @@
     back = dot3(split(across), (ch[side_block, :], cl[side_block, :]))
     work[touching, :] += back
     work[side_block, :] += product[SB:]
-    first = mixing(th, tl, other_at, SB, split(work[other_rows, :]))
-    second = mixing(th, tl, (3 - core) * NB, NB, split(product[SB:]))
-    for d in range(4):
-        total[d] = mixed[d] + first[d] + second[d]
+    stacked = jnp.concatenate([work[other_rows, :], product[SB:]], axis=0)
+    added = mixing(th, tl, [(other_at, SB), ((3 - core) * NB, NB)], split(stacked))
+    for pair in range(2):
+        total[pair] = mixed[pair] + added[pair]
 
 
 def new_blocks(present, coef, ch, cl, work, total, places, fresh, fh, fl):
-    zero = jnp.zeros((NB, NB), f32)
     for d in range(0, 4, 2):
         cols = slice(d * NB, (d + 2) * NB)
-        square = split(join(total[d], zero, zero, total[d + 1]))
+        square = split(total[d // 2])
         for block, count, at in places:
             rows = pl.ds(aligned(block, NB), count * NB)
             moved = dot3((ch[rows, cols], cl[rows, cols]), square)
@@ -738,7 +745,7 @@
 CROSS = vmem((NB, NB))
 
 
-def total_over_all(made, before_last, before_sum):
+def total_over_all(made, after_near, before_sum):
     side_a, side_b, keep, arrived = made
     side_a, side_b = call(
         near_keep_kernel,
@@ -746,12 +753,12 @@
         (vmem((A_ROWS + HALF, NB)), B_OUT),
         "add_near",
     )
+    side_b = after_near(side_b)
     first_b = to_edge(side_b)
     first_a = to_orb(side_a)
     side_a, keep = call(add_keep_kernel, (side_a, first_a), (A_OUT, KEEP_OUT), "add_a")
     last_a = to_edge(side_a)
     (side_b,) = call(add_kernel, (side_b, first_b), (B_OUT,), "add_b")
-    side_b = before_last(side_b)
     last_b = before_sum(to_orb(side_b))
     side_a, side_b, near = call(
         total_kernel,
@@ -800,8 +807,7 @@
         "rho_first",
         flops=5 * unit,
     )
-    edge_far, rest, rho = lax.optimization_barrier((edge_far, rest, rho))
-    partner = to_orb(rest)
+    edge_far, rho = lax.optimization_barrier((edge_far, rho))
     other_lists = edge_far[5 * HALF, :8].reshape(2, 4).astype(jnp.int32)
 
     packed = None
@@ -825,46 +831,45 @@
         )
         ready = {}
 
-        def before_last(value):
+        def after_near(value):
             if iteration == 0:
-                value, ready["partner"] = lax.optimization_barrier((value, partner))
-                return value
-            gathered = call(
-                gather_kernel,
-                (fresh1, fresh2),
-                (coef_out, coef_half, coef_half, turned_half, turned_half),
-                "gather",
-                flops=unit,
-            )
-            value, *ready["gathered"] = lax.optimization_barrier((value, *gathered))
+                value, mine = lax.optimization_barrier((value, rest))
+                ready["partner"] = to_orb(mine)
             return value
 
         def before_sum(value):
-            if iteration > 0:
-                return value
-            spread = call(
-                functools.partial(spread_kernel, total_blocks),
-                (domain_blocks, other_lists, blocks, hbm(early), hbm(ready["partner"])),
-                (coef_out, coef_half, coef_half, turned_half, turned_half, vmem((24, NB))),
-                "spread",
-                smem=(0, 1),
-                plain=(2, 3, 4),
-                flops=3 * unit,
-            )
-            value, *ready["spread"] = lax.optimization_barrier((value, *spread))
+            if iteration == 0:
+                made = call(
+                    functools.partial(spread_kernel, total_blocks),
+                    (domain_blocks, other_lists, blocks, hbm(early), hbm(ready["partner"])),
+                    (coef_out, coef_half, coef_half, turned_half, turned_half, vmem((24, NB))),
+                    "spread",
+                    smem=(0, 1),
+                    plain=(2, 3, 4),
+                    flops=3 * unit,
+                )
+            else:
+                made = call(
+                    gather_kernel,
+                    (fresh1, fresh2),
+                    (coef_out, coef_half, coef_half, turned_half, turned_half),
+                    "gather",
+                    flops=3 * unit,
+                )
+            value, *ready["made"] = lax.optimization_barrier((value, *made))
             return value
 
         side_a, side_b, arriving = total_over_all(
-            (side_a, side_b, keep, arrived), before_last, before_sum
+            (side_a, side_b, keep, arrived), after_near, before_sum
         )
         if iteration == 0:
-            coef, *halves, present = ready["spread"]
+            coef, *halves, present = ready["made"]
         else:
-            coef, *halves = ready["gathered"]
+            coef, *halves = ready["made"]
         gradient, mixed = call(
             domain_side,
             (side_a, side_b, *halves),
-            (vmem((4 * NB, 4 * NB)), vmem((4, NB, NB))),
+            (vmem((4 * NB, 4 * NB)), vmem((2, SB, SB))),
             "domain_side",
             flops=unit,
         )
@@ -872,7 +877,7 @@
             present, coef, *halves, gradient, mixed, side_b, arriving
         )
         new_outs = (vmem((3 * NB, 4 * NB)),) + (vmem((3 * NB, 4 * NB), bf16),) * 2
-        far_outs = new_outs + (coef_out, vmem((4, NB, NB)))
+        far_outs = new_outs + (coef_out, vmem((2, SB, SB)))
         if iteration < ITERS - 1:
             fresh1, f1h, f1l, work, total, mine = call(
                 domain_far,

time: 91.5 us -> 89.4 us (0.977)
  waiting for transfers between devices: 25.5 us -> 23.1 us
    ppermute x8, waiting for transfers between devices: 12.9 us -> 10.4 us  [to_edge(): return lax.ppermute(value, 'grid', route)]
  transfers between devices with their start and end apart: 25 -> 25, of which waited for: 12 -> 15; matrix products, arithmetic and copies ran while one was open for 1% -> 1% of each run, Pallas kernels for 26% -> 27%
where the time goes in v2:
time: 89.4 us; the launch traced here: 89.2 us
  Pallas kernels  33.6 us (38%)
  starting transfers between devices  30.2 us (34%)
  waiting for transfers between devices  23.1 us (26%)
  local copies, waits for them, and re-layouts  1.39 us (2%)
  between operations  0.98 us (1%)
    pallas_call x30, Pallas kernels, call(): pl.pallas_call(kernel, out_shape=list(outs), in_specs=specs, out_specs=[p...  27.8 us
    ppermute x8, starting transfers between devices, to_edge(): return lax.ppermute(value, 'grid', route)  18.6 us
    ppermute x8, waiting for transfers between devices, to_orb(): return lax.ppermute(value, 'orb', [(0, 1), (1, 0)])  11.1 us
    ppermute x8, starting transfers between devices, to_orb(): return lax.ppermute(value, 'orb', [(0, 1), (1, 0)])  10.5 us
    ppermute x8, waiting for transfers between devices, to_edge(): return lax.ppermute(value, 'grid', route)  10.4 us
    pallas_call x1, Pallas kernels, sort_basis(): pl.pallas_call(functools.partial(sort_kernel, total_blocks), out_shape=ha...  3.28 us
    pallas_call x1, Pallas kernels, cut(): pl.pallas_call(cut_kernel, out_shape=[vmem(own.shape), vmem((EARLY, HALF,...  2.55 us
  transfers between devices with their start and end apart: 25, of which 15 were waited for; matrix products, arithmetic and copies ran while one was open for 1% of the time, Pallas kernels for 27%

profile of v2, /device:TPU:0, one launch (start us, length us, event | category | flops | bytes accessed | tf_op | source)
XLA Modules:
  0.0 89.2 jit_solution(11043674768037675150)
XLA Ops:
  1.1 2.6 %collective-permute-start.3 = (f32[6,64,128]{2,1,0:T(8,128)}, f32[6,64,128]{2,1,0:T(8,128)S(1)}, u32[]{:S(2)}, u32[]{:S(2)}) collective-permute-start(f32[6,64,128]{2,1,0:T(8,128)} %bitcast.7), channel_id=1, source_target_pairs={{0,1},{1,0},{2,3},{3,2},{4,5},{5,4},{6,7},{7,6},{8,9},{9,8},{10,11... | collective-permute-start | bytes 589832 | tf_op jit(solution)/shard_map/ppermute | solution.py:737
  3.7 4.3 %collective-permute-start.1 = (f32[6,64,128]{2,1,0:T(8,128)}, f32[6,64,128]{2,1,0:T(8,128)S(1)}, u32[]{:S(2)}, u32[]{:S(2)}) collective-permute-start(f32[6,64,128]{2,1,0:T(8,128)} %bitcast.8), channel_id=1, source_target_pairs={{0,30},{2,4},{4,2},{6,8},{8,6},{10,12},{12,10},{14,16},{16,14},{18... | collective-permute-start | bytes 589832 | tf_op jit(solution)/shard_map/ppermute | solution.py:733
  8.0 2.5 %cut.1 = (f32[6,64,128]{2,1,0:T(8,128)S(1)}, f32[8,64,128]{2,1,0:T(8,128)S(1)}, f32[8,64,128]{2,1,0:T(8,128)}, f32[8,128]{1,0:T(8,128)S(1)}) custom-call(s32[2,4]{1,0:T(2,128)} %own_lists.3, f32[6,64,128]{2,1,0:T(8,128)} %bitcast.9, f32[16,64,128]{2,1,0:T(8,128)} %bitcast.4, f32[6,64,128]{2,1,0:T(8,128)S(1)} %collective-permute-done.other), custom_call_target="tpu_custom_call" | custom-call | tf_op jit(solution)/shard_map/cut/pallas_call | solution.py:132
  10.6 0.6 collective-permute-start.5
  11.2 3.3 %sort_basis.1 = (bf16[768,1280]{1,0:T(8,128)(2,1)S(1)}, bf16[768,1280]{1,0:T(8,128)(2,1)S(1)}, bf16[1280,768]{1,0:T(8,128)(2,1)S(1)}, bf16[1280,768]{1,0:T(8,128)(2,1)S(1)}, f32[8,128]{1,0:T(8,128)S(1)}) custom-call(s32[1,6]{1,0:T(1,128)} %blocks.1, f32[1,1280,768]{2,1,0:T(8,128)} %basis.1), custom_call_target="tpu_custom_call" | custom-call | flops 3019898880 | tf_op jit(solution)/shard_map/sort_basis/pallas_call | solution.py:153
  14.7 1.6 %collective-permute-start.2 = (f32[328,128]{1,0:T(8,128)S(1)}, f32[328,128]{1,0:T(8,128)S(1)}, u32[]{:S(2)}, u32[]{:S(2)}) collective-permute-start(f32[328,128]{1,0:T(8,128)S(1)} %far_message.1), channel_id=1, source_target_pairs={{0,1},{1,0},{2,3},{3,2},{4,5},{5,4},{6,7},{7,6},{8,9},{9,8},{10,11... | collective-permute-start | bytes 503816 | tf_op jit(solution)/shard_map/ppermute | solution.py:737
  16.2 0.8 collective-permute-done.5.early
  17.0 2.8 %rho_first.1.rho = f32[1,1280]{1,0:T(1,128)S(1)} custom-call(bf16[768,1280]{1,0:T(8,128)(2,1)S(1)} %get-tuple-element.94.th, bf16[768,1280]{1,0:T(8,128)(2,1)S(1)} %get-tuple-element.95.tl, f32[6,64,128]{2,1,0:T(8,128)S(1)} %get-tuple-element.100.own, f32[6,64,128]{2,1,0:T(8,128)S(1)} %hold.1.own_far, f32[6,64,128]{2,1,0:T(8,128)S(1)} %collective-permute-done.1.edge, ...), custom_call_target="tpu_custom_call" | custom-call | flops 2516582400 | tf_op jit(solution)/shard_map/rho_first/pallas_call | solution.py:81
  19.8 1.6 %collective-permute-done.2.edge_far = f32[328,128]{1,0:T(8,128)S(1)} collective-permute-done((f32[328,128]{1,0:T(8,128)S(1)}, f32[328,128]{1,0:T(8,128)S(1)}, u32[]{:S(2)}, u32[]{:S(2)}) %collective-permute-start.2) | collective-permute-done | bytes 167968 | tf_op jit(solution)/shard_map/ppermute | solution.py:737
  21.4 1.6 %fock_other.2 = (f32[1,1280]{1,0:T(1,128)S(1)}, f32[328,128]{1,0:T(8,128)S(1)}, f32[64,128]{1,0:T(8,128)S(1)}) custom-call(f32[1,1280]{1,0:T(1,128)S(1)} %copy-done.7, f32[1,1280]{1,0:T(1,128)S(1)} %copy-done.8, bf16[768,1280]{1,0:T(8,128)(2,1)S(1)} %get-tuple-element.94.th, bf16[768,1280]{1,0:T(8,128)(2,1)S(1)} %get-tuple-element.95.tl, ...), custom_call_target="tpu_custom_call" | custom-call | flops 1509949440 | tf_op jit(solution)/shard_map/fock_other/pallas_call | solution.py:81
  23.2 1.6 %fock_side.2 = (f32[336,128]{1,0:T(8,128)S(1)}, f32[320,128]{1,0:T(8,128)S(1)}) custom-call(bf16[768,1280]{1,0:T(8,128)(2,1)S(1)} %get-tuple-element.94.th, bf16[768,1280]{1,0:T(8,128)(2,1)S(1)} %get-tuple-element.95.tl, bf16[1280,768]{1,0:T(8,128)(2,1)S(1)} %get-tuple-element.96.nh, bf16[1280,768]{1,0:T(8,128)(2,1)S(1)} %get-tuple-element.97.nl, ...), custom_call_target="tpu_custom_call" | custom-call | flops 1509949440 | tf_op jit(solution)/shard_map/fock_side/pallas_call | solution.py:81
  24.8 1.6 %collective-permute-start.10 = (f32[400,128]{1,0:T(8,128)S(1)}, f32[400,128]{1,0:T(8,128)S(1)}, u32[]{:S(2)}, u32[]{:S(2)}) collective-permute-start(f32[400,128]{1,0:T(8,128)S(1)} %get-tuple-element.125.side_a), channel_id=1, source_target_pairs={{0,1},{1,0},{2,3},{3,2},{4,5},{5,4},{6,7},{7,6},{8,9},{9,8},{10,11... | collective-permute-start | bytes 614408 | tf_op jit(solution)/shard_map/ppermute | solution.py:737
  26.4 1.9 %collective-permute-start.7 = (f32[320,128]{1,0:T(8,128)S(1)}, f32[320,128]{1,0:T(8,128)S(1)}, u32[]{:S(2)}, u32[]{:S(2)}) collective-permute-start(f32[320,128]{1,0:T(8,128)S(1)} %get-tuple-element.111.left), channel_id=1, source_target_pairs={{0,30},{2,4},{4,2},{6,8},{8,6},{10,12},{12,10},{14,16},{16,14},{18... | collective-permute-start | bytes 491528 | tf_op jit(solution)/shard_map/ppermute | solution.py:733
  28.8 5.1 %collective-permute-done.7.right = f32[320,128]{1,0:T(8,128)S(1)} collective-permute-done((f32[320,128]{1,0:T(8,128)S(1)}, f32[320,128]{1,0:T(8,128)S(1)}, u32[]{:S(2)}, u32[]{:S(2)}) %collective-permute-start.7) | collective-permute-done | bytes 163872 | tf_op jit(solution)/shard_map/ppermute | solution.py:733
  33.9 0.6 collective-permute-start.8
  34.5 1.6 %collective-permute-start.11 = (f32[336,128]{1,0:T(8,128)S(1)}, f32[336,128]{1,0:T(8,128)S(1)}, u32[]{:S(2)}, u32[]{:S(2)}) collective-permute-start(f32[336,128]{1,0:T(8,128)S(1)} %get-tuple-element.126.side_a), channel_id=1, source_target_pairs={{0,30},{2,4},{4,2},{6,8},{8,6},{10,12},{12,10},{14,16},{16,14},{18... | collective-permute-start | bytes 516104 | tf_op jit(solution)/shard_map/ppermute | solution.py:733
  36.1 0.6 convert_element_type.6.other_lists
  36.8 1.6 %collective-permute-done.9.partner = f32[8,64,128]{2,1,0:T(8,128)S(1)} collective-permute-done((f32[8,64,128]{2,1,0:T(8,128)}, f32[8,64,128]{2,1,0:T(8,128)S(1)}, u32[]{:S(2)}, u32[]{:S(2)}) %collective-permute-start.9) | collective-permute-done | bytes 262176 | tf_op jit(solution)/shard_map/ppermute | solution.py:737
  38.4 0.7 copy-done.10
  39.1 1.8 %spread.1 = (f32[768,512]{1,0:T(8,128)S(1)}, bf16[768,512]{1,0:T(8,128)(2,1)S(1)}, bf16[768,512]{1,0:T(8,128)(2,1)S(1)}, bf16[512,768]{1,0:T(8,128)(2,1)S(1)}, b...) custom-call(s32[2,4]{1,0:T(2,128)} %own_lists.3, s32[2,4]{1,0:T(2,128)} %convert_element_type.6.other_lists, ...), custom_call_target="tpu_custom_call" | custom-call | flops 1509949440 | tf_op jit(solution)/shard_map/spread/pallas_call | solution.py:81
  40.9 0.6 collective-permute-done.8.arrived_b
  41.5 0.6 collective-permute-done.11.arrived_a
  42.2 1.3 %domain_side.2 = (f32[512,512]{1,0:T(8,128)S(1)}, f32[2,256,256]{2,1,0:T(8,128)S(1)}) custom-call(f32[336,128]{1,0:T(8,128)S(1)} %get-tuple-element.129.side_a, f32[384,128]{1,0:T(8,128)S(1)} %get-tuple-element.130.side_b, bf16[768,512]{1,0:T(8,128)(2,1)S(1)} %get-tuple-element.121.ch, bf16[768,512]{1,0:T(8,128)(2,1)S(1)} %get-tuple-element.122.cl, ...), custom_call_target="tpu_custom_call" | custom-call | flops 503316480 | tf_op jit(solution)/shard_map/domain_side/pallas_call | solution.py:81
  43.6 2.4 %domain_far.1 = (f32[384,512]{1,0:T(8,128)S(1)}, bf16[384,512]{1,0:T(8,128)(2,1)S(1)}, bf16[384,512]{1,0:T(8,128)(2,1)S(1)}, f32[768,512]{1,0:T(8,128)S(1)}, f32...) custom-call(f32[24,128]{1,0:T(8,128)S(1)} %get-tuple-element.119.present, f32[768,512]{1,0:T(8,128)S(1)} %get-tuple-element.120.coef, ...), custom_call_target="tpu_custom_call" | custom-call | flops 1006632960 | tf_op jit(solution)/shard_map/domain_far/pallas_call | solution.py:81
  46.0 1.6 %collective-permute-start.14 = (f32[392,128]{1,0:T(8,128)S(1)}, f32[392,128]{1,0:T(8,128)S(1)}, u32[]{:S(2)}, u32[]{:S(2)}) collective-permute-start(f32[392,128]{1,0:T(8,128)S(1)} %get-tuple-element.144.mine), channel_id=1, source_target_pairs={{0,30},{2,4},{4,2},{6,8},{8,6},{10,12},{12,10},{14,16},{16,14},{18... | collective-permute-start | bytes 602120 | tf_op jit(solution)/shard_map/ppermute | solution.py:733
  47.6 1.3 %domain_other.1 = (f32[384,512]{1,0:T(8,128)S(1)}, bf16[384,512]{1,0:T(8,128)(2,1)S(1)}, bf16[384,512]{1,0:T(8,128)(2,1)S(1)}, f32[328,128]{1,0:T(8,128)S(1)}, f32[64,128]{1,0:T(8,128)S(1)}) custom-call(f32[24,128]{1,0:T(8,128)S(1)} %get-tuple-element.119.present, f32[768,512]{1,0:T(8,128)S(1)} %get-tuple-element.120.coef, ...), custom_call_target="tpu_custom_call" | custom-call | flops 503316480 | tf_op jit(solution)/shard_map/domain_other/pallas_call | solution.py:81
  49.4 1.0 %collective-permute-done.13.arrived = f32[328,128]{1,0:T(8,128)S(1)} collective-permute-done((f32[328,128]{1,0:T(8,128)S(1)}, f32[328,128]{1,0:T(8,128)S(1)}, u32[]{:S(2)}, u32[]{:S(2)}) %collective-permute-start.13) | collective-permute-done | bytes 167968 | tf_op jit(solution)/shard_map/ppermute | solution.py:727
  50.4 2.9 %collective-permute-start.16 = (f32[336,128]{1,0:T(8,128)S(1)}, f32[336,128]{1,0:T(8,128)S(1)}, u32[]{:S(2)}, u32[]{:S(2)}) collective-permute-start(f32[336,128]{1,0:T(8,128)S(1)} %get-tuple-element.142.near), channel_id=1, source_target_pairs={{0,30},{2,4},{4,2},{6,8},{8,6},{10,12},{12,10},{14,16},{16,14},{18... | collective-permute-start | bytes 516104 | tf_op jit(solution)/shard_map/ppermute | solution.py:733
  53.3 0.6 collective-permute-done.14.arrived
  54.1 0.9 rho_near.1.before
  55.5 0.9 rho_other.1.rho
  56.4 1.6 %collective-permute-done.16.arrived = f32[336,128]{1,0:T(8,128)S(1)} collective-permute-done((f32[336,128]{1,0:T(8,128)S(1)}, f32[336,128]{1,0:T(8,128)S(1)}, u32[]{:S(2)}, u32[]{:S(2)}) %collective-permute-start.16) | collective-permute-done | bytes 172064 | tf_op jit(solution)/shard_map/ppermute | solution.py:733
  58.0 2.1 %fock_other.3 = (f32[1,1280]{1,0:T(1,128)S(1)}, f32[328,128]{1,0:T(8,128)S(1)}, f32[64,128]{1,0:T(8,128)S(1)}) custom-call(f32[1,1280]{1,0:T(1,128)S(1)} %copy-done.7, f32[1,1280]{1,0:T(1,128)S(1)} %copy-done.8, bf16[768,1280]{1,0:T(8,128)(2,1)S(1)} %get-tuple-element.94.th, bf16[768,1280]{1,0:T(8,128)(2,1)S(1)} %copy-done.1, ...), custom_call_target="tpu_custom_call" | custom-call | flops 1509949440 | tf_op jit(solution)/shard_map/fock_other/pallas_call | solution.py:81
  60.2 1.5 %fock_side.3 = (f32[336,128]{1,0:T(8,128)S(1)}, f32[320,128]{1,0:T(8,128)S(1)}) custom-call(bf16[768,1280]{1,0:T(8,128)(2,1)S(1)} %get-tuple-element.94.th, bf16[768,1280]{1,0:T(8,128)(2,1)S(1)} %copy-done.1, bf16[1280,768]{1,0:T(8,128)(2,1)S(1)} %copy-done.3, bf16[1280,768]{1,0:T(8,128)(2,1)S(1)} %copy-done.5, f32[1,1280]{1,0:T(1,128)S(1)} %get-tuple-element.147.scale), custom_call_target="tpu_custom_call" | custom-call | flops 1509949440 | tf_op jit(solution)/shard_map/fock_side/pallas_call | solution.py:81
  61.8 1.6 %collective-permute-start.20 = (f32[400,128]{1,0:T(8,128)S(1)}, f32[400,128]{1,0:T(8,128)S(1)}, u32[]{:S(2)}, u32[]{:S(2)}) collective-permute-start(f32[400,128]{1,0:T(8,128)S(1)} %get-tuple-element.165.side_a), channel_id=1, source_target_pairs={{0,1},{1,0},{2,3},{3,2},{4,5},{5,4},{6,7},{7,6},{8,9},{9,8},{10,11... | collective-permute-start | bytes 614408 | tf_op jit(solution)/shard_map/ppermute | solution.py:737
  63.3 2.5 %collective-permute-start.18 = (f32[320,128]{1,0:T(8,128)S(1)}, f32[320,128]{1,0:T(8,128)S(1)}, u32[]{:S(2)}, u32[]{:S(2)}) collective-permute-start(f32[320,128]{1,0:T(8,128)S(1)} %get-tuple-element.152.left), channel_id=1, source_target_pairs={{0,30},{2,4},{4,2},{6,8},{8,6},{10,12},{12,10},{14,16},{16,14},{18... | collective-permute-start | bytes 491528 | tf_op jit(solution)/shard_map/ppermute | solution.py:733
  65.9 3.5 %collective-permute-done.20.arrived = f32[400,128]{1,0:T(8,128)S(1)} collective-permute-done((f32[400,128]{1,0:T(8,128)S(1)}, f32[400,128]{1,0:T(8,128)S(1)}, u32[]{:S(2)}, u32[]{:S(2)}) %collective-permute-start.20) | collective-permute-done | bytes 204832 | tf_op jit(solution)/shard_map/ppermute | solution.py:737
  69.4 1.6 %collective-permute-start.21 = (f32[336,128]{1,0:T(8,128)S(1)}, f32[336,128]{1,0:T(8,128)S(1)}, u32[]{:S(2)}, u32[]{:S(2)}) collective-permute-start(f32[336,128]{1,0:T(8,128)S(1)} %get-tuple-element.166.side_a), channel_id=1, source_target_pairs={{0,30},{2,4},{4,2},{6,8},{8,6},{10,12},{12,10},{14,16},{16,14},{18... | collective-permute-start | bytes 516104 | tf_op jit(solution)/shard_map/ppermute | solution.py:733
  71.0 1.6 %collective-permute-start.19 = (f32[320,128]{1,0:T(8,128)S(1)}, f32[320,128]{1,0:T(8,128)S(1)}, u32[]{:S(2)}, u32[]{:S(2)}) collective-permute-start(f32[320,128]{1,0:T(8,128)S(1)} %add_b.3.side_b), channel_id=1, source_target_pairs={{0,1},{1,0},{2,3},{3,2},{4,5},{5,4},{6,7},{7,6},{8,9},{9,8},{10,11... | collective-permute-start | bytes 491528 | tf_op jit(solution)/shard_map/ppermute | solution.py:737
  72.6 0.8 gather.1
  73.4 3.0 %collective-permute-done.19.arrived_b = f32[320,128]{1,0:T(8,128)S(1)} collective-permute-done((f32[320,128]{1,0:T(8,128)S(1)}, f32[320,128]{1,0:T(8,128)S(1)}, u32[]{:S(2)}, u32[]{:S(2)}) %collective-permute-start.19) | collective-permute-done | bytes 163872 | tf_op jit(solution)/shard_map/ppermute | solution.py:737
  77.1 1.3 %domain_side.3 = (f32[512,512]{1,0:T(8,128)S(1)}, f32[2,256,256]{2,1,0:T(8,128)S(1)}) custom-call(f32[336,128]{1,0:T(8,128)S(1)} %get-tuple-element.169.side_a, f32[384,128]{1,0:T(8,128)S(1)} %get-tuple-element.170.side_b, bf16[768,512]{1,0:T(8,128)(2,1)S(1)} %get-tuple-element.161.ch, bf16[768,512]{1,0:T(8,128)(2,1)S(1)} %get-tuple-element.162.cl, ...), custom_call_target="tpu_custom_call" | custom-call | flops 503316480 | tf_op jit(solution)/shard_map/domain_side/pallas_call | solution.py:81
  78.5 2.4 %domain_edge.1 = (f32[384,512]{1,0:T(8,128)S(1)}, bf16[384,512]{1,0:T(8,128)(2,1)S(1)}, bf16[384,512]{1,0:T(8,128)(2,1)S(1)}, f32[768,512]{1,0:T(8,128)S(1)}, f3...) custom-call(f32[24,128]{1,0:T(8,128)S(1)} %get-tuple-element.119.present, f32[768,512]{1,0:T(8,128)S(1)} %get-tuple-element.160.coef, ...), custom_call_target="tpu_custom_call" | custom-call | flops 1006632960 | tf_op jit(solution)/shard_map/domain_edge/pallas_call | solution.py:81
  80.9 2.1 %collective-permute-start.24 = (f32[336,128]{1,0:T(8,128)S(1)}, f32[336,128]{1,0:T(8,128)S(1)}, u32[]{:S(2)}, u32[]{:S(2)}) collective-permute-start(f32[336,128]{1,0:T(8,128)S(1)} %get-tuple-element.184), channel_id=1, source_target_pairs={{0,30},{2,4},{4,2},{6,8},{8,6},{10,12},{12,10},{14,16},{16,14},{18... | collective-permute-start | bytes 516104 | tf_op jit(solution)/shard_map/ppermute | solution.py:733
  83.0 1.2 %domain_give.1 = (f32[384,512]{1,0:T(8,128)S(1)}, bf16[384,512]{1,0:T(8,128)(2,1)S(1)}, bf16[384,512]{1,0:T(8,128)(2,1)S(1)}, f32[5,64,128]{2,1,0:T(8,128)S(1)}) custom-call(f32[24,128]{1,0:T(8,128)S(1)} %get-tuple-element.119.present, f32[768,512]{1,0:T(8,128)S(1)} %get-tuple-element.160.coef, bf16[768,512]{1,0:T(8,128)(2,1)S(1)} %get-tuple-element.161.ch, ...), custom_call_target="tpu_custom_call" | custom-call | flops 503316480 | tf_op jit(solution)/shard_map/domain_give/pallas_call | solution.py:81
  84.3 2.3 %domain_last.1 = (f32[2,4,128,128]{3,2,1,0:T(8,128)}, f32[6,64,128]{2,1,0:T(8,128)S(1)}) custom-call(s32[2,4]{1,0:T(2,128)} %own_lists.3, f32[384,512]{1,0:T(8,128)S(1)} %get-tuple-element.174.fresh1, bf16[384,512]{1,0:T(8,128)(2,1)S(1)} %get-tuple-element.175.f1h, bf16[384,512]{1,0:T(8,128)(2,1)S(1)} %get-tuple-element.176.f1l, ...), custom_call_target="tpu_custom_call" | custom-call | tf_op jit(solution)/shard_map/domain_last/pallas_call | solution.py:81
  86.6 1.9 %collective-permute-done.24.from_edge = f32[336,128]{1,0:T(8,128)S(1)} collective-permute-done((f32[336,128]{1,0:T(8,128)S(1)}, f32[336,128]{1,0:T(8,128)S(1)}, u32[]{:S(2)}, u32[]{:S(2)}) %collective-permute-start.24) | collective-permute-done | bytes 172064 | tf_op jit(solution)/shard_map/ppermute | solution.py:733
  88.5 0.7 owner_rows.1
  (58 shorter events, 3.7 us)
Async XLA Ops:
  0.6 7.4 %collective-permute-start = (f32[6,64,128]{2,1,0:T(8,128)}, f32[6,64,128]{2,1,0:T(8,128)S(1)}, u32[]{:S(2)}, u32[]{:S(2)}) collective-permute-start(f32[6,64,128]{2,1,0:T(8,128)} %bitcast.6), channel_id=1, source_target_pairs={{0,2},{2,0},{4,6},{6,4},{8,10},{10,8},{12,14},{14,12},{16,18},{18,... | collective-permute-start | bytes 589832 | tf_op jit(solution)/shard_map/ppermute | solution.py:727
  1.1 13.4 %collective-permute-start.3 = (f32[6,64,128]{2,1,0:T(8,128)}, f32[6,64,128]{2,1,0:T(8,128)S(1)}, u32[]{:S(2)}, u32[]{:S(2)}) collective-permute-start(f32[6,64,128]{2,1,0:T(8,128)} %bitcast.7), channel_id=1, source_target_pairs={{0,1},{1,0},{2,3},{3,2},{4,5},{5,4},{6,7},{7,6},{8,9},{9,8},{10,11... | collective-permute-start | bytes 589832 | tf_op jit(solution)/shard_map/ppermute | solution.py:737
  3.7 10.9 %collective-permute-start.1 = (f32[6,64,128]{2,1,0:T(8,128)}, f32[6,64,128]{2,1,0:T(8,128)S(1)}, u32[]{:S(2)}, u32[]{:S(2)}) collective-permute-start(f32[6,64,128]{2,1,0:T(8,128)} %bitcast.8), channel_id=1, source_target_pairs={{0,30},{2,4},{4,2},{6,8},{8,6},{10,12},{12,10},{14,16},{16,14},{18... | collective-permute-start | bytes 589832 | tf_op jit(solution)/shard_map/ppermute | solution.py:733
  10.6 6.4 %collective-permute-start.5 = (f32[8,64,128]{2,1,0:T(8,128)S(1)}, f32[8,64,128]{2,1,0:T(8,128)S(1)}, u32[]{:S(2)}, u32[]{:S(2)}) collective-permute-start(f32[8,64,128]{2,1,0:T(8,128)S(1)} %get-tuple-element.101), channel_id=1, source_target_pairs={{0,1},{1,0},{2,3},{3,2},{4,5},{5,4},{6,7},{7,6},{8,9},{9,8},{10,11... | collective-permute-start | bytes 786440 | tf_op jit(solution)/shard_map/ppermute | solution.py:737
  14.5 8.7 %copy-start = (bf16[768,1280]{1,0:T(8,128)(2,1)}, bf16[768,1280]{1,0:T(8,128)(2,1)S(1)}, u32[]{:S(2)}) copy-start(bf16[768,1280]{1,0:T(8,128)(2,1)S(1)} %get-tuple-element.95.tl) | copy-start | bytes 5898244
  14.5 8.7 %copy-start.2 = (bf16[1280,768]{1,0:T(8,128)(2,1)}, bf16[1280,768]{1,0:T(8,128)(2,1)S(1)}, u32[]{:S(2)}) copy-start(bf16[1280,768]{1,0:T(8,128)(2,1)S(1)} %get-tuple-element.96.nh) | copy-start | bytes 5898244
  14.5 8.7 %copy-start.4 = (bf16[1280,768]{1,0:T(8,128)(2,1)}, bf16[1280,768]{1,0:T(8,128)(2,1)S(1)}, u32[]{:S(2)}) copy-start(bf16[1280,768]{1,0:T(8,128)(2,1)S(1)} %get-tuple-element.97.nl) | copy-start | bytes 5898244
  14.6 1.7 %collective-permute-start.4 = (f32[6,64,128]{2,1,0:T(8,128)S(1)}, f32[6,64,128]{2,1,0:T(8,128)S(1)}, u32[]{:S(2)}, u32[]{:S(2)}) collective-permute-start(f32[6,64,128]{2,1,0:T(8,128)S(1)} %hold.1.own_far), channel_id=1, source_target_pairs={{0,2},{2,0},{4,6},{6,4},{8,10},{10,8},{12,14},{14,12},{16,18},{18,... | collective-permute-start | bytes 589832 | tf_op jit(solution)/shard_map/ppermute | solution.py:727
  14.7 6.7 %collective-permute-start.2 = (f32[328,128]{1,0:T(8,128)S(1)}, f32[328,128]{1,0:T(8,128)S(1)}, u32[]{:S(2)}, u32[]{:S(2)}) collective-permute-start(f32[328,128]{1,0:T(8,128)S(1)} %far_message.1), channel_id=1, source_target_pairs={{0,1},{1,0},{2,3},{3,2},{4,5},{5,4},{6,7},{7,6},{8,9},{9,8},{10,11... | collective-permute-start | bytes 503816 | tf_op jit(solution)/shard_map/ppermute | solution.py:737
  17.0 2.8 %copy-start.9 = (f32[8,64,128]{2,1,0:T(8,128)}, f32[8,64,128]{2,1,0:T(8,128)S(1)}, u32[]{:S(2)}) copy-start(f32[8,64,128]{2,1,0:T(8,128)S(1)} %collective-permute-done.5.early) | copy-start | bytes 786436
  17.0 4.4 %copy-start.7 = (f32[1,1280]{1,0:T(1,128)S(1)}, f32[1,1280]{1,0:T(1,128)}, u32[]{:S(2)}) copy-start(f32[1,1280]{1,0:T(1,128)} %weights.3) | copy-start | bytes 15364
  17.0 4.4 %copy-start.8 = (f32[1,1280]{1,0:T(1,128)S(1)}, f32[1,1280]{1,0:T(1,128)}, u32[]{:S(2)}) copy-start(f32[1,1280]{1,0:T(1,128)} %external.3) | copy-start | bytes 15364
  23.1 1.7 %collective-permute-start.6 = (f32[328,128]{1,0:T(8,128)S(1)}, f32[328,128]{1,0:T(8,128)S(1)}, u32[]{:S(2)}, u32[]{:S(2)}) collective-permute-start(f32[328,128]{1,0:T(8,128)S(1)} %get-tuple-element.108), channel_id=1, source_target_pairs={{0,2},{2,0},{4,6},{6,4},{8,10},{10,8},{12,14},{14,12},{16,18},{18,... | collective-permute-start | bytes 503816 | tf_op jit(solution)/shard_map/ppermute | solution.py:727
  23.2 15.9 %copy-start.6 = (f32[2,4,128,128]{3,2,1,0:T(8,128)S(1)}, f32[2,4,128,128]{3,2,1,0:T(8,128)}, u32[]{:S(2)}) copy-start(f32[2,4,128,128]{3,2,1,0:T(8,128)} %param.13) | copy-start | bytes 1572868
  24.8 9.6 %collective-permute-start.10 = (f32[400,128]{1,0:T(8,128)S(1)}, f32[400,128]{1,0:T(8,128)S(1)}, u32[]{:S(2)}, u32[]{:S(2)}) collective-permute-start(f32[400,128]{1,0:T(8,128)S(1)} %get-tuple-element.125.side_a), channel_id=1, source_target_pairs={{0,1},{1,0},{2,3},{3,2},{4,5},{5,4},{6,7},{7,6},{8,9},{9,8},{10,11... | collective-permute-start | bytes 614408 | tf_op jit(solution)/shard_map/ppermute | solution.py:737
  26.4 7.4 %collective-permute-start.7 = (f32[320,128]{1,0:T(8,128)S(1)}, f32[320,128]{1,0:T(8,128)S(1)}, u32[]{:S(2)}, u32[]{:S(2)}) collective-permute-start(f32[320,128]{1,0:T(8,128)S(1)} %get-tuple-element.111.left), channel_id=1, source_target_pairs={{0,30},{2,4},{4,2},{6,8},{8,6},{10,12},{12,10},{14,16},{16,14},{18... | collective-permute-start | bytes 491528 | tf_op jit(solution)/shard_map/ppermute | solution.py:733
  28.2 10.1 %collective-permute-start.9 = (f32[8,64,128]{2,1,0:T(8,128)}, f32[8,64,128]{2,1,0:T(8,128)S(1)}, u32[]{:S(2)}, u32[]{:S(2)}) collective-permute-start(f32[8,64,128]{2,1,0:T(8,128)} %get-tuple-element.112), channel_id=1, source_target_pairs={{0,1},{1,0},{2,3},{3,2},{4,5},{5,4},{6,7},{7,6},{8,9},{9,8},{10,11... | collective-permute-start | bytes 786440 | tf_op jit(solution)/shard_map/ppermute | solution.py:737
  33.9 7.6 %collective-permute-start.8 = (f32[320,128]{1,0:T(8,128)S(1)}, f32[320,128]{1,0:T(8,128)S(1)}, u32[]{:S(2)}, u32[]{:S(2)}) collective-permute-start(f32[320,128]{1,0:T(8,128)S(1)} %add_b.2.side_b), channel_id=1, source_target_pairs={{0,1},{1,0},{2,3},{3,2},{4,5},{5,4},{6,7},{7,6},{8,9},{9,8},{10,11... | collective-permute-start | bytes 491528 | tf_op jit(solution)/shard_map/ppermute | solution.py:737
  34.5 7.6 %collective-permute-start.11 = (f32[336,128]{1,0:T(8,128)S(1)}, f32[336,128]{1,0:T(8,128)S(1)}, u32[]{:S(2)}, u32[]{:S(2)}) collective-permute-start(f32[336,128]{1,0:T(8,128)S(1)} %get-tuple-element.126.side_a), channel_id=1, source_target_pairs={{0,30},{2,4},{4,2},{6,8},{8,6},{10,12},{12,10},{14,16},{16,14},{18... | collective-permute-start | bytes 516104 | tf_op jit(solution)/shard_map/ppermute | solution.py:733
  38.4 0.7 copy-start.10
  42.1 1.5 %collective-permute-start.12 = (f32[328,128]{1,0:T(8,128)S(1)}, f32[328,128]{1,0:T(8,128)S(1)}, u32[]{:S(2)}, u32[]{:S(2)}) collective-permute-start(f32[328,128]{1,0:T(8,128)S(1)} %get-tuple-element.133), channel_id=1, source_target_pairs={{0,2},{2,0},{4,6},{6,4},{8,10},{10,8},{12,14},{14,12},{16,18},{18,... | collective-permute-start | bytes 503816 | tf_op jit(solution)/shard_map/ppermute | solution.py:727
  46.0 8.0 %collective-permute-start.14 = (f32[392,128]{1,0:T(8,128)S(1)}, f32[392,128]{1,0:T(8,128)S(1)}, u32[]{:S(2)}, u32[]{:S(2)}) collective-permute-start(f32[392,128]{1,0:T(8,128)S(1)} %get-tuple-element.144.mine), channel_id=1, source_target_pairs={{0,30},{2,4},{4,2},{6,8},{8,6},{10,12},{12,10},{14,16},{16,14},{18... | collective-permute-start | bytes 602120 | tf_op jit(solution)/shard_map/ppermute | solution.py:733
  48.9 5.2 %copy-start.1 = (bf16[768,1280]{1,0:T(8,128)(2,1)S(1)}, bf16[768,1280]{1,0:T(8,128)(2,1)}, u32[]{:S(2)}) copy-start(bf16[768,1280]{1,0:T(8,128)(2,1)} %copy-done) | copy-start | bytes 5898244
  48.9 1.5 %collective-permute-start.13 = (f32[328,128]{1,0:T(8,128)S(1)}, f32[328,128]{1,0:T(8,128)S(1)}, u32[]{:S(2)}, u32[]{:S(2)}) collective-permute-start(f32[328,128]{1,0:T(8,128)S(1)} %get-tuple-element.141), channel_id=1, source_target_pairs={{0,2},{2,0},{4,6},{6,4},{8,10},{10,8},{12,14},{14,12},{16,18},{18,... | collective-permute-start | bytes 503816 | tf_op jit(solution)/shard_map/ppermute | solution.py:727
  50.4 7.6 %collective-permute-start.16 = (f32[336,128]{1,0:T(8,128)S(1)}, f32[336,128]{1,0:T(8,128)S(1)}, u32[]{:S(2)}, u32[]{:S(2)}) collective-permute-start(f32[336,128]{1,0:T(8,128)S(1)} %get-tuple-element.142.near), channel_id=1, source_target_pairs={{0,30},{2,4},{4,2},{6,8},{8,6},{10,12},{12,10},{14,16},{16,14},{18... | collective-permute-start | bytes 516104 | tf_op jit(solution)/shard_map/ppermute | solution.py:733
  54.0 1.5 %collective-permute-start.15 = (f32[328,128]{1,0:T(8,128)S(1)}, f32[328,128]{1,0:T(8,128)S(1)}, u32[]{:S(2)}, u32[]{:S(2)}) collective-permute-start(f32[328,128]{1,0:T(8,128)S(1)} %get-tuple-element.145.near), channel_id=1, source_target_pairs={{0,2},{2,0},{4,6},{6,4},{8,10},{10,8},{12,14},{14,12},{16,18},{18,... | collective-permute-start | bytes 503816 | tf_op jit(solution)/shard_map/ppermute | solution.py:727
  55.0 3.0 %copy-start.3 = (bf16[1280,768]{1,0:T(8,128)(2,1)S(1)}, bf16[1280,768]{1,0:T(8,128)(2,1)}, u32[]{:S(2)}) copy-start(bf16[1280,768]{1,0:T(8,128)(2,1)} %copy-done.2) | copy-start | bytes 5898244
  55.0 3.0 %copy-start.5 = (bf16[1280,768]{1,0:T(8,128)(2,1)S(1)}, bf16[1280,768]{1,0:T(8,128)(2,1)}, u32[]{:S(2)}) copy-start(bf16[1280,768]{1,0:T(8,128)(2,1)} %copy-done.4) | copy-start | bytes 5898244
  60.1 1.6 %collective-permute-start.17 = (f32[328,128]{1,0:T(8,128)S(1)}, f32[328,128]{1,0:T(8,128)S(1)}, u32[]{:S(2)}, u32[]{:S(2)}) collective-permute-start(f32[328,128]{1,0:T(8,128)S(1)} %get-tuple-element.151), channel_id=1, source_target_pairs={{0,2},{2,0},{4,6},{6,4},{8,10},{10,8},{12,14},{14,12},{16,18},{18,... | collective-permute-start | bytes 503816 | tf_op jit(solution)/shard_map/ppermute | solution.py:727
  61.8 7.6 %collective-permute-start.20 = (f32[400,128]{1,0:T(8,128)S(1)}, f32[400,128]{1,0:T(8,128)S(1)}, u32[]{:S(2)}, u32[]{:S(2)}) collective-permute-start(f32[400,128]{1,0:T(8,128)S(1)} %get-tuple-element.165.side_a), channel_id=1, source_target_pairs={{0,1},{1,0},{2,3},{3,2},{4,5},{5,4},{6,7},{7,6},{8,9},{9,8},{10,11... | collective-permute-start | bytes 614408 | tf_op jit(solution)/shard_map/ppermute | solution.py:737
  63.3 7.7 %collective-permute-start.18 = (f32[320,128]{1,0:T(8,128)S(1)}, f32[320,128]{1,0:T(8,128)S(1)}, u32[]{:S(2)}, u32[]{:S(2)}) collective-permute-start(f32[320,128]{1,0:T(8,128)S(1)} %get-tuple-element.152.left), channel_id=1, source_target_pairs={{0,30},{2,4},{4,2},{6,8},{8,6},{10,12},{12,10},{14,16},{16,14},{18... | collective-permute-start | bytes 491528 | tf_op jit(solution)/shard_map/ppermute | solution.py:733
  69.4 7.6 %collective-permute-start.21 = (f32[336,128]{1,0:T(8,128)S(1)}, f32[336,128]{1,0:T(8,128)S(1)}, u32[]{:S(2)}, u32[]{:S(2)}) collective-permute-start(f32[336,128]{1,0:T(8,128)S(1)} %get-tuple-element.166.side_a), channel_id=1, source_target_pairs={{0,30},{2,4},{4,2},{6,8},{8,6},{10,12},{12,10},{14,16},{16,14},{18... | collective-permute-start | bytes 516104 | tf_op jit(solution)/shard_map/ppermute | solution.py:733
  71.0 5.4 %collective-permute-start.19 = (f32[320,128]{1,0:T(8,128)S(1)}, f32[320,128]{1,0:T(8,128)S(1)}, u32[]{:S(2)}, u32[]{:S(2)}) collective-permute-start(f32[320,128]{1,0:T(8,128)S(1)} %add_b.3.side_b), channel_id=1, source_target_pairs={{0,1},{1,0},{2,3},{3,2},{4,5},{5,4},{6,7},{7,6},{8,9},{9,8},{10,11... | collective-permute-start | bytes 491528 | tf_op jit(solution)/shard_map/ppermute | solution.py:737
  77.0 1.5 %collective-permute-start.22 = (f32[328,128]{1,0:T(8,128)S(1)}, f32[328,128]{1,0:T(8,128)S(1)}, u32[]{:S(2)}, u32[]{:S(2)}) collective-permute-start(f32[328,128]{1,0:T(8,128)S(1)} %get-tuple-element.173), channel_id=1, source_target_pairs={{0,2},{2,0},{4,6},{6,4},{8,10},{10,8},{12,14},{14,12},{16,18},{18,... | collective-permute-start | bytes 503816 | tf_op jit(solution)/shard_map/ppermute | solution.py:727
  80.9 7.6 %collective-permute-start.24 = (f32[336,128]{1,0:T(8,128)S(1)}, f32[336,128]{1,0:T(8,128)S(1)}, u32[]{:S(2)}, u32[]{:S(2)}) collective-permute-start(f32[336,128]{1,0:T(8,128)S(1)} %get-tuple-element.184), channel_id=1, source_target_pairs={{0,30},{2,4},{4,2},{6,8},{8,6},{10,12},{12,10},{14,16},{16,14},{18... | collective-permute-start | bytes 516104 | tf_op jit(solution)/shard_map/ppermute | solution.py:733
  84.2 2.4 %collective-permute-start.23 = (f32[5,64,128]{2,1,0:T(8,128)S(1)}, f32[5,64,128]{2,1,0:T(8,128)S(1)}, u32[]{:S(2)}, u32[]{:S(2)}) collective-permute-start(f32[5,64,128]{2,1,0:T(8,128)S(1)} %get-tuple-element.183), channel_id=1, source_target_pairs={{0,2},{2,0},{4,6},{6,4},{8,10},{10,8},{12,14},{14,12},{16,18},{18,... | collective-permute-start | bytes 491528 | tf_op jit(solution)/shard_map/ppermute | solution.py:727

commit v3 on v2

--- a/solution.py
+++ b/solution.py
@@ -846,7 +846,7 @@
                     "spread",
                     smem=(0, 1),
                     plain=(2, 3, 4),
-                    flops=3 * unit,
+                    flops=unit,
                 )
             else:
                 made = call(

time: 89.4 us -> 88.9 us (level)
  waiting for transfers between devices: 23.1 us -> 21.7 us
    ppermute x8, waiting for transfers between devices: 10.4 us -> 4.25 us  [to_edge(): return lax.ppermute(value, 'grid', route)]
    ppermute x8, waiting for transfers between devices: 11.1 us -> 15.9 us  [to_orb(): return lax.ppermute(value, 'orb', [(0, 1), (1, 0)])]
    ppermute x8, starting transfers between devices: 10.5 us -> 11.5 us  [to_orb(): return lax.ppermute(value, 'orb', [(0, 1), (1, 0)])]
  transfers between devices with their start and end apart: 25 -> 25, of which waited for: 15 -> 14; matrix products, arithmetic and copies ran while one was open for 1% -> 1% of each run, Pallas kernels for 27% -> 27%
where the time goes in v3:
time: 88.9 us; the launch traced here: 88.7 us
  Pallas kernels  33.6 us (38%)
  starting transfers between devices  31 us (35%)
  waiting for transfers between devices  21.7 us (24%)
  local copies, waits for them, and re-layouts  1.39 us (2%)
  between operations  0.98 us (1%)
    pallas_call x30, Pallas kernels, call(): pl.pallas_call(kernel, out_shape=list(outs), in_specs=specs, out_specs=[p...  27.8 us
    ppermute x8, starting transfers between devices, to_edge(): return lax.ppermute(value, 'grid', route)  18.5 us
    ppermute x8, waiting for transfers between devices, to_orb(): return lax.ppermute(value, 'orb', [(0, 1), (1, 0)])  15.9 us
    ppermute x8, starting transfers between devices, to_orb(): return lax.ppermute(value, 'orb', [(0, 1), (1, 0)])  11.5 us
    ppermute x8, waiting for transfers between devices, to_edge(): return lax.ppermute(value, 'grid', route)  4.25 us
    pallas_call x1, Pallas kernels, sort_basis(): pl.pallas_call(functools.partial(sort_kernel, total_blocks), out_shape=ha...  3.28 us
    pallas_call x1, Pallas kernels, cut(): pl.pallas_call(cut_kernel, out_shape=[vmem(own.shape), vmem((EARLY, HALF,...  2.55 us
  transfers between devices with their start and end apart: 25, of which 14 were waited for; matrix products, arithmetic and copies ran while one was open for 1% of the time, Pallas kernels for 27%

profile of v3, /device:TPU:0, one launch (start us, length us, event | category | flops | bytes accessed | tf_op | source)
XLA Modules:
  0.0 88.7 jit_solution(11983116815273186650)
XLA Ops:
  1.1 2.6 %collective-permute-start.3 = (f32[6,64,128]{2,1,0:T(8,128)}, f32[6,64,128]{2,1,0:T(8,128)S(1)}, u32[]{:S(2)}, u32[]{:S(2)}) collective-permute-start(f32[6,64,128]{2,1,0:T(8,128)} %bitcast.7), channel_id=1, source_target_pairs={{0,1},{1,0},{2,3},{3,2},{4,5},{5,4},{6,7},{7,6},{8,9},{9,8},{10,11... | collective-permute-start | bytes 589832 | tf_op jit(solution)/shard_map/ppermute | solution.py:737
  3.7 4.3 %collective-permute-start.1 = (f32[6,64,128]{2,1,0:T(8,128)}, f32[6,64,128]{2,1,0:T(8,128)S(1)}, u32[]{:S(2)}, u32[]{:S(2)}) collective-permute-start(f32[6,64,128]{2,1,0:T(8,128)} %bitcast.8), channel_id=1, source_target_pairs={{0,30},{2,4},{4,2},{6,8},{8,6},{10,12},{12,10},{14,16},{16,14},{18... | collective-permute-start | bytes 589832 | tf_op jit(solution)/shard_map/ppermute | solution.py:733
  8.0 2.5 %cut.1 = (f32[6,64,128]{2,1,0:T(8,128)S(1)}, f32[8,64,128]{2,1,0:T(8,128)S(1)}, f32[8,64,128]{2,1,0:T(8,128)}, f32[8,128]{1,0:T(8,128)S(1)}) custom-call(s32[2,4]{1,0:T(2,128)} %own_lists.3, f32[6,64,128]{2,1,0:T(8,128)} %bitcast.9, f32[16,64,128]{2,1,0:T(8,128)} %bitcast.4, f32[6,64,128]{2,1,0:T(8,128)S(1)} %collective-permute-done.other), custom_call_target="tpu_custom_call" | custom-call | tf_op jit(solution)/shard_map/cut/pallas_call | solution.py:132
  10.6 0.6 collective-permute-start.5
  11.2 3.3 %sort_basis.1 = (bf16[768,1280]{1,0:T(8,128)(2,1)S(1)}, bf16[768,1280]{1,0:T(8,128)(2,1)S(1)}, bf16[1280,768]{1,0:T(8,128)(2,1)S(1)}, bf16[1280,768]{1,0:T(8,128)(2,1)S(1)}, f32[8,128]{1,0:T(8,128)S(1)}) custom-call(s32[1,6]{1,0:T(1,128)} %blocks.1, f32[1,1280,768]{2,1,0:T(8,128)} %basis.1), custom_call_target="tpu_custom_call" | custom-call | flops 3019898880 | tf_op jit(solution)/shard_map/sort_basis/pallas_call | solution.py:153
  14.7 1.6 %collective-permute-start.2 = (f32[328,128]{1,0:T(8,128)S(1)}, f32[328,128]{1,0:T(8,128)S(1)}, u32[]{:S(2)}, u32[]{:S(2)}) collective-permute-start(f32[328,128]{1,0:T(8,128)S(1)} %far_message.1), channel_id=1, source_target_pairs={{0,1},{1,0},{2,3},{3,2},{4,5},{5,4},{6,7},{7,6},{8,9},{9,8},{10,11... | collective-permute-start | bytes 503816 | tf_op jit(solution)/shard_map/ppermute | solution.py:737
  16.2 0.8 collective-permute-done.5.early
  17.0 2.8 %rho_first.1.rho = f32[1,1280]{1,0:T(1,128)S(1)} custom-call(bf16[768,1280]{1,0:T(8,128)(2,1)S(1)} %get-tuple-element.94.th, bf16[768,1280]{1,0:T(8,128)(2,1)S(1)} %get-tuple-element.95.tl, f32[6,64,128]{2,1,0:T(8,128)S(1)} %get-tuple-element.100.own, f32[6,64,128]{2,1,0:T(8,128)S(1)} %hold.1.own_far, f32[6,64,128]{2,1,0:T(8,128)S(1)} %collective-permute-done.1.edge, ...), custom_call_target="tpu_custom_call" | custom-call | flops 2516582400 | tf_op jit(solution)/shard_map/rho_first/pallas_call | solution.py:81
  19.8 1.6 %collective-permute-done.2.edge_far = f32[328,128]{1,0:T(8,128)S(1)} collective-permute-done((f32[328,128]{1,0:T(8,128)S(1)}, f32[328,128]{1,0:T(8,128)S(1)}, u32[]{:S(2)}, u32[]{:S(2)}) %collective-permute-start.2) | collective-permute-done | bytes 167968 | tf_op jit(solution)/shard_map/ppermute | solution.py:737
  21.4 1.6 %fock_other.2 = (f32[1,1280]{1,0:T(1,128)S(1)}, f32[328,128]{1,0:T(8,128)S(1)}, f32[64,128]{1,0:T(8,128)S(1)}) custom-call(f32[1,1280]{1,0:T(1,128)S(1)} %copy-done.7, f32[1,1280]{1,0:T(1,128)S(1)} %copy-done.8, bf16[768,1280]{1,0:T(8,128)(2,1)S(1)} %get-tuple-element.94.th, bf16[768,1280]{1,0:T(8,128)(2,1)S(1)} %get-tuple-element.95.tl, ...), custom_call_target="tpu_custom_call" | custom-call | flops 1509949440 | tf_op jit(solution)/shard_map/fock_other/pallas_call | solution.py:81
  23.2 1.6 %fock_side.2 = (f32[336,128]{1,0:T(8,128)S(1)}, f32[320,128]{1,0:T(8,128)S(1)}) custom-call(bf16[768,1280]{1,0:T(8,128)(2,1)S(1)} %get-tuple-element.94.th, bf16[768,1280]{1,0:T(8,128)(2,1)S(1)} %get-tuple-element.95.tl, bf16[1280,768]{1,0:T(8,128)(2,1)S(1)} %get-tuple-element.96.nh, bf16[1280,768]{1,0:T(8,128)(2,1)S(1)} %get-tuple-element.97.nl, ...), custom_call_target="tpu_custom_call" | custom-call | flops 1509949440 | tf_op jit(solution)/shard_map/fock_side/pallas_call | solution.py:81
  24.8 1.6 %collective-permute-start.10 = (f32[400,128]{1,0:T(8,128)S(1)}, f32[400,128]{1,0:T(8,128)S(1)}, u32[]{:S(2)}, u32[]{:S(2)}) collective-permute-start(f32[400,128]{1,0:T(8,128)S(1)} %get-tuple-element.125.side_a), channel_id=1, source_target_pairs={{0,1},{1,0},{2,3},{3,2},{4,5},{5,4},{6,7},{7,6},{8,9},{9,8},{10,11... | collective-permute-start | bytes 614408 | tf_op jit(solution)/shard_map/ppermute | solution.py:737
  26.4 1.9 %collective-permute-start.7 = (f32[320,128]{1,0:T(8,128)S(1)}, f32[320,128]{1,0:T(8,128)S(1)}, u32[]{:S(2)}, u32[]{:S(2)}) collective-permute-start(f32[320,128]{1,0:T(8,128)S(1)} %get-tuple-element.111.left), channel_id=1, source_target_pairs={{0,30},{2,4},{4,2},{6,8},{8,6},{10,12},{12,10},{14,16},{16,14},{18... | collective-permute-start | bytes 491528 | tf_op jit(solution)/shard_map/ppermute | solution.py:733
  28.8 4.0 %collective-permute-done.10.arrived = f32[400,128]{1,0:T(8,128)S(1)} collective-permute-done((f32[400,128]{1,0:T(8,128)S(1)}, f32[400,128]{1,0:T(8,128)S(1)}, u32[]{:S(2)}, u32[]{:S(2)}) %collective-permute-start.10) | collective-permute-done | bytes 204832 | tf_op jit(solution)/shard_map/ppermute | solution.py:737
  32.8 1.0 %collective-permute-start.11 = (f32[336,128]{1,0:T(8,128)S(1)}, f32[336,128]{1,0:T(8,128)S(1)}, u32[]{:S(2)}, u32[]{:S(2)}) collective-permute-start(f32[336,128]{1,0:T(8,128)S(1)} %get-tuple-element.126.side_a), channel_id=1, source_target_pairs={{0,30},{2,4},{4,2},{6,8},{8,6},{10,12},{12,10},{14,16},{16,14},{18... | collective-permute-start | bytes 516104 | tf_op jit(solution)/shard_map/ppermute | solution.py:733
  33.9 1.5 %collective-permute-start.8 = (f32[320,128]{1,0:T(8,128)S(1)}, f32[320,128]{1,0:T(8,128)S(1)}, u32[]{:S(2)}, u32[]{:S(2)}) collective-permute-start(f32[320,128]{1,0:T(8,128)S(1)} %add_b.2.side_b), channel_id=1, source_target_pairs={{0,1},{1,0},{2,3},{3,2},{4,5},{5,4},{6,7},{7,6},{8,9},{9,8},{10,11... | collective-permute-start | bytes 491528 | tf_op jit(solution)/shard_map/ppermute | solution.py:737
  35.4 0.6 convert_element_type.6.other_lists
  36.0 2.3 %collective-permute-done.9.partner = f32[8,64,128]{2,1,0:T(8,128)S(1)} collective-permute-done((f32[8,64,128]{2,1,0:T(8,128)}, f32[8,64,128]{2,1,0:T(8,128)S(1)}, u32[]{:S(2)}, u32[]{:S(2)}) %collective-permute-start.9) | collective-permute-done | bytes 262176 | tf_op jit(solution)/shard_map/ppermute | solution.py:737
  38.4 0.7 copy-done.10
  39.1 1.8 %spread.1 = (f32[768,512]{1,0:T(8,128)S(1)}, bf16[768,512]{1,0:T(8,128)(2,1)S(1)}, bf16[768,512]{1,0:T(8,128)(2,1)S(1)}, bf16[512,768]{1,0:T(8,128)(2,1)S(1)}, b...) custom-call(s32[2,4]{1,0:T(2,128)} %own_lists.3, s32[2,4]{1,0:T(2,128)} %convert_element_type.6.other_lists, ...), custom_call_target="tpu_custom_call" | custom-call | flops 503316480 | tf_op jit(solution)/shard_map/spread/pallas_call | solution.py:81
  40.9 0.6 collective-permute-done.8.arrived_b
  41.6 1.3 %domain_side.2 = (f32[512,512]{1,0:T(8,128)S(1)}, f32[2,256,256]{2,1,0:T(8,128)S(1)}) custom-call(f32[336,128]{1,0:T(8,128)S(1)} %get-tuple-element.129.side_a, f32[384,128]{1,0:T(8,128)S(1)} %get-tuple-element.130.side_b, bf16[768,512]{1,0:T(8,128)(2,1)S(1)} %get-tuple-element.121.ch, bf16[768,512]{1,0:T(8,128)(2,1)S(1)} %get-tuple-element.122.cl, ...), custom_call_target="tpu_custom_call" | custom-call | flops 503316480 | tf_op jit(solution)/shard_map/domain_side/pallas_call | solution.py:81
  43.0 2.4 %domain_far.1 = (f32[384,512]{1,0:T(8,128)S(1)}, bf16[384,512]{1,0:T(8,128)(2,1)S(1)}, bf16[384,512]{1,0:T(8,128)(2,1)S(1)}, f32[768,512]{1,0:T(8,128)S(1)}, f32...) custom-call(f32[24,128]{1,0:T(8,128)S(1)} %get-tuple-element.119.present, f32[768,512]{1,0:T(8,128)S(1)} %get-tuple-element.120.coef, ...), custom_call_target="tpu_custom_call" | custom-call | flops 1006632960 | tf_op jit(solution)/shard_map/domain_far/pallas_call | solution.py:81
  45.4 1.7 %collective-permute-start.14 = (f32[392,128]{1,0:T(8,128)S(1)}, f32[392,128]{1,0:T(8,128)S(1)}, u32[]{:S(2)}, u32[]{:S(2)}) collective-permute-start(f32[392,128]{1,0:T(8,128)S(1)} %get-tuple-element.144.mine), channel_id=1, source_target_pairs={{0,30},{2,4},{4,2},{6,8},{8,6},{10,12},{12,10},{14,16},{16,14},{18... | collective-permute-start | bytes 602120 | tf_op jit(solution)/shard_map/ppermute | solution.py:733
  47.1 1.3 %domain_other.1 = (f32[384,512]{1,0:T(8,128)S(1)}, bf16[384,512]{1,0:T(8,128)(2,1)S(1)}, bf16[384,512]{1,0:T(8,128)(2,1)S(1)}, f32[328,128]{1,0:T(8,128)S(1)}, f32[64,128]{1,0:T(8,128)S(1)}) custom-call(f32[24,128]{1,0:T(8,128)S(1)} %get-tuple-element.119.present, f32[768,512]{1,0:T(8,128)S(1)} %get-tuple-element.120.coef, ...), custom_call_target="tpu_custom_call" | custom-call | flops 503316480 | tf_op jit(solution)/shard_map/domain_other/pallas_call | solution.py:81
  48.9 1.0 %collective-permute-done.13.arrived = f32[328,128]{1,0:T(8,128)S(1)} collective-permute-done((f32[328,128]{1,0:T(8,128)S(1)}, f32[328,128]{1,0:T(8,128)S(1)}, u32[]{:S(2)}, u32[]{:S(2)}) %collective-permute-start.13) | collective-permute-done | bytes 167968 | tf_op jit(solution)/shard_map/ppermute | solution.py:727
  49.9 2.8 %collective-permute-start.16 = (f32[336,128]{1,0:T(8,128)S(1)}, f32[336,128]{1,0:T(8,128)S(1)}, u32[]{:S(2)}, u32[]{:S(2)}) collective-permute-start(f32[336,128]{1,0:T(8,128)S(1)} %get-tuple-element.142.near), channel_id=1, source_target_pairs={{0,30},{2,4},{4,2},{6,8},{8,6},{10,12},{12,10},{14,16},{16,14},{18... | collective-permute-start | bytes 516104 | tf_op jit(solution)/shard_map/ppermute | solution.py:733
  52.7 0.6 collective-permute-done.14.arrived
  53.5 0.9 rho_near.1.before
  54.9 0.9 rho_other.1.rho
  55.8 1.8 %collective-permute-done.16.arrived = f32[336,128]{1,0:T(8,128)S(1)} collective-permute-done((f32[336,128]{1,0:T(8,128)S(1)}, f32[336,128]{1,0:T(8,128)S(1)}, u32[]{:S(2)}, u32[]{:S(2)}) %collective-permute-start.16) | collective-permute-done | bytes 172064 | tf_op jit(solution)/shard_map/ppermute | solution.py:733
  57.5 2.1 %fock_other.3 = (f32[1,1280]{1,0:T(1,128)S(1)}, f32[328,128]{1,0:T(8,128)S(1)}, f32[64,128]{1,0:T(8,128)S(1)}) custom-call(f32[1,1280]{1,0:T(1,128)S(1)} %copy-done.7, f32[1,1280]{1,0:T(1,128)S(1)} %copy-done.8, bf16[768,1280]{1,0:T(8,128)(2,1)S(1)} %get-tuple-element.94.th, bf16[768,1280]{1,0:T(8,128)(2,1)S(1)} %copy-done.1, ...), custom_call_target="tpu_custom_call" | custom-call | flops 1509949440 | tf_op jit(solution)/shard_map/fock_other/pallas_call | solution.py:81
  59.7 1.5 %fock_side.3 = (f32[336,128]{1,0:T(8,128)S(1)}, f32[320,128]{1,0:T(8,128)S(1)}) custom-call(bf16[768,1280]{1,0:T(8,128)(2,1)S(1)} %get-tuple-element.94.th, bf16[768,1280]{1,0:T(8,128)(2,1)S(1)} %copy-done.1, bf16[1280,768]{1,0:T(8,128)(2,1)S(1)} %copy-done.3, bf16[1280,768]{1,0:T(8,128)(2,1)S(1)} %copy-done.5, f32[1,1280]{1,0:T(1,128)S(1)} %get-tuple-element.147.scale), custom_call_target="tpu_custom_call" | custom-call | flops 1509949440 | tf_op jit(solution)/shard_map/fock_side/pallas_call | solution.py:81
  61.3 1.6 %collective-permute-start.20 = (f32[400,128]{1,0:T(8,128)S(1)}, f32[400,128]{1,0:T(8,128)S(1)}, u32[]{:S(2)}, u32[]{:S(2)}) collective-permute-start(f32[400,128]{1,0:T(8,128)S(1)} %get-tuple-element.165.side_a), channel_id=1, source_target_pairs={{0,1},{1,0},{2,3},{3,2},{4,5},{5,4},{6,7},{7,6},{8,9},{9,8},{10,11... | collective-permute-start | bytes 614408 | tf_op jit(solution)/shard_map/ppermute | solution.py:737
  62.8 2.4 %collective-permute-start.18 = (f32[320,128]{1,0:T(8,128)S(1)}, f32[320,128]{1,0:T(8,128)S(1)}, u32[]{:S(2)}, u32[]{:S(2)}) collective-permute-start(f32[320,128]{1,0:T(8,128)S(1)} %get-tuple-element.152.left), channel_id=1, source_target_pairs={{0,30},{2,4},{4,2},{6,8},{8,6},{10,12},{12,10},{14,16},{16,14},{18... | collective-permute-start | bytes 491528 | tf_op jit(solution)/shard_map/ppermute | solution.py:733
  65.3 3.6 %collective-permute-done.20.arrived = f32[400,128]{1,0:T(8,128)S(1)} collective-permute-done((f32[400,128]{1,0:T(8,128)S(1)}, f32[400,128]{1,0:T(8,128)S(1)}, u32[]{:S(2)}, u32[]{:S(2)}) %collective-permute-start.20) | collective-permute-done | bytes 204832 | tf_op jit(solution)/shard_map/ppermute | solution.py:737
  68.9 1.5 %collective-permute-start.21 = (f32[336,128]{1,0:T(8,128)S(1)}, f32[336,128]{1,0:T(8,128)S(1)}, u32[]{:S(2)}, u32[]{:S(2)}) collective-permute-start(f32[336,128]{1,0:T(8,128)S(1)} %get-tuple-element.166.side_a), channel_id=1, source_target_pairs={{0,30},{2,4},{4,2},{6,8},{8,6},{10,12},{12,10},{14,16},{16,14},{18... | collective-permute-start | bytes 516104 | tf_op jit(solution)/shard_map/ppermute | solution.py:733
  70.4 1.6 %collective-permute-start.19 = (f32[320,128]{1,0:T(8,128)S(1)}, f32[320,128]{1,0:T(8,128)S(1)}, u32[]{:S(2)}, u32[]{:S(2)}) collective-permute-start(f32[320,128]{1,0:T(8,128)S(1)} %add_b.3.side_b), channel_id=1, source_target_pairs={{0,1},{1,0},{2,3},{3,2},{4,5},{5,4},{6,7},{7,6},{8,9},{9,8},{10,11... | collective-permute-start | bytes 491528 | tf_op jit(solution)/shard_map/ppermute | solution.py:737
  72.0 0.8 gather.1
  72.8 3.0 %collective-permute-done.19.arrived_b = f32[320,128]{1,0:T(8,128)S(1)} collective-permute-done((f32[320,128]{1,0:T(8,128)S(1)}, f32[320,128]{1,0:T(8,128)S(1)}, u32[]{:S(2)}, u32[]{:S(2)}) %collective-permute-start.19) | collective-permute-done | bytes 163872 | tf_op jit(solution)/shard_map/ppermute | solution.py:737
  75.8 0.7 collective-permute-done.21.arrived_a
  76.6 1.3 %domain_side.3 = (f32[512,512]{1,0:T(8,128)S(1)}, f32[2,256,256]{2,1,0:T(8,128)S(1)}) custom-call(f32[336,128]{1,0:T(8,128)S(1)} %get-tuple-element.169.side_a, f32[384,128]{1,0:T(8,128)S(1)} %get-tuple-element.170.side_b, bf16[768,512]{1,0:T(8,128)(2,1)S(1)} %get-tuple-element.161.ch, bf16[768,512]{1,0:T(8,128)(2,1)S(1)} %get-tuple-element.162.cl, ...), custom_call_target="tpu_custom_call" | custom-call | flops 503316480 | tf_op jit(solution)/shard_map/domain_side/pallas_call | solution.py:81
  78.0 2.4 %domain_edge.1 = (f32[384,512]{1,0:T(8,128)S(1)}, bf16[384,512]{1,0:T(8,128)(2,1)S(1)}, bf16[384,512]{1,0:T(8,128)(2,1)S(1)}, f32[768,512]{1,0:T(8,128)S(1)}, f3...) custom-call(f32[24,128]{1,0:T(8,128)S(1)} %get-tuple-element.119.present, f32[768,512]{1,0:T(8,128)S(1)} %get-tuple-element.160.coef, ...), custom_call_target="tpu_custom_call" | custom-call | flops 1006632960 | tf_op jit(solution)/shard_map/domain_edge/pallas_call | solution.py:81
  80.5 2.8 %collective-permute-start.24 = (f32[336,128]{1,0:T(8,128)S(1)}, f32[336,128]{1,0:T(8,128)S(1)}, u32[]{:S(2)}, u32[]{:S(2)}) collective-permute-start(f32[336,128]{1,0:T(8,128)S(1)} %get-tuple-element.184), channel_id=1, source_target_pairs={{0,30},{2,4},{4,2},{6,8},{8,6},{10,12},{12,10},{14,16},{16,14},{18... | collective-permute-start | bytes 516104 | tf_op jit(solution)/shard_map/ppermute | solution.py:733
  83.3 1.2 %domain_give.1 = (f32[384,512]{1,0:T(8,128)S(1)}, bf16[384,512]{1,0:T(8,128)(2,1)S(1)}, bf16[384,512]{1,0:T(8,128)(2,1)S(1)}, f32[5,64,128]{2,1,0:T(8,128)S(1)}) custom-call(f32[24,128]{1,0:T(8,128)S(1)} %get-tuple-element.119.present, f32[768,512]{1,0:T(8,128)S(1)} %get-tuple-element.160.coef, bf16[768,512]{1,0:T(8,128)(2,1)S(1)} %get-tuple-element.161.ch, ...), custom_call_target="tpu_custom_call" | custom-call | flops 503316480 | tf_op jit(solution)/shard_map/domain_give/pallas_call | solution.py:81
  84.5 2.3 %domain_last.1 = (f32[2,4,128,128]{3,2,1,0:T(8,128)}, f32[6,64,128]{2,1,0:T(8,128)S(1)}) custom-call(s32[2,4]{1,0:T(2,128)} %own_lists.3, f32[384,512]{1,0:T(8,128)S(1)} %get-tuple-element.174.fresh1, bf16[384,512]{1,0:T(8,128)(2,1)S(1)} %get-tuple-element.175.f1h, bf16[384,512]{1,0:T(8,128)(2,1)S(1)} %get-tuple-element.176.f1l, ...), custom_call_target="tpu_custom_call" | custom-call | tf_op jit(solution)/shard_map/domain_last/pallas_call | solution.py:81
  86.9 1.1 %collective-permute-done.24.from_edge = f32[336,128]{1,0:T(8,128)S(1)} collective-permute-done((f32[336,128]{1,0:T(8,128)S(1)}, f32[336,128]{1,0:T(8,128)S(1)}, u32[]{:S(2)}, u32[]{:S(2)}) %collective-permute-start.24) | collective-permute-done | bytes 172064 | tf_op jit(solution)/shard_map/ppermute | solution.py:733
  88.0 0.7 owner_rows.1
  (58 shorter events, 3.1 us)
Async XLA Ops:
  0.6 7.4 %collective-permute-start = (f32[6,64,128]{2,1,0:T(8,128)}, f32[6,64,128]{2,1,0:T(8,128)S(1)}, u32[]{:S(2)}, u32[]{:S(2)}) collective-permute-start(f32[6,64,128]{2,1,0:T(8,128)} %bitcast.6), channel_id=1, source_target_pairs={{0,2},{2,0},{4,6},{6,4},{8,10},{10,8},{12,14},{14,12},{16,18},{18,... | collective-permute-start | bytes 589832 | tf_op jit(solution)/shard_map/ppermute | solution.py:727
  1.1 13.4 %collective-permute-start.3 = (f32[6,64,128]{2,1,0:T(8,128)}, f32[6,64,128]{2,1,0:T(8,128)S(1)}, u32[]{:S(2)}, u32[]{:S(2)}) collective-permute-start(f32[6,64,128]{2,1,0:T(8,128)} %bitcast.7), channel_id=1, source_target_pairs={{0,1},{1,0},{2,3},{3,2},{4,5},{5,4},{6,7},{7,6},{8,9},{9,8},{10,11... | collective-permute-start | bytes 589832 | tf_op jit(solution)/shard_map/ppermute | solution.py:737
  3.7 10.9 %collective-permute-start.1 = (f32[6,64,128]{2,1,0:T(8,128)}, f32[6,64,128]{2,1,0:T(8,128)S(1)}, u32[]{:S(2)}, u32[]{:S(2)}) collective-permute-start(f32[6,64,128]{2,1,0:T(8,128)} %bitcast.8), channel_id=1, source_target_pairs={{0,30},{2,4},{4,2},{6,8},{8,6},{10,12},{12,10},{14,16},{16,14},{18... | collective-permute-start | bytes 589832 | tf_op jit(solution)/shard_map/ppermute | solution.py:733
  10.6 6.4 %collective-permute-start.5 = (f32[8,64,128]{2,1,0:T(8,128)S(1)}, f32[8,64,128]{2,1,0:T(8,128)S(1)}, u32[]{:S(2)}, u32[]{:S(2)}) collective-permute-start(f32[8,64,128]{2,1,0:T(8,128)S(1)} %get-tuple-element.101), channel_id=1, source_target_pairs={{0,1},{1,0},{2,3},{3,2},{4,5},{5,4},{6,7},{7,6},{8,9},{9,8},{10,11... | collective-permute-start | bytes 786440 | tf_op jit(solution)/shard_map/ppermute | solution.py:737
  14.5 8.7 %copy-start = (bf16[768,1280]{1,0:T(8,128)(2,1)}, bf16[768,1280]{1,0:T(8,128)(2,1)S(1)}, u32[]{:S(2)}) copy-start(bf16[768,1280]{1,0:T(8,128)(2,1)S(1)} %get-tuple-element.95.tl) | copy-start | bytes 5898244
  14.5 8.7 %copy-start.2 = (bf16[1280,768]{1,0:T(8,128)(2,1)}, bf16[1280,768]{1,0:T(8,128)(2,1)S(1)}, u32[]{:S(2)}) copy-start(bf16[1280,768]{1,0:T(8,128)(2,1)S(1)} %get-tuple-element.96.nh) | copy-start | bytes 5898244
  14.5 8.7 %copy-start.4 = (bf16[1280,768]{1,0:T(8,128)(2,1)}, bf16[1280,768]{1,0:T(8,128)(2,1)S(1)}, u32[]{:S(2)}) copy-start(bf16[1280,768]{1,0:T(8,128)(2,1)S(1)} %get-tuple-element.97.nl) | copy-start | bytes 5898244
  14.6 1.7 %collective-permute-start.4 = (f32[6,64,128]{2,1,0:T(8,128)S(1)}, f32[6,64,128]{2,1,0:T(8,128)S(1)}, u32[]{:S(2)}, u32[]{:S(2)}) collective-permute-start(f32[6,64,128]{2,1,0:T(8,128)S(1)} %hold.1.own_far), channel_id=1, source_target_pairs={{0,2},{2,0},{4,6},{6,4},{8,10},{10,8},{12,14},{14,12},{16,18},{18,... | collective-permute-start | bytes 589832 | tf_op jit(solution)/shard_map/ppermute | solution.py:727
  14.7 6.7 %collective-permute-start.2 = (f32[328,128]{1,0:T(8,128)S(1)}, f32[328,128]{1,0:T(8,128)S(1)}, u32[]{:S(2)}, u32[]{:S(2)}) collective-permute-start(f32[328,128]{1,0:T(8,128)S(1)} %far_message.1), channel_id=1, source_target_pairs={{0,1},{1,0},{2,3},{3,2},{4,5},{5,4},{6,7},{7,6},{8,9},{9,8},{10,11... | collective-permute-start | bytes 503816 | tf_op jit(solution)/shard_map/ppermute | solution.py:737
  17.0 2.8 %copy-start.9 = (f32[8,64,128]{2,1,0:T(8,128)}, f32[8,64,128]{2,1,0:T(8,128)S(1)}, u32[]{:S(2)}) copy-start(f32[8,64,128]{2,1,0:T(8,128)S(1)} %collective-permute-done.5.early) | copy-start | bytes 786436
  17.0 4.4 %copy-start.7 = (f32[1,1280]{1,0:T(1,128)S(1)}, f32[1,1280]{1,0:T(1,128)}, u32[]{:S(2)}) copy-start(f32[1,1280]{1,0:T(1,128)} %weights.3) | copy-start | bytes 15364
  17.0 4.4 %copy-start.8 = (f32[1,1280]{1,0:T(1,128)S(1)}, f32[1,1280]{1,0:T(1,128)}, u32[]{:S(2)}) copy-start(f32[1,1280]{1,0:T(1,128)} %external.3) | copy-start | bytes 15364
  23.1 1.7 %collective-permute-start.6 = (f32[328,128]{1,0:T(8,128)S(1)}, f32[328,128]{1,0:T(8,128)S(1)}, u32[]{:S(2)}, u32[]{:S(2)}) collective-permute-start(f32[328,128]{1,0:T(8,128)S(1)} %get-tuple-element.108), channel_id=1, source_target_pairs={{0,2},{2,0},{4,6},{6,4},{8,10},{10,8},{12,14},{14,12},{16,18},{18,... | collective-permute-start | bytes 503816 | tf_op jit(solution)/shard_map/ppermute | solution.py:727
  23.2 15.9 %copy-start.6 = (f32[2,4,128,128]{3,2,1,0:T(8,128)S(1)}, f32[2,4,128,128]{3,2,1,0:T(8,128)}, u32[]{:S(2)}) copy-start(f32[2,4,128,128]{3,2,1,0:T(8,128)} %param.13) | copy-start | bytes 1572868
  24.8 7.9 %collective-permute-start.10 = (f32[400,128]{1,0:T(8,128)S(1)}, f32[400,128]{1,0:T(8,128)S(1)}, u32[]{:S(2)}, u32[]{:S(2)}) collective-permute-start(f32[400,128]{1,0:T(8,128)S(1)} %get-tuple-element.125.side_a), channel_id=1, source_target_pairs={{0,1},{1,0},{2,3},{3,2},{4,5},{5,4},{6,7},{7,6},{8,9},{9,8},{10,11... | collective-permute-start | bytes 614408 | tf_op jit(solution)/shard_map/ppermute | solution.py:737
  26.4 7.4 %collective-permute-start.7 = (f32[320,128]{1,0:T(8,128)S(1)}, f32[320,128]{1,0:T(8,128)S(1)}, u32[]{:S(2)}, u32[]{:S(2)}) collective-permute-start(f32[320,128]{1,0:T(8,128)S(1)} %get-tuple-element.111.left), channel_id=1, source_target_pairs={{0,30},{2,4},{4,2},{6,8},{8,6},{10,12},{12,10},{14,16},{16,14},{18... | collective-permute-start | bytes 491528 | tf_op jit(solution)/shard_map/ppermute | solution.py:733
  28.2 10.1 %collective-permute-start.9 = (f32[8,64,128]{2,1,0:T(8,128)}, f32[8,64,128]{2,1,0:T(8,128)S(1)}, u32[]{:S(2)}, u32[]{:S(2)}) collective-permute-start(f32[8,64,128]{2,1,0:T(8,128)} %get-tuple-element.112), channel_id=1, source_target_pairs={{0,1},{1,0},{2,3},{3,2},{4,5},{5,4},{6,7},{7,6},{8,9},{9,8},{10,11... | collective-permute-start | bytes 786440 | tf_op jit(solution)/shard_map/ppermute | solution.py:737
  32.8 8.7 %collective-permute-start.11 = (f32[336,128]{1,0:T(8,128)S(1)}, f32[336,128]{1,0:T(8,128)S(1)}, u32[]{:S(2)}, u32[]{:S(2)}) collective-permute-start(f32[336,128]{1,0:T(8,128)S(1)} %get-tuple-element.126.side_a), channel_id=1, source_target_pairs={{0,30},{2,4},{4,2},{6,8},{8,6},{10,12},{12,10},{14,16},{16,14},{18... | collective-permute-start | bytes 516104 | tf_op jit(solution)/shard_map/ppermute | solution.py:733
  33.9 7.6 %collective-permute-start.8 = (f32[320,128]{1,0:T(8,128)S(1)}, f32[320,128]{1,0:T(8,128)S(1)}, u32[]{:S(2)}, u32[]{:S(2)}) collective-permute-start(f32[320,128]{1,0:T(8,128)S(1)} %add_b.2.side_b), channel_id=1, source_target_pairs={{0,1},{1,0},{2,3},{3,2},{4,5},{5,4},{6,7},{7,6},{8,9},{9,8},{10,11... | collective-permute-start | bytes 491528 | tf_op jit(solution)/shard_map/ppermute | solution.py:737
  38.4 0.7 copy-start.10
  41.5 1.5 %collective-permute-start.12 = (f32[328,128]{1,0:T(8,128)S(1)}, f32[328,128]{1,0:T(8,128)S(1)}, u32[]{:S(2)}, u32[]{:S(2)}) collective-permute-start(f32[328,128]{1,0:T(8,128)S(1)} %get-tuple-element.133), channel_id=1, source_target_pairs={{0,2},{2,0},{4,6},{6,4},{8,10},{10,8},{12,14},{14,12},{16,18},{18,... | collective-permute-start | bytes 503816 | tf_op jit(solution)/shard_map/ppermute | solution.py:727
  45.4 8.0 %collective-permute-start.14 = (f32[392,128]{1,0:T(8,128)S(1)}, f32[392,128]{1,0:T(8,128)S(1)}, u32[]{:S(2)}, u32[]{:S(2)}) collective-permute-start(f32[392,128]{1,0:T(8,128)S(1)} %get-tuple-element.144.mine), channel_id=1, source_target_pairs={{0,30},{2,4},{4,2},{6,8},{8,6},{10,12},{12,10},{14,16},{16,14},{18... | collective-permute-start | bytes 602120 | tf_op jit(solution)/shard_map/ppermute | solution.py:733
  48.4 5.1 %copy-start.1 = (bf16[768,1280]{1,0:T(8,128)(2,1)S(1)}, bf16[768,1280]{1,0:T(8,128)(2,1)}, u32[]{:S(2)}) copy-start(bf16[768,1280]{1,0:T(8,128)(2,1)} %copy-done) | copy-start | bytes 5898244
  48.4 1.5 %collective-permute-start.13 = (f32[328,128]{1,0:T(8,128)S(1)}, f32[328,128]{1,0:T(8,128)S(1)}, u32[]{:S(2)}, u32[]{:S(2)}) collective-permute-start(f32[328,128]{1,0:T(8,128)S(1)} %get-tuple-element.141), channel_id=1, source_target_pairs={{0,2},{2,0},{4,6},{6,4},{8,10},{10,8},{12,14},{14,12},{16,18},{18,... | collective-permute-start | bytes 503816 | tf_op jit(solution)/shard_map/ppermute | solution.py:727
  49.9 7.6 %collective-permute-start.16 = (f32[336,128]{1,0:T(8,128)S(1)}, f32[336,128]{1,0:T(8,128)S(1)}, u32[]{:S(2)}, u32[]{:S(2)}) collective-permute-start(f32[336,128]{1,0:T(8,128)S(1)} %get-tuple-element.142.near), channel_id=1, source_target_pairs={{0,30},{2,4},{4,2},{6,8},{8,6},{10,12},{12,10},{14,16},{16,14},{18... | collective-permute-start | bytes 516104 | tf_op jit(solution)/shard_map/ppermute | solution.py:733
  53.4 1.5 %collective-permute-start.15 = (f32[328,128]{1,0:T(8,128)S(1)}, f32[328,128]{1,0:T(8,128)S(1)}, u32[]{:S(2)}, u32[]{:S(2)}) collective-permute-start(f32[328,128]{1,0:T(8,128)S(1)} %get-tuple-element.145.near), channel_id=1, source_target_pairs={{0,2},{2,0},{4,6},{6,4},{8,10},{10,8},{12,14},{14,12},{16,18},{18,... | collective-permute-start | bytes 503816 | tf_op jit(solution)/shard_map/ppermute | solution.py:727
  54.4 3.1 %copy-start.3 = (bf16[1280,768]{1,0:T(8,128)(2,1)S(1)}, bf16[1280,768]{1,0:T(8,128)(2,1)}, u32[]{:S(2)}) copy-start(bf16[1280,768]{1,0:T(8,128)(2,1)} %copy-done.2) | copy-start | bytes 5898244
  54.4 3.1 %copy-start.5 = (bf16[1280,768]{1,0:T(8,128)(2,1)S(1)}, bf16[1280,768]{1,0:T(8,128)(2,1)}, u32[]{:S(2)}) copy-start(bf16[1280,768]{1,0:T(8,128)(2,1)} %copy-done.4) | copy-start | bytes 5898244
  59.6 1.6 %collective-permute-start.17 = (f32[328,128]{1,0:T(8,128)S(1)}, f32[328,128]{1,0:T(8,128)S(1)}, u32[]{:S(2)}, u32[]{:S(2)}) collective-permute-start(f32[328,128]{1,0:T(8,128)S(1)} %get-tuple-element.151), channel_id=1, source_target_pairs={{0,2},{2,0},{4,6},{6,4},{8,10},{10,8},{12,14},{14,12},{16,18},{18,... | collective-permute-start | bytes 503816 | tf_op jit(solution)/shard_map/ppermute | solution.py:727
  61.3 7.6 %collective-permute-start.20 = (f32[400,128]{1,0:T(8,128)S(1)}, f32[400,128]{1,0:T(8,128)S(1)}, u32[]{:S(2)}, u32[]{:S(2)}) collective-permute-start(f32[400,128]{1,0:T(8,128)S(1)} %get-tuple-element.165.side_a), channel_id=1, source_target_pairs={{0,1},{1,0},{2,3},{3,2},{4,5},{5,4},{6,7},{7,6},{8,9},{9,8},{10,11... | collective-permute-start | bytes 614408 | tf_op jit(solution)/shard_map/ppermute | solution.py:737
  62.8 7.5 %collective-permute-start.18 = (f32[320,128]{1,0:T(8,128)S(1)}, f32[320,128]{1,0:T(8,128)S(1)}, u32[]{:S(2)}, u32[]{:S(2)}) collective-permute-start(f32[320,128]{1,0:T(8,128)S(1)} %get-tuple-element.152.left), channel_id=1, source_target_pairs={{0,30},{2,4},{4,2},{6,8},{8,6},{10,12},{12,10},{14,16},{16,14},{18... | collective-permute-start | bytes 491528 | tf_op jit(solution)/shard_map/ppermute | solution.py:733
  68.9 7.6 %collective-permute-start.21 = (f32[336,128]{1,0:T(8,128)S(1)}, f32[336,128]{1,0:T(8,128)S(1)}, u32[]{:S(2)}, u32[]{:S(2)}) collective-permute-start(f32[336,128]{1,0:T(8,128)S(1)} %get-tuple-element.166.side_a), channel_id=1, source_target_pairs={{0,30},{2,4},{4,2},{6,8},{8,6},{10,12},{12,10},{14,16},{16,14},{18... | collective-permute-start | bytes 516104 | tf_op jit(solution)/shard_map/ppermute | solution.py:733
  70.4 5.4 %collective-permute-start.19 = (f32[320,128]{1,0:T(8,128)S(1)}, f32[320,128]{1,0:T(8,128)S(1)}, u32[]{:S(2)}, u32[]{:S(2)}) collective-permute-start(f32[320,128]{1,0:T(8,128)S(1)} %add_b.3.side_b), channel_id=1, source_target_pairs={{0,1},{1,0},{2,3},{3,2},{4,5},{5,4},{6,7},{7,6},{8,9},{9,8},{10,11... | collective-permute-start | bytes 491528 | tf_op jit(solution)/shard_map/ppermute | solution.py:737
  76.5 1.5 %collective-permute-start.22 = (f32[328,128]{1,0:T(8,128)S(1)}, f32[328,128]{1,0:T(8,128)S(1)}, u32[]{:S(2)}, u32[]{:S(2)}) collective-permute-start(f32[328,128]{1,0:T(8,128)S(1)} %get-tuple-element.173), channel_id=1, source_target_pairs={{0,2},{2,0},{4,6},{6,4},{8,10},{10,8},{12,14},{14,12},{16,18},{18,... | collective-permute-start | bytes 503816 | tf_op jit(solution)/shard_map/ppermute | solution.py:727
  80.5 7.6 %collective-permute-start.24 = (f32[336,128]{1,0:T(8,128)S(1)}, f32[336,128]{1,0:T(8,128)S(1)}, u32[]{:S(2)}, u32[]{:S(2)}) collective-permute-start(f32[336,128]{1,0:T(8,128)S(1)} %get-tuple-element.184), channel_id=1, source_target_pairs={{0,30},{2,4},{4,2},{6,8},{8,6},{10,12},{12,10},{14,16},{16,14},{18... | collective-permute-start | bytes 516104 | tf_op jit(solution)/shard_map/ppermute | solution.py:733
  84.5 2.4 %collective-permute-start.23 = (f32[5,64,128]{2,1,0:T(8,128)S(1)}, f32[5,64,128]{2,1,0:T(8,128)S(1)}, u32[]{:S(2)}, u32[]{:S(2)}) collective-permute-start(f32[5,64,128]{2,1,0:T(8,128)S(1)} %get-tuple-element.183), channel_id=1, source_target_pairs={{0,2},{2,0},{4,6},{6,4},{8,10},{10,8},{12,14},{14,12},{16,18},{18,... | collective-permute-start | bytes 491528 | tf_op jit(solution)/shard_map/ppermute | solution.py:727
